TPU v7x, 32 devices: a whole 2x2x4 slice. The times are simulated.
32 devices in a mesh: inner: 8 (over y, x, core), outer: 4 (over z).
Axes of the slice: x: 2, y: 2, z: 4, core: 2. Of those that a mesh axis runs over, the one named last changes fastest.
Arguments:
- gradients: bfloat16 [8, 4, 256, 8192], P('inner', 'outer'), may hold values from -6 to 6
- master_shard: float32 [256, 8192], P('outer', 'inner'), may hold values from -6 to 6
- first_moment: float32 [256, 8192], P('outer', 'inner'), may hold values from -48 to 48
- second_moment: float32 [256, 8192], P('outer', 'inner'), may hold values from 100 to 1000
Outputs:
- new_master: float32 [256, 8192], P('outer', 'inner')
- new_first: float32 [256, 8192], P('outer', 'inner')
- new_second: float32 [256, 8192], P('outer', 'inner')
- group_weights: bfloat16 [256, 8192], P(None, 'inner')
All inputs are finite; a program needn't handle non-finite values.
Results may differ from a plain program's by a relative error of at most 0.0025.
Values may be sent and summed in bfloat16 or wider, within the bound.
No kernel may reach another device: no remote copies, remote signals or barrier semaphores. Data moves between devices by JAX's collectives and lax.ppermute only.
A program may use at most 64 MiB of HBM per device.

v0:
```python
import jax
import jax.numpy as jnp
from jax import lax
from jax.sharding import PartitionSpec as P

beta_first = 0.9
beta_second = 0.95
learn_rate = 0.05
decay_rate = 0.1
adam_eps = 1e-05
bias_first = 1.0 - 0.9**10
bias_second = 1.0 - 0.95**10


def sum_sources(pieces):
    return jnp.sum(pieces.astype(jnp.float32), axis=0)


def body(gradients, master_shard, first_moment, second_moment):
    local = gradients.reshape(1, gradients.shape[2], gradients.shape[3])
    partial_value = sum_sources(
        lax.all_to_all(local, "inner", split_axis=2, concat_axis=0, tiled=True)
    )
    reduced = sum_sources(
        lax.all_to_all(
            partial_value[None].astype(jnp.bfloat16),
            "outer",
            split_axis=1,
            concat_axis=0,
            tiled=True,
        ).astype(jnp.float32)
    )
    new_first = beta_first * first_moment + (1.0 - beta_first) * reduced
    new_second = beta_second * second_moment + (1.0 - beta_second) * reduced * reduced
    update = (
        new_first / bias_first / (jnp.sqrt(new_second / bias_second) + adam_eps)
        + decay_rate * master_shard
    )
    new_master = master_shard - learn_rate * update
    copy_weights = lax.all_gather(new_master.astype(jnp.bfloat16), "outer", axis=0, tiled=True)
    return (new_master, new_first, new_second, copy_weights)


def solution(mesh):
    return jax.shard_map(
        body,
        mesh=mesh,
        in_specs=(
            P("inner", "outer", None, None),
            P("outer", "inner"),
            P("outer", "inner"),
            P("outer", "inner"),
        ),
        out_specs=(P("outer", "inner"), P("outer", "inner"), P("outer", "inner"), P(None, "inner")),
        check_vma=False,
    )
```

profile of v0, /device:TPU:0, one launch (start us, length us, event | category | flops | bytes accessed | tf_op | source)
XLA Modules:
  0.0 184.6 jit_solution(8340274724152886732)
XLA Ops:
  0.6 17.9 %copy.11 = bf16[1,256,8192]{1,0,2:T(2,128)(2,1)} copy(bf16[1,256,8192]{2,1,0:T(8,128)(2,1)} %bitcast.11) | data formatting | bytes 8388608 | tf_op jit(solution)/shard_map/reshape | solution.py:20
  18.5 0.5 broadcast.18
  19.0 43.5 %reduce.4 = bf16[8192,256]{1,0:T(8,128)(2,1)} reduce(bf16[8192,1,256]{2,1,0:T(2,128)(2,1)} %bitcast.8, bf16[]{:T(256)} %broadcast.18), dimensions={1}, to_apply=%bitcast.4.reduce_sub_computation | reduce | bytes 8388610
  62.5 7.0 %reshape.29 = bf16[8,2,131072]{2,1,0:T(2,128)(2,1)} reshape(bf16[8192,256]{1,0:T(8,128)(2,1)} %reduce.4) | data formatting | bytes 8388608
  69.5 54.3 %all_to_all.21 = bf16[8,2,131072]{2,1,0:T(2,128)(2,1)} all-to-all(bf16[8,2,131072]{2,1,0:T(2,128)(2,1)} %reshape.29), channel_id=1, replica_groups=mesh['inner'=8,'outer'=4] {'inner'}, dimensions={0} | all-to-all | bytes 8388608 | tf_op jit(solution)/shard_map/all_to_all | solution.py:22
  123.8 8.8 %reshape.30 = bf16[8192,1,256]{2,1,0:T(2,128)(2,1)} reshape(bf16[8,2,131072]{2,1,0:T(2,128)(2,1)} %all_to_all.21) | data formatting | bytes 8388608
  132.6 6.1 %copy.16 = bf16[1,256,8192]{1,2,0:T(8,128)(2,1)} copy(bf16[1,256,8192]{1,0,2:T(2,128)(2,1)} %bitcast.9) | data formatting | bytes 8388608
  138.7 3.0 %reduce_sum.21 = bf16[256,1024]{0,1:T(8,128)(2,1)S(1)} reduce(bf16[256,8,1024]{0,2,1:T(8,128)(2,1)} %bitcast.10, bf16[]{:T(256)} %constant.4.clone.1), dimensions={1}, to_apply=%region_0.0 | reduce | flops 1835008 | bytes 4718594 | tf_op jit(solution)/shard_map/reduce_sum | solution.py:16
  141.7 1.0 copy.13
  142.7 0.0 copy-start
  142.7 0.0 copy-start.1
  142.8 0.0 copy-start.2
  142.8 3.8 %reduce.5 = bf16[256,1024]{1,0:T(8,128)(2,1)S(1)} reduce(bf16[256,1,1024]{2,1,0:T(2,128)(2,1)S(1)} %bitcast.12, bf16[]{:T(256)} %broadcast.18), dimensions={1}, to_apply=%bitcast.6.reduce_sub_computation | reduce | bytes 1048578
  146.5 0.4 reshape.31
  146.9 19.2 %all_to_all.22 = bf16[4,2,32768]{2,1,0:T(2,128)(2,1)S(1)} all-to-all(bf16[4,2,32768]{2,1,0:T(2,128)(2,1)S(1)} %reshape.31), channel_id=1, replica_groups=mesh['inner'=8,'outer'=4] {'outer'}, dimensions={0} | all-to-all | bytes 1048576 | tf_op jit(solution)/shard_map/all_to_all | solution.py:25
  166.1 0.5 reshape.32
  166.7 0.2 copy.17
  166.9 0.1 reduce_sum.22
  167.0 0.0 copy-done
  167.0 0.0 copy-done.1
  167.0 0.0 copy-done.2
  167.0 1.0 fusion.1
  168.0 15.8 %all_gather.3 = bf16[256,1024]{1,0:T(8,128)(2,1)S(1)} all-gather(bf16[64,1024]{1,0:T(8,128)(2,1)S(1)} %get-tuple-element.4), channel_id=1, replica_groups=mesh['inner'=8,'outer'=4] {'outer'}, dimensions={0}, use_global_device_ids=true | all-gather | bytes 655360 | tf_op jit(solution)/shard_map/all_gather | solution.py:40
  183.8 0.8 copy.19
Async XLA Ops:
  142.7 24.2 %copy-start = (f32[64,1024]{1,0:T(8,128)S(1)}, f32[64,1024]{1,0:T(8,128)}, u32[]{:S(2)}) copy-start(f32[64,1024]{1,0:T(8,128)} %param.5) | copy-start | bytes 786436
  142.7 24.2 %copy-start.1 = (f32[64,1024]{1,0:T(8,128)S(1)}, f32[64,1024]{1,0:T(8,128)}, u32[]{:S(2)}) copy-start(f32[64,1024]{1,0:T(8,128)} %param.6) | copy-start | bytes 786436
  142.8 24.2 %copy-start.2 = (f32[64,1024]{1,0:T(8,128)S(1)}, f32[64,1024]{1,0:T(8,128)}, u32[]{:S(2)}) copy-start(f32[64,1024]{1,0:T(8,128)} %param.7) | copy-start | bytes 786436
where the time goes:
time: 186 us; the launch traced here: 185 us
  blocking collectives  89.3 us (48%)
  other arithmetic  51.4 us (28%)
  local copies, waits for them, and re-layouts  43.1 us (23%)
    all_to_all x1, blocking collectives, body(): lax.all_to_all(local, 'inner', split_axis=2, concat_axis=0, tiled=True)  54.3 us
    unnamed x2, other arithmetic  47.3 us
    unnamed x14, local copies, waits for them, and re-layouts  24.3 us
    all_to_all x1, blocking collectives, body(): lax.all_to_all(partial_value[None].astype(jnp.bfloat16), 'outer', split_a...  19.2 us
    reshape x1, local copies, waits for them, and re-layouts, body(): local = gradients.reshape(1, gradients.shape[2], gradients.shape[3])  17.9 us
    all_gather x1, blocking collectives, body(): lax.all_gather(new_master.astype(jnp.bfloat16), 'outer', axis=0, tiled=True)  15.8 us

commit v1 on v0

v1 whole, which is shorter than its diff:
```python
import functools

import jax
import jax.numpy as jnp
from jax import lax
from jax.experimental import pallas as pl
from jax.experimental.pallas import tpu as pltpu
from jax.sharding import PartitionSpec as P

beta_first = 0.9
beta_second = 0.95
learn_rate = 0.05
decay_rate = 0.1
adam_eps = 1e-05
bias_first = 1.0 - 0.9**10
bias_second = 1.0 - 0.95**10

CORES = 2
SUPERS = 2
STEP = 16
ANY = pl.BlockSpec(memory_space=pl.ANY)
VMEM = pl.BlockSpec(memory_space=pltpu.VMEM)


def estimate(nbytes):
    return pl.CostEstimate(flops=nbytes, bytes_accessed=nbytes, transcendentals=0)


def place(chips):
    me = lax.axis_index("inner")
    return me // CORES, lax.rem(me, CORES)


def grad_block(grad_ref, rows, chip, core, width):
    start = pl.multiple_of((CORES * chip + core) * width, width)
    return grad_ref.at[:, pl.ds(*rows), pl.ds(start, width)]


def load(sources, slots, sems):
    copies = [pltpu.make_async_copy(s, d, sems.at[i]) for i, (s, d) in enumerate(zip(sources, slots))]
    for copy in copies:
        copy.start()
    for copy in copies:
        copy.wait()


def total_of(terms, index):
    value = terms[0][index].astype(jnp.float32)
    for term in terms[1:]:
        value = value + term[index].astype(jnp.float32)
    return value


def add_pieces(out, terms):
    blocks, depth, _ = terms[0].shape
    per = depth // STEP

    def step(i, carry):
        index = (i // per, pl.ds(pl.multiple_of(lax.rem(i, per) * STEP, STEP), STEP))
        out[index] = total_of(terms, index).astype(out.dtype)
        return carry

    lax.fori_loop(0, blocks * per, step, 0)


def pack(grads, rows, width, chips):
    outer = grads.shape[0]

    def kernel(grad_ref, out_ref, sems):
        _, core = place(chips)
        load(
            [grad_block(grad_ref, rows, chip, 1 - core, width) for chip in range(chips)],
            [out_ref.at[chip] for chip in range(chips)],
            sems,
        )

    shape = (chips, outer, rows[1], width)
    return pl.pallas_call(
        kernel,
        out_shape=jax.ShapeDtypeStruct(shape, grads.dtype),
        in_specs=[ANY],
        out_specs=ANY,
        scratch_shapes=[pltpu.SemaphoreType.DMA((chips,))],
        cost_estimate=estimate(2 * 2 * chips * outer * rows[1] * width),
        name="pack",
    )(grads)


def sums(grads, core_in, extra, rows, width, chips, targets, name):
    outer = grads.shape[0]
    n_terms = [2 + len(t["extra"]) for t in targets]
    total = sum(n_terms)

    def kernel(*refs):
        grad_ref, core_ref = refs[:2]
        extra_refs = refs[2 : 2 + len(extra)]
        outs = refs[2 + len(extra) : 2 + len(extra) + len(targets)]
        slots = refs[2 + len(extra) + len(targets) : -1]
        sems = refs[-1]
        chip, core = place(chips)
        groups, at = [], 0
        for t, n in zip(targets, n_terms):
            to = t["chip"](chip)
            base, depth = t["rows"]
            sources = [
                grad_block(grad_ref, (rows[0] + base, depth), to, core, width),
                core_ref.at[to, :, pl.ds(base, depth)],
            ] + [extra_refs[i].at[j] if j is not None else extra_refs[i] for i, j in t["extra"]]
            copies = [
                pltpu.make_async_copy(s, slots[at + i], sems.at[at + i]) for i, s in enumerate(sources)
            ]
            for copy in copies:
                copy.start()
            groups.append((copies, slots[at : at + n]))
            at += n
        for (copies, terms), out in zip(groups, outs):
            for copy in copies:
                copy.wait()
            add_pieces(out, terms)

    shapes = [(outer, t["rows"][1], width) for t in targets]
    scratch = [pltpu.VMEM(s, jnp.bfloat16) for s, n in zip(shapes, n_terms) for _ in range(n)]
    return pl.pallas_call(
        kernel,
        out_shape=[jax.ShapeDtypeStruct(s, jnp.bfloat16) for s in shapes],
        in_specs=[ANY] * (2 + len(extra)),
        out_specs=[VMEM] * len(targets),
        scratch_shapes=scratch + [pltpu.SemaphoreType.DMA((total,))],
        cost_estimate=estimate(sum(2 * (n + 1) * s[0] * s[1] * s[2] for s, n in zip(shapes, n_terms))),
        name=name,
    )(grads, core_in, *extra)


def group_sum(grads, core_in, extra, rows, width, chips, parts):
    outer = grads.shape[0]
    depth = rows[1]
    n_terms = [2 + len(p["extra"]) for p in parts]
    total = sum(n_terms)

    def kernel(*refs):
        grad_ref, core_ref = refs[:2]
        extra_refs = refs[2 : 2 + len(extra)]
        outs = refs[2 + len(extra) : 2 + len(extra) + outer]
        slots = refs[2 + len(extra) + outer : -1]
        sems = refs[-1]
        chip, core = place(chips)
        here = lax.axis_index("outer")
        groups, at = [], 0
        for p, n in zip(parts, n_terms):
            base, size = p["rows"]
            sources = [
                grad_block(grad_ref, (rows[0] + base, size), chip, core, width),
                core_ref.at[chip, :, pl.ds(base, size)],
            ] + [extra_refs[i].at[j] if j is not None else extra_refs[i] for i, j in p["extra"]]
            copies = [
                pltpu.make_async_copy(s, slots[at + i], sems.at[at + i]) for i, s in enumerate(sources)
            ]
            for copy in copies:
                copy.start()
            groups.append((copies, slots[at : at + n], base, size))
            at += n
        for copies, terms, base, size in groups:
            for copy in copies:
                copy.wait()
            for shift in range(outer):
                block = lax.rem(here + shift, outer)
                for at in range(0, size, STEP):
                    value = total_of(terms, (block, pl.ds(at, STEP)))
                    outs[shift][pl.ds(base + at, STEP)] = value.astype(outs[shift].dtype)

    shapes = [(outer, p["rows"][1], width) for p in parts]
    scratch = [pltpu.VMEM(s, jnp.bfloat16) for s, n in zip(shapes, n_terms) for _ in range(n)]
    return pl.pallas_call(
        kernel,
        out_shape=[
            jax.ShapeDtypeStruct((depth, width), jnp.float32 if s == 0 else jnp.bfloat16) for s in range(outer)
        ],
        in_specs=[ANY] * (2 + len(extra)),
        out_specs=[VMEM] * outer,
        scratch_shapes=scratch + [pltpu.SemaphoreType.DMA((total,))],
        cost_estimate=estimate(sum(2 * (n + 1) * s[0] * s[1] * s[2] for s, n in zip(shapes, n_terms))),
        name="group_sum",
    )(grads, core_in, *extra)


def adam(total, master, first, second):
    new_first = beta_first * first + (1.0 - beta_first) * total
    new_second = beta_second * second + (1.0 - beta_second) * total * total
    update = new_first / bias_first / (jnp.sqrt(new_second / bias_second) + adam_eps) + decay_rate * master
    return master - learn_rate * update, new_first, new_second


def weights(kept, received, rows, master, first, second):
    depth, width = kept.shape

    def kernel(*refs):
        *terms, master_ref, first_ref, second_ref, out_ref = refs

        def step(i, carry):
            here = pl.ds(pl.multiple_of(i * STEP, STEP), STEP)
            there = pl.ds(pl.multiple_of(rows[0] + i * STEP, STEP), STEP)
            value, _, _ = adam(total_of(terms, here), master_ref[there], first_ref[there], second_ref[there])
            out_ref[here] = value.astype(jnp.bfloat16)
            return carry

        lax.fori_loop(0, depth // STEP, step, 0)

    return pl.pallas_call(
        kernel,
        out_shape=jax.ShapeDtypeStruct((depth, width), jnp.bfloat16),
        in_specs=[VMEM] * (4 + len(received)),
        out_specs=VMEM,
        cost_estimate=estimate(depth * width * 24),
        name="weights",
    )(kept, *received, master, first, second)


def finish(totals, spans, master, first, second):
    n = len(totals[0])

    def kernel(*refs):
        terms = refs[: n * len(spans)]
        master_ref, first_ref, second_ref, *outs = refs[n * len(spans) :]
        for k, (base, depth) in enumerate(spans):

            def step(i, carry, k=k, base=base):
                here = pl.ds(pl.multiple_of(i * STEP, STEP), STEP)
                there = pl.ds(pl.multiple_of(base + i * STEP, STEP), STEP)
                values = adam(
                    total_of(terms[n * k : n * k + n], here), master_ref[there], first_ref[there], second_ref[there]
                )
                for out, value in zip(outs, values):
                    out[there] = value
                return carry

            lax.fori_loop(0, depth // STEP, step, 0)

    return pl.pallas_call(
        kernel,
        out_shape=[jax.ShapeDtypeStruct(master.shape, jnp.float32)] * 3,
        in_specs=[VMEM] * (n * len(spans) + 3),
        out_specs=[VMEM] * 3,
        cost_estimate=estimate(master.size * 34),
        name="finish",
    )(*[t for group in totals for t in group], master, first, second)


def assemble(own, received, spans, outer, owned):
    width = own[0].shape[1]

    def kernel(*refs):
        *pieces, out_ref, sems = refs
        here = lax.axis_index("outer")
        sources, places = [], []
        at = 0
        for base, depth in spans:
            for shift in range(outer):
                block = lax.rem(here + outer - shift, outer)
                sources.append(pieces[at])
                places.append(out_ref.at[block, pl.ds(base, depth)])
                at += 1
        load(sources, places, sems)

    return pl.pallas_call(
        kernel,
        out_shape=jax.ShapeDtypeStruct((outer, owned, width), jnp.bfloat16),
        in_specs=[ANY] * (outer * len(spans)),
        out_specs=ANY,
        scratch_shapes=[pltpu.SemaphoreType.DMA((outer * len(spans),))],
        cost_estimate=estimate(4 * outer * owned * width),
        name="assemble",
    )(*[piece for w, got in zip(own, received) for piece in (w, *got)])


def to_chip(x, target, chips):
    pairs = [(CORES * c + k, CORES * target(c) + k) for c in range(chips) for k in range(CORES)]
    return lax.ppermute(x, "inner", pairs)


def to_group(x, shift, outer):
    return lax.ppermute(x, "outer", [(i, (i + shift) % outer) for i in range(outer)])


def body(gradients, master, first, second, *, inner, outer):
    depth, columns = gradients.shape[2:]
    chips, owned, width = inner // CORES, depth // outer, columns // inner
    grads = gradients.reshape(outer, owned, columns)

    supers = SUPERS if owned % (2 * STEP * SUPERS) == 0 else 1
    per = owned // supers
    spans = [(k * per, per) for k in range(supers)]
    two_steps = chips == 4 and per % (2 * STEP) == 0

    totals, own, received = [], [], []
    for rows in spans:
        packed = pack(grads, rows, width, chips)
        core_in = lax.ppermute(packed, "inner", [(i, i ^ 1) for i in range(inner)])
        if two_steps:
            half = per // 2
            runs = [((0, half), 1, 2), ((half, half), 2, 1)]
            targets = [
                dict(rows=run, chip=lambda c, t=t: c ^ t, extra=[])
                for run, a, b in runs
                for t in (a, a ^ b)
            ]
            made = sums(grads, core_in, [], rows, width, chips, targets, "first_sum")
            got = [
                [to_chip(made[2 * h + i], lambda c, a=a: c ^ a, chips) for i in range(2)]
                for h, (_, a, _) in enumerate(runs)
            ]
            targets = [
                dict(rows=run, chip=lambda c, b=b: c ^ b, extra=[(h, None)]) for h, (run, _, b) in enumerate(runs)
            ]
            made = sums(grads, core_in, [g[1] for g in got], rows, width, chips, targets, "second_sum")
            last = [to_chip(made[h], lambda c, b=b: c ^ b, chips) for h, (_, _, b) in enumerate(runs)]
            extra = [g[0] for g in got] + last
            parts = [dict(rows=run, extra=[(h, None), (2 + h, None)]) for h, (run, _, _) in enumerate(runs)]
        else:
            moves = [lambda c, m=m: (c + m) % chips for m in range(1, chips)]
            targets = [dict(rows=(0, per), chip=lambda c, m=m: lax.rem(c + m, chips), extra=[]) for m in range(1, chips)]
            made = sums(grads, core_in, [], rows, width, chips, targets, "first_sum")
            extra = [to_chip(x, move, chips) for x, move in zip(made, moves)]
            parts = [dict(rows=(0, per), extra=[(i, None) for i in range(chips - 1)])]
        kept, *sends = group_sum(grads, core_in, extra, rows, width, chips, parts)
        arrived = [to_group(x, s + 1, outer) for s, x in enumerate(sends)]
        totals.append((kept, *arrived))
        w = weights(kept, arrived, rows, master, first, second)
        own.append(w)
        received.append([to_group(w, s, outer) for s in range(1, outer)])

    new = finish(totals, spans, master, first, second)
    copy = assemble(own, received, spans, outer, owned).reshape(depth, width)
    return (*new, copy)


def solution(mesh):
    return jax.shard_map(
        functools.partial(body, inner=mesh.shape["inner"], outer=mesh.shape["outer"]),
        mesh=mesh,
        in_specs=(
            P("inner", "outer", None, None),
            P("outer", "inner"),
            P("outer", "inner"),
            P("outer", "inner"),
        ),
        out_specs=(P("outer", "inner"), P("outer", "inner"), P("outer", "inner"), P(None, "inner")),
        check_vma=False,
    )
```

time: 186 us -> 144 us (0.77)
  Pallas kernels: 0 us -> 102 us
  blocking collectives: 89.3 us -> 0 us
  other arithmetic: 51.4 us -> 0 us
  local copies, waits for them, and re-layouts: 43.1 us -> 6.81 us
  starting transfers between devices: 0 us -> 33 us
    pallas_call x0 -> x12, Pallas kernels: none -> 102 us  [the longest x2 65.8 us: pack(): pl.pallas_call(kernel, out_shape=jax.ShapeDtypeStruct(shape, grads.dtype)...]
    all_to_all x2 -> x0, blocking collectives: 73.5 us -> none  [the longest x1 54.3 us: body(): lax.all_to_all(local, 'inner', split_axis=2, concat_axis=0, tiled=True)]
    unnamed x2 -> x0, other arithmetic: 47.3 us -> none
    ppermute x0 -> x26, starting transfers between devices: none -> 33 us  [the longest x12 18.3 us: to_group(): lax.ppermute(x, 'outer', [(i, (i + shift) % outer) for i in range(outer)])]
    reshape x1 -> x0, local copies, waits for them, and re-layouts: 17.9 us -> none  [body(): local = gradients.reshape(1, gradients.shape[2], gradients.shape[3])]
    unnamed x14 -> x58, local copies, waits for them, and re-layouts: 24.3 us -> 6.81 us
    all_gather x1 -> x0, blocking collectives: 15.8 us -> none  [body(): lax.all_gather(new_master.astype(jnp.bfloat16), 'outer', axis=0, tiled=True)]
    reduce_sum x2 -> x0, other arithmetic: 3.12 us -> none  [sum_sources(): return jnp.sum(pieces.astype(jnp.float32), axis=0)]
  transfers between devices with their start and end apart: 0 -> 26, of which waited for: 0 -> 1; matrix products, arithmetic and copies ran while one was open for 0% -> 0% of each run, Pallas kernels for 0% -> 36%
where the time goes in v1:
time: 144 us; the launch traced here: 143 us
  Pallas kernels  102 us (71%)
  starting transfers between devices  33 us (23%)
  local copies, waits for them, and re-layouts  6.81 us (5%)
    pallas_call x2, Pallas kernels, pack(): pl.pallas_call(kernel, out_shape=jax.ShapeDtypeStruct(shape, grads.dtype)...  65.8 us
    ppermute x12, starting transfers between devices, to_group(): lax.ppermute(x, 'outer', [(i, (i + shift) % outer) for i in range(outer)])  18.3 us
    pallas_call x1, Pallas kernels, assemble(): pl.pallas_call(kernel, out_shape=jax.ShapeDtypeStruct((outer, owned, widt...  17.1 us
    ppermute x12, starting transfers between devices, to_chip(): return lax.ppermute(x, 'inner', pairs)  14.1 us
    pallas_call x4, Pallas kernels, sums(): pl.pallas_call(kernel, out_shape=[jax.ShapeDtypeStruct(s, jnp.bfloat16) f...  8.34 us
    unnamed x58, local copies, waits for them, and re-layouts  6.81 us
    pallas_call x2, Pallas kernels, group_sum(): pl.pallas_call(kernel, out_shape=[jax.ShapeDtypeStruct((depth, width), jn...  4.21 us
    pallas_call x2, Pallas kernels, weights(): pl.pallas_call(kernel, out_shape=jax.ShapeDtypeStruct((depth, width), jnp...  4.09 us
  transfers between devices with their start and end apart: 26, of which 1 were waited for; matrix products, arithmetic and copies ran while one was open for 0% of the time, Pallas kernels for 36%

profile of v1, /device:TPU:0, one launch (start us, length us, event | category | flops | bytes accessed | tf_op | source)
XLA Modules:
  0.0 143.3 jit_solution(17856473579505556953)
XLA Ops:
  0.6 32.9 %pack.2 = bf16[4,4,32,1024]{3,2,1,0:T(8,128)(2,1)} custom-call(bf16[4,64,8192]{2,1,0:T(8,128)(2,1)} %bitcast.2), custom_call_target="tpu_custom_call" | custom-call | flops 2097152 | bytes 2097152 | tf_op jit(solution)/shard_map/pack/pallas_call | solution.py:78
  34.1 32.9 %pack.3 = bf16[4,4,32,1024]{3,2,1,0:T(8,128)(2,1)} custom-call(bf16[4,64,8192]{2,1,0:T(8,128)(2,1)} %bitcast.3), custom_call_target="tpu_custom_call" | custom-call | flops 2097152 | bytes 2097152 | tf_op jit(solution)/shard_map/pack/pallas_call | solution.py:78
  68.1 2.2 %first_sum.2 = (bf16[4,16,1024]{2,1,0:T(8,128)(2,1)}, bf16[4,16,1024]{2,1,0:T(8,128)(2,1)}, bf16[4,16,1024]{2,1,0:T(8,128)(2,1)}, bf16[4,16,1024]{2,1,0:T(8,128)(2,1)}) custom-call(bf16[4,64,8192]{2,1,0:T(8,128)(2,1)} %bitcast.4, bf16[4,4,32,1024]{3,2,1,0:T(8,128)(2,1)} %copy-done.1), custom_call_target="tpu_custom_call" | custom-call | flops 1572864 | bytes 1572864 | tf_op jit(solution)/shard_map/first_sum/pallas_call | solution.py:123
  70.3 3.0 %collective-permute-start.3 = (bf16[4,16,1024]{2,1,0:T(8,128)(2,1)}, bf16[4,16,1024]{2,1,0:T(8,128)(2,1)S(1)}, u32[]{:S(2)}, u32[]{:S(2)}) collective-permute-start(bf16[4,16,1024]{2,1,0:T(8,128)(2,1)} %get-tuple-element.29), channel_id=1, source_target_pairs={{0,8},{4,12},{8,0},{12,4},{16,24},{20,28},{24,16},{28,20},{1,9},{5... | collective-permute-start | bytes 393224 | tf_op jit(solution)/shard_map/ppermute | solution.py:277
  73.3 1.5 %collective-permute-start.4 = (bf16[4,16,1024]{2,1,0:T(8,128)(2,1)}, bf16[4,16,1024]{2,1,0:T(8,128)(2,1)S(1)}, u32[]{:S(2)}, u32[]{:S(2)}) collective-permute-start(bf16[4,16,1024]{2,1,0:T(8,128)(2,1)} %get-tuple-element.30), channel_id=1, source_target_pairs={{0,16},{4,20},{8,24},{12,28},{16,0},{20,4},{24,8},{28,12},{1,17},{... | collective-permute-start | bytes 393224 | tf_op jit(solution)/shard_map/ppermute | solution.py:277
  76.4 2.2 %first_sum.3 = (bf16[4,16,1024]{2,1,0:T(8,128)(2,1)}, bf16[4,16,1024]{2,1,0:T(8,128)(2,1)}, bf16[4,16,1024]{2,1,0:T(8,128)(2,1)}, bf16[4,16,1024]{2,1,0:T(8,128)(2,1)}) custom-call(bf16[4,64,8192]{2,1,0:T(8,128)(2,1)} %bitcast.5, bf16[4,4,32,1024]{3,2,1,0:T(8,128)(2,1)} %copy-done), custom_call_target="tpu_custom_call" | custom-call | flops 1572864 | bytes 1572864 | tf_op jit(solution)/shard_map/first_sum/pallas_call | solution.py:123
  78.6 1.6 %collective-permute-start.13 = (bf16[4,16,1024]{2,1,0:T(8,128)(2,1)}, bf16[4,16,1024]{2,1,0:T(8,128)(2,1)S(1)}, u32[]{:S(2)}, u32[]{:S(2)}) collective-permute-start(bf16[4,16,1024]{2,1,0:T(8,128)(2,1)} %get-tuple-element.39), channel_id=1, source_target_pairs={{0,8},{4,12},{8,0},{12,4},{16,24},{20,28},{24,16},{28,20},{1,9},{5... | collective-permute-start | bytes 393224 | tf_op jit(solution)/shard_map/ppermute | solution.py:277
  80.7 1.6 %collective-permute-start.2 = (bf16[4,16,1024]{2,1,0:T(8,128)(2,1)S(1)}, bf16[4,16,1024]{2,1,0:T(8,128)(2,1)S(1)}, u32[]{:S(2)}, u32[]{:S(2)}) collective-permute-start(bf16[4,16,1024]{2,1,0:T(8,128)(2,1)S(1)} %copy-done.28), channel_id=1, source_target_pairs={{0,16},{4,20},{8,24},{12,28},{16,0},{20,4},{24,8},{28,12},{1,17},{... | collective-permute-start | bytes 393224 | tf_op jit(solution)/shard_map/ppermute | solution.py:277
  82.9 2.0 %second_sum.2 = (bf16[4,16,1024]{2,1,0:T(8,128)(2,1)}, bf16[4,16,1024]{2,1,0:T(8,128)(2,1)}) custom-call(bf16[4,64,8192]{2,1,0:T(8,128)(2,1)} %bitcast.6, bf16[4,4,32,1024]{3,2,1,0:T(8,128)(2,1)} %copy-done.1, bf16[4,16,1024]{2,1,0:T(8,128)(2,1)} %copy-done.18, bf16[4,16,1024]{2,1,0:T(8,128)(2,1)} %copy-done.19), custom_call_target="tpu_custom_call" | custom-call | flops 1048576 | bytes 1048576 | tf_op jit(solution)/shard_map/second_sum/pallas_call | solution.py:123
  86.1 1.6 %collective-permute-start.11 = (bf16[4,16,1024]{2,1,0:T(8,128)(2,1)S(1)}, bf16[4,16,1024]{2,1,0:T(8,128)(2,1)S(1)}, u32[]{:S(2)}, u32[]{:S(2)}) collective-permute-start(bf16[4,16,1024]{2,1,0:T(8,128)(2,1)S(1)} %copy-done.27), channel_id=1, source_target_pairs={{0,8},{4,12},{8,0},{12,4},{16,24},{20,28},{24,16},{28,20},{1,9},{5... | collective-permute-start | bytes 393224 | tf_op jit(solution)/shard_map/ppermute | solution.py:277
  87.7 1.5 %collective-permute-start.12 = (bf16[4,16,1024]{2,1,0:T(8,128)(2,1)S(1)}, bf16[4,16,1024]{2,1,0:T(8,128)(2,1)S(1)}, u32[]{:S(2)}, u32[]{:S(2)}) collective-permute-start(bf16[4,16,1024]{2,1,0:T(8,128)(2,1)S(1)} %copy-done.26), channel_id=1, source_target_pairs={{0,16},{4,20},{8,24},{12,28},{16,0},{20,4},{24,8},{28,12},{1,17},{... | collective-permute-start | bytes 393224 | tf_op jit(solution)/shard_map/ppermute | solution.py:277
  89.2 2.0 %second_sum.3 = (bf16[4,16,1024]{2,1,0:T(8,128)(2,1)}, bf16[4,16,1024]{2,1,0:T(8,128)(2,1)}) custom-call(bf16[4,64,8192]{2,1,0:T(8,128)(2,1)} %bitcast.7, bf16[4,4,32,1024]{3,2,1,0:T(8,128)(2,1)} %copy-done, bf16[4,16,1024]{2,1,0:T(8,128)(2,1)} %copy-done.14, bf16[4,16,1024]{2,1,0:T(8,128)(2,1)} %copy-done.15), custom_call_target="tpu_custom_call" | custom-call | flops 1048576 | bytes 1048576 | tf_op jit(solution)/shard_map/second_sum/pallas_call | solution.py:123
  93.2 2.1 %group_sum.2 = (f32[32,1024]{1,0:T(8,128)}, bf16[32,1024]{1,0:T(8,128)(2,1)}, bf16[32,1024]{1,0:T(8,128)(2,1)}, bf16[32,1024]{1,0:T(8,128)(2,1)}) custom-call(bf16[4,64,8192]{2,1,0:T(8,128)(2,1)} %bitcast.8, bf16[4,4,32,1024]{3,2,1,0:T(8,128)(2,1)} %copy-done.1, bf16[4,16,1024]{2,1,0:T(8,128)(2,1)} %copy-done.8, bf16[4,16,1024]{2,1,0:T(8,128)(2,1)} %copy-done.10, ...), custom_call_target="tpu_custom_call" | custom-call | flops 1310720 | bytes 1310720 | tf_op jit(solution)/shard_map/group_sum/pallas_call | solution.py:173
  95.3 1.6 %collective-permute-start.7 = (bf16[32,1024]{1,0:T(8,128)(2,1)}, bf16[32,1024]{1,0:T(8,128)(2,1)S(1)}, u32[]{:S(2)}, u32[]{:S(2)}) collective-permute-start(bf16[32,1024]{1,0:T(8,128)(2,1)} %get-tuple-element.34), channel_id=1, source_target_pairs={{0,1},{1,2},{2,3},{3,0},{4,5},{5,6},{6,7},{7,4},{8,9},{9,10},{10,1... | collective-permute-start | bytes 196616 | tf_op jit(solution)/shard_map/ppermute | solution.py:281
  96.9 2.6 %collective-permute-start.8 = (bf16[32,1024]{1,0:T(8,128)(2,1)}, bf16[32,1024]{1,0:T(8,128)(2,1)S(1)}, u32[]{:S(2)}, u32[]{:S(2)}) collective-permute-start(bf16[32,1024]{1,0:T(8,128)(2,1)} %get-tuple-element.35), channel_id=1, source_target_pairs={{0,2},{1,3},{2,0},{3,1},{4,6},{5,7},{6,4},{7,5},{8,10},{9,11},{10,... | collective-permute-start | bytes 196616 | tf_op jit(solution)/shard_map/ppermute | solution.py:281
  102.2 2.1 %group_sum.3 = (f32[32,1024]{1,0:T(8,128)}, bf16[32,1024]{1,0:T(8,128)(2,1)}, bf16[32,1024]{1,0:T(8,128)(2,1)}, bf16[32,1024]{1,0:T(8,128)(2,1)}) custom-call(bf16[4,64,8192]{2,1,0:T(8,128)(2,1)} %bitcast.9, bf16[4,4,32,1024]{3,2,1,0:T(8,128)(2,1)} %copy-done, bf16[4,16,1024]{2,1,0:T(8,128)(2,1)} %copy-done.9, bf16[4,16,1024]{2,1,0:T(8,128)(2,1)} %copy-done.11, ...), custom_call_target="tpu_custom_call" | custom-call | flops 1310720 | bytes 1310720 | tf_op jit(solution)/shard_map/group_sum/pallas_call | solution.py:173
  105.4 2.9 %collective-permute-start.19 = (bf16[32,1024]{1,0:T(8,128)(2,1)}, bf16[32,1024]{1,0:T(8,128)(2,1)S(1)}, u32[]{:S(2)}, u32[]{:S(2)}) collective-permute-start(bf16[32,1024]{1,0:T(8,128)(2,1)} %get-tuple-element.46), channel_id=1, source_target_pairs={{0,3},{1,0},{2,1},{3,2},{4,7},{5,4},{6,5},{7,6},{8,11},{9,8},{10,9... | collective-permute-start | bytes 196616 | tf_op jit(solution)/shard_map/ppermute | solution.py:281
  108.9 2.0 %weights.2.refs_0_ = bf16[32,1024]{1,0:T(8,128)(2,1)} custom-call(f32[32,1024]{1,0:T(8,128)} %get-tuple-element.33.refs_0_, bf16[32,1024]{1,0:T(8,128)(2,1)} %copy-done.2, bf16[32,1024]{1,0:T(8,128)(2,1)} %copy-done.3, bf16[32,1024]{1,0:T(8,128)(2,1)} %copy-done.4, f32[64,1024]{1,0:T(8,128)} %refs_4_.3, f32[64,1024]{1,0:T(8,128)} %refs_5_.3, f32[64,1024]{1,0:T(8,128)} %refs_6_.3), custom_call_target="tpu_custom_call" | custom-call | flops 786432 | bytes 786432 | tf_op jit(solution)/shard_map/weights/pallas_call | solution.py:208
  111.4 1.5 %collective-permute-start.21 = (bf16[32,1024]{1,0:T(8,128)(2,1)}, bf16[32,1024]{1,0:T(8,128)(2,1)S(1)}, u32[]{:S(2)}, u32[]{:S(2)}) collective-permute-start(bf16[32,1024]{1,0:T(8,128)(2,1)} %weights.2.refs_0_), channel_id=1, source_target_pairs={{0,2},{1,3},{2,0},{3,1},{4,6},{5,7},{6,4},{7,5},{8,10},{9,11},{10,... | collective-permute-start | bytes 196616 | tf_op jit(solution)/shard_map/ppermute | solution.py:281
  112.9 2.9 %collective-permute-start.22 = (bf16[32,1024]{1,0:T(8,128)(2,1)}, bf16[32,1024]{1,0:T(8,128)(2,1)S(1)}, u32[]{:S(2)}, u32[]{:S(2)}) collective-permute-start(bf16[32,1024]{1,0:T(8,128)(2,1)} %weights.2.refs_0_), channel_id=1, source_target_pairs={{0,3},{1,0},{2,1},{3,2},{4,7},{5,4},{6,5},{7,6},{8,11},{9,8},{10,9... | collective-permute-start | bytes 196616 | tf_op jit(solution)/shard_map/ppermute | solution.py:281
  116.5 2.0 %weights.3.refs_4_ = bf16[32,1024]{1,0:T(8,128)(2,1)} custom-call(f32[32,1024]{1,0:T(8,128)} %get-tuple-element.43.refs_4_.refs_0_, bf16[32,1024]{1,0:T(8,128)(2,1)} %copy-done.5, bf16[32,1024]{1,0:T(8,128)(2,1)} %copy-done.6, bf16[32,1024]{1,0:T(8,128)(2,1)} %copy-done.7, f32[64,1024]{1,0:T(8,128)} %refs_4_.3, f32[64,1024]{1,0:T(8,128)} %refs_5_.3, ...), custom_call_target="tpu_custom_call" | custom-call | flops 786432 | bytes 786432 | tf_op jit(solution)/shard_map/weights/pallas_call | solution.py:208
  119.5 2.9 %collective-permute-start.25 = (bf16[32,1024]{1,0:T(8,128)(2,1)}, bf16[32,1024]{1,0:T(8,128)(2,1)S(1)}, u32[]{:S(2)}, u32[]{:S(2)}) collective-permute-start(bf16[32,1024]{1,0:T(8,128)(2,1)} %weights.3.refs_4_), channel_id=1, source_target_pairs={{0,3},{1,0},{2,1},{3,2},{4,7},{5,4},{6,5},{7,6},{8,11},{9,8},{10,9... | collective-permute-start | bytes 196616 | tf_op jit(solution)/shard_map/ppermute | solution.py:281
  122.4 2.5 %finish.1 = (f32[64,1024]{1,0:T(8,128)}, f32[64,1024]{1,0:T(8,128)}, f32[64,1024]{1,0:T(8,128)}) custom-call(f32[32,1024]{1,0:T(8,128)} %get-tuple-element.33.refs_0_, bf16[32,1024]{1,0:T(8,128)(2,1)} %copy-done.2, bf16[32,1024]{1,0:T(8,128)(2,1)} %copy-done.3, bf16[32,1024]{1,0:T(8,128)(2,1)} %copy-done.4, f32[32,1024]{1,0:T(8,128)} %get-tuple-element.43.refs_4_.refs_0_, ...), custom_call_target="tpu_custom_call" | custom-call | flops 2228224 | bytes 2228224 | tf_op jit(solution)/shard_map/finish/pallas_call | solution.py:238
  126.3 17.1 %assemble.1 = bf16[4,64,1024]{2,1,0:T(8,128)(2,1)} custom-call(bf16[32,1024]{1,0:T(8,128)(2,1)} %weights.2.refs_0_, bf16[32,1024]{1,0:T(8,128)(2,1)} %copy-done.20, bf16[32,1024]{1,0:T(8,128)(2,1)} %copy-done.21, bf16[32,1024]{1,0:T(8,128)(2,1)} %copy-done.22, bf16[32,1024]{1,0:T(8,128)(2,1)} %weights.3.refs_4_, bf16[32,1024]{1,0:T(8,128)(2,1)} %copy-done.23, ...), custom_call_target="tpu_custom_call" | custom-call | flops 1048576 | bytes 1048576 | tf_op jit(solution)/shard_map/assemble/pallas_call | solution.py:264
  (98 shorter events, 15.3 us)
Async XLA Ops:
  33.6 33.6 %collective-permute-start = (bf16[4,4,32,1024]{3,2,1,0:T(8,128)(2,1)}, bf16[4,4,32,1024]{3,2,1,0:T(8,128)(2,1)S(1)}, u32[]{:S(2)}, u32[]{:S(2)}) collective-permute-start(bf16[4,4,32,1024]{3,2,1,0:T(8,128)(2,1)} %pack.2), channel_id=1, source_target_pairs={{0,4},{4,0},{8,12},{12,8},{16,20},{20,16},{24,28},{28,24},{1,5},{5... | collective-permute-start | bytes 3145736 | tf_op jit(solution)/shard_map/ppermute | solution.py:297
  67.0 8.4 %collective-permute-start.10 = (bf16[4,4,32,1024]{3,2,1,0:T(8,128)(2,1)}, bf16[4,4,32,1024]{3,2,1,0:T(8,128)(2,1)S(1)}, u32[]{:S(2)}, u32[]{:S(2)}) collective-permute-start(bf16[4,4,32,1024]{3,2,1,0:T(8,128)(2,1)} %pack.3), channel_id=1, source_target_pairs={{0,4},{4,0},{8,12},{12,8},{16,20},{20,16},{24,28},{28,24},{1,5},{5... | collective-permute-start | bytes 3145736 | tf_op jit(solution)/shard_map/ppermute | solution.py:297
  70.3 10.4 %collective-permute-start.3 = (bf16[4,16,1024]{2,1,0:T(8,128)(2,1)}, bf16[4,16,1024]{2,1,0:T(8,128)(2,1)S(1)}, u32[]{:S(2)}, u32[]{:S(2)}) collective-permute-start(bf16[4,16,1024]{2,1,0:T(8,128)(2,1)} %get-tuple-element.29), channel_id=1, source_target_pairs={{0,8},{4,12},{8,0},{12,4},{16,24},{20,28},{24,16},{28,20},{1,9},{5... | collective-permute-start | bytes 393224 | tf_op jit(solution)/shard_map/ppermute | solution.py:277
  73.3 8.9 %collective-permute-start.4 = (bf16[4,16,1024]{2,1,0:T(8,128)(2,1)}, bf16[4,16,1024]{2,1,0:T(8,128)(2,1)S(1)}, u32[]{:S(2)}, u32[]{:S(2)}) collective-permute-start(bf16[4,16,1024]{2,1,0:T(8,128)(2,1)} %get-tuple-element.30), channel_id=1, source_target_pairs={{0,16},{4,20},{8,24},{12,28},{16,0},{20,4},{24,8},{28,12},{1,17},{... | collective-permute-start | bytes 393224 | tf_op jit(solution)/shard_map/ppermute | solution.py:277
  74.8 10.7 %collective-permute-start.1 = (bf16[4,16,1024]{2,1,0:T(8,128)(2,1)}, bf16[4,16,1024]{2,1,0:T(8,128)(2,1)S(1)}, u32[]{:S(2)}, u32[]{:S(2)}) collective-permute-start(bf16[4,16,1024]{2,1,0:T(8,128)(2,1)} %get-tuple-element.27), channel_id=1, source_target_pairs={{0,8},{4,12},{8,0},{12,4},{16,24},{20,28},{24,16},{28,20},{1,9},{5... | collective-permute-start | bytes 393224 | tf_op jit(solution)/shard_map/ppermute | solution.py:277
  78.6 7.5 %collective-permute-start.13 = (bf16[4,16,1024]{2,1,0:T(8,128)(2,1)}, bf16[4,16,1024]{2,1,0:T(8,128)(2,1)S(1)}, u32[]{:S(2)}, u32[]{:S(2)}) collective-permute-start(bf16[4,16,1024]{2,1,0:T(8,128)(2,1)} %get-tuple-element.39), channel_id=1, source_target_pairs={{0,8},{4,12},{8,0},{12,4},{16,24},{20,28},{24,16},{28,20},{1,9},{5... | collective-permute-start | bytes 393224 | tf_op jit(solution)/shard_map/ppermute | solution.py:277
  80.1 7.5 %collective-permute-start.14 = (bf16[4,16,1024]{2,1,0:T(8,128)(2,1)}, bf16[4,16,1024]{2,1,0:T(8,128)(2,1)S(1)}, u32[]{:S(2)}, u32[]{:S(2)}) collective-permute-start(bf16[4,16,1024]{2,1,0:T(8,128)(2,1)} %get-tuple-element.40), channel_id=1, source_target_pairs={{0,16},{4,20},{8,24},{12,28},{16,0},{20,4},{24,8},{28,12},{1,17},{... | collective-permute-start | bytes 393224 | tf_op jit(solution)/shard_map/ppermute | solution.py:277
  80.7 10.5 %collective-permute-start.2 = (bf16[4,16,1024]{2,1,0:T(8,128)(2,1)S(1)}, bf16[4,16,1024]{2,1,0:T(8,128)(2,1)S(1)}, u32[]{:S(2)}, u32[]{:S(2)}) collective-permute-start(bf16[4,16,1024]{2,1,0:T(8,128)(2,1)S(1)} %copy-done.28), channel_id=1, source_target_pairs={{0,16},{4,20},{8,24},{12,28},{16,0},{20,4},{24,8},{28,12},{1,17},{... | collective-permute-start | bytes 393224 | tf_op jit(solution)/shard_map/ppermute | solution.py:277
  84.9 7.0 %collective-permute-start.5 = (bf16[4,16,1024]{2,1,0:T(8,128)(2,1)}, bf16[4,16,1024]{2,1,0:T(8,128)(2,1)S(1)}, u32[]{:S(2)}, u32[]{:S(2)}) collective-permute-start(bf16[4,16,1024]{2,1,0:T(8,128)(2,1)} %get-tuple-element.31), channel_id=1, source_target_pairs={{0,16},{4,20},{8,24},{12,28},{16,0},{20,4},{24,8},{28,12},{1,17},{... | collective-permute-start | bytes 393224 | tf_op jit(solution)/shard_map/ppermute | solution.py:277
  85.6 6.8 %collective-permute-start.6 = (bf16[4,16,1024]{2,1,0:T(8,128)(2,1)}, bf16[4,16,1024]{2,1,0:T(8,128)(2,1)S(1)}, u32[]{:S(2)}, u32[]{:S(2)}) collective-permute-start(bf16[4,16,1024]{2,1,0:T(8,128)(2,1)} %get-tuple-element.32), channel_id=1, source_target_pairs={{0,8},{4,12},{8,0},{12,4},{16,24},{20,28},{24,16},{28,20},{1,9},{5... | collective-permute-start | bytes 393224 | tf_op jit(solution)/shard_map/ppermute | solution.py:277
  86.1 10.8 %collective-permute-start.11 = (bf16[4,16,1024]{2,1,0:T(8,128)(2,1)S(1)}, bf16[4,16,1024]{2,1,0:T(8,128)(2,1)S(1)}, u32[]{:S(2)}, u32[]{:S(2)}) collective-permute-start(bf16[4,16,1024]{2,1,0:T(8,128)(2,1)S(1)} %copy-done.27), channel_id=1, source_target_pairs={{0,8},{4,12},{8,0},{12,4},{16,24},{20,28},{24,16},{28,20},{1,9},{5... | collective-permute-start | bytes 393224 | tf_op jit(solution)/shard_map/ppermute | solution.py:277
  87.7 11.8 %collective-permute-start.12 = (bf16[4,16,1024]{2,1,0:T(8,128)(2,1)S(1)}, bf16[4,16,1024]{2,1,0:T(8,128)(2,1)S(1)}, u32[]{:S(2)}, u32[]{:S(2)}) collective-permute-start(bf16[4,16,1024]{2,1,0:T(8,128)(2,1)S(1)} %copy-done.26), channel_id=1, source_target_pairs={{0,16},{4,20},{8,24},{12,28},{16,0},{20,4},{24,8},{28,12},{1,17},{... | collective-permute-start | bytes 393224 | tf_op jit(solution)/shard_map/ppermute | solution.py:277
  91.2 9.7 %collective-permute-start.15 = (bf16[4,16,1024]{2,1,0:T(8,128)(2,1)}, bf16[4,16,1024]{2,1,0:T(8,128)(2,1)S(1)}, u32[]{:S(2)}, u32[]{:S(2)}) collective-permute-start(bf16[4,16,1024]{2,1,0:T(8,128)(2,1)} %get-tuple-element.41), channel_id=1, source_target_pairs={{0,16},{4,20},{8,24},{12,28},{16,0},{20,4},{24,8},{28,12},{1,17},{... | collective-permute-start | bytes 393224 | tf_op jit(solution)/shard_map/ppermute | solution.py:277
  91.9 9.0 %collective-permute-start.16 = (bf16[4,16,1024]{2,1,0:T(8,128)(2,1)}, bf16[4,16,1024]{2,1,0:T(8,128)(2,1)S(1)}, u32[]{:S(2)}, u32[]{:S(2)}) collective-permute-start(bf16[4,16,1024]{2,1,0:T(8,128)(2,1)} %get-tuple-element.42), channel_id=1, source_target_pairs={{0,8},{4,12},{8,0},{12,4},{16,24},{20,28},{24,16},{28,20},{1,9},{5... | collective-permute-start | bytes 393224 | tf_op jit(solution)/shard_map/ppermute | solution.py:277
  95.3 10.1 %collective-permute-start.7 = (bf16[32,1024]{1,0:T(8,128)(2,1)}, bf16[32,1024]{1,0:T(8,128)(2,1)S(1)}, u32[]{:S(2)}, u32[]{:S(2)}) collective-permute-start(bf16[32,1024]{1,0:T(8,128)(2,1)} %get-tuple-element.34), channel_id=1, source_target_pairs={{0,1},{1,2},{2,3},{3,0},{4,5},{5,6},{6,7},{7,4},{8,9},{9,10},{10,1... | collective-permute-start | bytes 196616 | tf_op jit(solution)/shard_map/ppermute | solution.py:281
  96.9 11.3 %collective-permute-start.8 = (bf16[32,1024]{1,0:T(8,128)(2,1)}, bf16[32,1024]{1,0:T(8,128)(2,1)S(1)}, u32[]{:S(2)}, u32[]{:S(2)}) collective-permute-start(bf16[32,1024]{1,0:T(8,128)(2,1)} %get-tuple-element.35), channel_id=1, source_target_pairs={{0,2},{1,3},{2,0},{3,1},{4,6},{5,7},{6,4},{7,5},{8,10},{9,11},{10,... | collective-permute-start | bytes 196616 | tf_op jit(solution)/shard_map/ppermute | solution.py:281
  99.5 8.7 %collective-permute-start.9 = (bf16[32,1024]{1,0:T(8,128)(2,1)}, bf16[32,1024]{1,0:T(8,128)(2,1)S(1)}, u32[]{:S(2)}, u32[]{:S(2)}) collective-permute-start(bf16[32,1024]{1,0:T(8,128)(2,1)} %get-tuple-element.36), channel_id=1, source_target_pairs={{0,3},{1,0},{2,1},{3,2},{4,7},{5,4},{6,5},{7,6},{8,11},{9,8},{10,9... | collective-permute-start | bytes 196616 | tf_op jit(solution)/shard_map/ppermute | solution.py:281
  104.3 8.6 %collective-permute-start.17 = (bf16[32,1024]{1,0:T(8,128)(2,1)}, bf16[32,1024]{1,0:T(8,128)(2,1)S(1)}, u32[]{:S(2)}, u32[]{:S(2)}) collective-permute-start(bf16[32,1024]{1,0:T(8,128)(2,1)} %get-tuple-element.44), channel_id=1, source_target_pairs={{0,1},{1,2},{2,3},{3,0},{4,5},{5,6},{6,7},{7,4},{8,9},{9,10},{10,1... | collective-permute-start | bytes 196616 | tf_op jit(solution)/shard_map/ppermute | solution.py:281
  105.0 10.8 %collective-permute-start.18 = (bf16[32,1024]{1,0:T(8,128)(2,1)}, bf16[32,1024]{1,0:T(8,128)(2,1)S(1)}, u32[]{:S(2)}, u32[]{:S(2)}) collective-permute-start(bf16[32,1024]{1,0:T(8,128)(2,1)} %get-tuple-element.45), channel_id=1, source_target_pairs={{0,2},{1,3},{2,0},{3,1},{4,6},{5,7},{6,4},{7,5},{8,10},{9,11},{10,... | collective-permute-start | bytes 196616 | tf_op jit(solution)/shard_map/ppermute | solution.py:281
  105.4 10.5 %collective-permute-start.19 = (bf16[32,1024]{1,0:T(8,128)(2,1)}, bf16[32,1024]{1,0:T(8,128)(2,1)S(1)}, u32[]{:S(2)}, u32[]{:S(2)}) collective-permute-start(bf16[32,1024]{1,0:T(8,128)(2,1)} %get-tuple-element.46), channel_id=1, source_target_pairs={{0,3},{1,0},{2,1},{3,2},{4,7},{5,4},{6,5},{7,6},{8,11},{9,8},{10,9... | collective-permute-start | bytes 196616 | tf_op jit(solution)/shard_map/ppermute | solution.py:281
  110.9 8.6 %collective-permute-start.20 = (bf16[32,1024]{1,0:T(8,128)(2,1)}, bf16[32,1024]{1,0:T(8,128)(2,1)S(1)}, u32[]{:S(2)}, u32[]{:S(2)}) collective-permute-start(bf16[32,1024]{1,0:T(8,128)(2,1)} %weights.2.refs_0_), channel_id=1, source_target_pairs={{0,1},{1,2},{2,3},{3,0},{4,5},{5,6},{6,7},{7,4},{8,9},{9,10},{10,1... | collective-permute-start | bytes 196616 | tf_op jit(solution)/shard_map/ppermute | solution.py:281
  111.4 13.5 %collective-permute-start.21 = (bf16[32,1024]{1,0:T(8,128)(2,1)}, bf16[32,1024]{1,0:T(8,128)(2,1)S(1)}, u32[]{:S(2)}, u32[]{:S(2)}) collective-permute-start(bf16[32,1024]{1,0:T(8,128)(2,1)} %weights.2.refs_0_), channel_id=1, source_target_pairs={{0,2},{1,3},{2,0},{3,1},{4,6},{5,7},{6,4},{7,5},{8,10},{9,11},{10,... | collective-permute-start | bytes 196616 | tf_op jit(solution)/shard_map/ppermute | solution.py:281
  112.9 12.0 %collective-permute-start.22 = (bf16[32,1024]{1,0:T(8,128)(2,1)}, bf16[32,1024]{1,0:T(8,128)(2,1)S(1)}, u32[]{:S(2)}, u32[]{:S(2)}) collective-permute-start(bf16[32,1024]{1,0:T(8,128)(2,1)} %weights.2.refs_0_), channel_id=1, source_target_pairs={{0,3},{1,0},{2,1},{3,2},{4,7},{5,4},{6,5},{7,6},{8,11},{9,8},{10,9... | collective-permute-start | bytes 196616 | tf_op jit(solution)/shard_map/ppermute | solution.py:281
  118.5 6.5 %collective-permute-start.24 = (bf16[32,1024]{1,0:T(8,128)(2,1)}, bf16[32,1024]{1,0:T(8,128)(2,1)S(1)}, u32[]{:S(2)}, u32[]{:S(2)}) collective-permute-start(bf16[32,1024]{1,0:T(8,128)(2,1)} %weights.3.refs_4_), channel_id=1, source_target_pairs={{0,2},{1,3},{2,0},{3,1},{4,6},{5,7},{6,4},{7,5},{8,10},{9,11},{10,... | collective-permute-start | bytes 196616 | tf_op jit(solution)/shard_map/ppermute | solution.py:281
  (31 other events, 81.9 us)

commit v2 on v0

v2 whole, which is shorter than its diff:
```python
import functools

import jax
import jax.numpy as jnp
from jax import lax
from jax.experimental import pallas as pl
from jax.experimental.pallas import tpu as pltpu
from jax.sharding import PartitionSpec as P

beta_first = 0.9
beta_second = 0.95
learn_rate = 0.05
decay_rate = 0.1
adam_eps = 1e-05
bias_first = 1.0 - 0.9**10
bias_second = 1.0 - 0.95**10

CORES = 2
SUPERS = 2
STEP = 16
ANY = pl.BlockSpec(memory_space=pl.ANY)
VMEM = pl.BlockSpec(memory_space=pltpu.VMEM)


def local_kernel(kernel, out_shape, operands, name, in_specs=None, out_specs=None, sems=0):
    if in_specs is None:
        in_specs = [VMEM] * len(operands)
    if out_specs is None:
        out_specs = jax.tree.map(lambda _: VMEM, out_shape)
    nbytes = sum(s.size * s.dtype.itemsize for s in jax.tree.leaves(out_shape)) * 3
    return pl.pallas_call(
        kernel,
        out_shape=out_shape,
        in_specs=in_specs,
        out_specs=out_specs,
        scratch_shapes=[pltpu.SemaphoreType.DMA((sems,))] if sems else [],
        compiler_params=pltpu.CompilerParams(vmem_limit_bytes=4 << 20),
        cost_estimate=pl.CostEstimate(flops=nbytes, bytes_accessed=nbytes, transcendentals=0),
        name=name,
    )(*operands)


def bf16(*shape):
    return jax.ShapeDtypeStruct(shape, jnp.bfloat16)


def place():
    me = lax.axis_index("inner")
    return me // CORES, lax.rem(me, CORES)


def transfer(sources, targets, sems):
    copies = [pltpu.make_async_copy(s, d, sems.at[i]) for i, (s, d) in enumerate(zip(sources, targets))]
    for copy in copies:
        copy.start()
    for copy in copies:
        copy.wait()


def load(grads, parts, width, chips, name):
    outer = grads.shape[0]

    def kernel(grad_ref, *refs):
        *outs, sems = refs
        _, core = place()
        sources, targets = [], []
        for ((base, depth), side), out in zip(parts, outs):
            for chip in range(chips):
                block = CORES * chip + (1 - core if side else core)
                start = pl.multiple_of(block * width, width)
                sources.append(grad_ref.at[:, pl.ds(base, depth), pl.ds(start, width)])
                targets.append(out.at[chip])
        transfer(sources, targets, sems)

    shapes = [bf16(chips, outer, depth, width) for (_, depth), _ in parts]
    return local_kernel(kernel, shapes, [grads], name, in_specs=[ANY], sems=chips * len(parts))


def sum_of(terms):
    value = terms[0].astype(jnp.float32)
    for term in terms[1:]:
        value = value + term.astype(jnp.float32)
    return value


def each_step(blocks, depth, do):
    per = depth // STEP

    def step(i, carry):
        do(i // per, lax.rem(i, per) * STEP)
        return carry

    lax.fori_loop(0, blocks * per, step, 0)


def rows_at(start):
    return pl.ds(pl.multiple_of(start, STEP), STEP)


def chip_sums(grads, core_in, runs, name):
    _, outer, _, width = grads.shape

    def kernel(grad_ref, core_ref, *outs):
        chip, _ = place()
        for (base, depth, targets), out in zip(runs, outs):
            for at, target in enumerate(targets):
                to = target(chip)

                def do(block, start, at=at, to=to, base=base, out=out):
                    here = rows_at(base + start)
                    value = sum_of([grad_ref[to, block, here], core_ref[to, block, here]])
                    out[at, block, rows_at(start)] = value.astype(out.dtype)

                each_step(outer, depth, do)

    shapes = [bf16(len(targets), outer, depth, width) for _, depth, targets in runs]
    return local_kernel(kernel, shapes, [grads, core_in], name)


def pair_sums(grads, core_in, got, runs, name):
    _, outer, _, width = grads.shape

    def kernel(grad_ref, core_ref, *refs):
        chip, _ = place()
        for (base, depth, target), got_ref, out in zip(runs, refs, refs[len(got) :]):
            to = target(chip)

            def do(block, start, to=to, base=base, out=out, got_ref=got_ref):
                here, there = rows_at(base + start), rows_at(start)
                value = sum_of([grad_ref[to, block, here], core_ref[to, block, here], got_ref[1, block, there]])
                out[block, there] = value.astype(out.dtype)

            each_step(outer, depth, do)

    shapes = [bf16(outer, depth, width) for _, depth, _ in runs]
    return local_kernel(kernel, shapes, [grads, core_in, *got], name)


def group_sum(grads, core_in, extra, runs, name):
    _, outer, depth, width = grads.shape

    def kernel(grad_ref, core_ref, *refs):
        extra_refs, outs = refs[: len(extra)], refs[len(extra) :]
        chip, _ = place()
        here = lax.axis_index("outer")
        for shift in list(range(1, outer)) + [0]:
            block = lax.rem(here + shift, outer)
            for base, size, terms in runs:

                def do(_, start, block=block, base=base, terms=terms, out=outs[shift]):
                    rows = rows_at(base + start)
                    values = [grad_ref[chip, block, rows], core_ref[chip, block, rows]]
                    values += [
                        extra_refs[i][block, rows_at(start)] if j is None else extra_refs[i][j, block, rows_at(start)]
                        for i, j in terms
                    ]
                    out[rows] = sum_of(values).astype(out.dtype)

                each_step(1, size, do)

    shapes = [jax.ShapeDtypeStruct((depth, width), jnp.bfloat16 if s else jnp.float32) for s in range(outer)]
    return local_kernel(kernel, shapes, [grads, core_in, *extra], name)


def adam(total, master, first, second):
    new_first = beta_first * first + (1.0 - beta_first) * total
    new_second = beta_second * second + (1.0 - beta_second) * total * total
    update = new_first / bias_first / (jnp.sqrt(new_second / bias_second) + adam_eps) + decay_rate * master
    return master - learn_rate * update, new_first, new_second


def weights(terms, span, state, name):
    base, depth = span

    def kernel(*refs):
        *term_refs, master_ref, first_ref, second_ref, out = refs

        def do(_, start):
            here, there = rows_at(start), rows_at(base + start)
            total = sum_of([ref[here] for ref in term_refs])
            out[here] = adam(total, master_ref[there], first_ref[there], second_ref[there])[0].astype(out.dtype)

        each_step(1, depth, do)

    return local_kernel(kernel, bf16(depth, terms[0].shape[1]), [*terms, *state], name)


def finish(groups, spans, state):
    n = len(groups[0])

    def kernel(*refs):
        master_ref, first_ref, second_ref, *outs = refs[n * len(spans) :]
        for k, (base, depth) in enumerate(spans):

            def do(_, start, k=k, base=base):
                here, there = rows_at(start), rows_at(base + start)
                total = sum_of([ref[here] for ref in refs[n * k : n * k + n]])
                for out, value in zip(outs, adam(total, master_ref[there], first_ref[there], second_ref[there])):
                    out[there] = value

            each_step(1, depth, do)

    shapes = [jax.ShapeDtypeStruct(state[0].shape, jnp.float32)] * 3
    return local_kernel(kernel, shapes, [t for group in groups for t in group] + list(state), "finish")


def assemble(groups, spans, outer, owned):
    width = groups[0][0].shape[1]

    def kernel(*refs):
        *pieces, out, sems = refs
        here = lax.axis_index("outer")
        targets = [
            out.at[lax.rem(here + outer - shift, outer), pl.ds(base, depth)]
            for base, depth in spans
            for shift in range(outer)
        ]
        transfer(pieces, targets, sems)

    operands = [piece for group in groups for piece in group]
    return local_kernel(
        kernel, bf16(outer, owned, width), operands, "assemble", out_specs=ANY, sems=len(operands)
    )


def to_chip(x, target, chips):
    pairs = [(CORES * c + k, CORES * target(c) + k) for c in range(chips) for k in range(CORES)]
    return lax.ppermute(x, "inner", pairs)


def to_group(x, shift, outer):
    return lax.ppermute(x, "outer", [(i, (i + shift) % outer) for i in range(outer)])


def flip(mask):
    return lambda chip: chip ^ mask


def onward(shift, chips):
    return lambda chip: (chip + shift) % chips


def body(gradients, master, first, second, *, inner, outer):
    depth, columns = gradients.shape[2:]
    chips, owned, width = inner // CORES, depth // outer, columns // inner
    grads = gradients.reshape(outer, owned, columns)
    state = (master, first, second)

    supers = SUPERS if owned % (2 * STEP * SUPERS) == 0 else 1
    per = owned // supers
    spans = [(k * per, per) for k in range(supers)]
    two_steps = chips == 4 and per % (2 * STEP) == 0

    theirs = [load(grads, [(span, 1)], width, chips, "load_theirs")[0] for span in spans]
    mine = [load(grads, [(span, 0)], width, chips, "load_mine")[0] for span in spans]
    core_in = [lax.ppermute(x, "inner", [(i, i ^ 1) for i in range(inner)]) for x in theirs]

    totals, copies = [], []
    for k, span in enumerate(spans):
        if two_steps:
            half = per // 2
            links = [(0, 1, 2), (half, 2, 1)]
            runs = [(base, half, (flip(a), flip(a ^ b))) for base, a, b in links]
            made = chip_sums(mine[k], core_in[k], runs, "first_sum")
            got = [to_chip(x, flip(a), chips) for x, (_, a, _) in zip(made, links)]
            runs = [(base, half, flip(b)) for base, _, b in links]
            made = pair_sums(mine[k], core_in[k], got, runs, "second_sum")
            last = [to_chip(x, flip(b), chips) for x, (_, _, b) in zip(made, links)]
            extra = got + last
            runs = [(base, half, [(h, 0), (2 + h, None)]) for h, (base, _, _) in enumerate(links)]
        else:
            moves = [onward(m, chips) for m in range(1, chips)]
            made = chip_sums(mine[k], core_in[k], [(0, per, (move,)) for move in moves], "first_sum")
            extra = [to_chip(x, move, chips) for x, move in zip(made, moves)]
            runs = [(0, per, [(i, 0) for i in range(chips - 1)])]
        kept, *sends = group_sum(mine[k], core_in[k], extra, runs, "group_sum")
        totals.append((kept, *[to_group(x, s + 1, outer) for s, x in enumerate(sends)]))
        new = weights(totals[k], span, state, "weights")
        copies.append((new, *[to_group(new, s, outer) for s in range(1, outer)]))

    results = finish(totals, spans, state)
    return (*results, assemble(copies, spans, outer, owned).reshape(depth, columns // inner))


def solution(mesh):
    return jax.shard_map(
        functools.partial(body, inner=mesh.shape["inner"], outer=mesh.shape["outer"]),
        mesh=mesh,
        in_specs=(
            P("inner", "outer", None, None),
            P("outer", "inner"),
            P("outer", "inner"),
            P("outer", "inner"),
        ),
        out_specs=(P("outer", "inner"), P("outer", "inner"), P("outer", "inner"), P(None, "inner")),
        check_vma=False,
    )
```

time: 186 us -> 53 us (0.28)
  blocking collectives: 89.3 us -> 0 us
  other arithmetic: 51.4 us -> 0 us
  local copies, waits for them, and re-layouts: 43.1 us -> 2.2 us
  starting transfers between devices: 0 us -> 31.7 us
  waiting for transfers between devices: 0 us -> 14.4 us
  Pallas kernels: 0 us -> 3.74 us
    all_to_all x2 -> x0, blocking collectives: 73.5 us -> none  [the longest x1 54.3 us: body(): lax.all_to_all(local, 'inner', split_axis=2, concat_axis=0, tiled=True)]
    unnamed x2 -> x0, other arithmetic: 47.3 us -> none
    ppermute x0 -> x22, starting transfers between devices: none -> 31.7 us  [the longest x12 21.3 us: to_group(): lax.ppermute(x, 'outer', [(i, (i + shift) % outer) for i in range(outer)])]
    unnamed x14 -> x10, local copies, waits for them, and re-layouts: 24.3 us -> 2.2 us
    reshape x1 -> x0, local copies, waits for them, and re-layouts: 17.9 us -> none  [body(): local = gradients.reshape(1, gradients.shape[2], gradients.shape[3])]
    all_gather x1 -> x0, blocking collectives: 15.8 us -> none  [body(): lax.all_gather(new_master.astype(jnp.bfloat16), 'outer', axis=0, tiled=True)]
    ppermute x0 -> x22, waiting for transfers between devices: none -> 14.4 us  [the longest x8 9.91 us: to_chip(): return lax.ppermute(x, 'inner', pairs)]
    pallas_call x0 -> x14, Pallas kernels: none -> 3.74 us  [local_kernel(): pl.pallas_call(kernel, out_shape=out_shape, in_specs=in_specs, out_specs=...]
  transfers between devices with their start and end apart: 0 -> 22, of which waited for: 0 -> 9; matrix products, arithmetic and copies ran while one was open for 0% -> 0% of each run, Pallas kernels for 0% -> 5%
where the time goes in v2:
time: 53 us; the launch traced here: 52.9 us
  starting transfers between devices  31.7 us (60%)
  waiting for transfers between devices  14.4 us (27%)
  Pallas kernels  3.74 us (7%)
  local copies, waits for them, and re-layouts  2.2 us (4%)
  between operations  0.77 us (1%)
    ppermute x12, starting transfers between devices, to_group(): lax.ppermute(x, 'outer', [(i, (i + shift) % outer) for i in range(outer)])  21.3 us
    ppermute x8, waiting for transfers between devices, to_chip(): return lax.ppermute(x, 'inner', pairs)  9.91 us
    ppermute x8, starting transfers between devices, to_chip(): return lax.ppermute(x, 'inner', pairs)  9.81 us
    pallas_call x14, Pallas kernels, local_kernel(): pl.pallas_call(kernel, out_shape=out_shape, in_specs=in_specs, out_specs=...  3.74 us
    ppermute x12, waiting for transfers between devices, to_group(): lax.ppermute(x, 'outer', [(i, (i + shift) % outer) for i in range(outer)])  2.6 us
    unnamed x10, local copies, waits for them, and re-layouts  2.2 us
    ppermute x2, waiting for transfers between devices, body(): lax.ppermute(x, 'inner', [(i, i ^ 1) for i in range(inner)])  1.91 us
  transfers between devices with their start and end apart: 22, of which 9 were waited for; matrix products, arithmetic and copies ran while one was open for 0% of the time, Pallas kernels for 5%

profile of v2, /device:TPU:0, one launch (start us, length us, event | category | flops | bytes accessed | tf_op | source)
XLA Modules:
  0.0 52.9 jit_solution(15484875715108424328)
XLA Ops:
  0.6 2.2 %copy-done = bf16[1,1,256,8192]{3,2,1,0:T(8,128)(2,1)S(1)} copy-done((bf16[1,1,256,8192]{3,2,1,0:T(8,128)(2,1)S(1)}, bf16[1,1,256,8192]{3,2,1,0:T(8,128)(2,1)}, u32[]{:S(2)}) %copy-start) | copy-done | bytes 4194328
  3.8 1.9 %collective-permute-done.core_ref = bf16[4,4,32,1024]{3,2,1,0:T(8,128)(2,1)S(1)} collective-permute-done((bf16[4,4,32,1024]{3,2,1,0:T(8,128)(2,1)S(1)}, bf16[4,4,32,1024]{3,2,1,0:T(8,128)(2,1)S(1)}, u32[]{:S(2)}, u32[]{:S(2)}) %collective-permute-start) | collective-permute-done | bytes 1048608 | tf_op jit(solution)/shard_map/ppermute | solution.py:256
  6.0 2.9 %collective-permute-start.1 = (bf16[2,4,16,1024]{3,2,1,0:T(8,128)(2,1)S(1)}, bf16[2,4,16,1024]{3,2,1,0:T(8,128)(2,1)S(1)}, u32[]{:S(2)}, u32[]{:S(2)}) collective-permute-start(bf16[2,4,16,1024]{3,2,1,0:T(8,128)(2,1)S(1)} %get-tuple-element.23), channel_id=1, source_target_pairs={{0,8},{4,12},{8,0},{12,4},{16,24},{20,28},{24,16},{28,20},{1,9},{5... | collective-permute-start | bytes 786440 | tf_op jit(solution)/shard_map/ppermute | solution.py:228
  8.9 1.5 %collective-permute-start.2 = (bf16[2,4,16,1024]{3,2,1,0:T(8,128)(2,1)S(1)}, bf16[2,4,16,1024]{3,2,1,0:T(8,128)(2,1)S(1)}, u32[]{:S(2)}, u32[]{:S(2)}) collective-permute-start(bf16[2,4,16,1024]{3,2,1,0:T(8,128)(2,1)S(1)} %get-tuple-element.24), channel_id=1, source_target_pairs={{0,16},{4,20},{8,24},{12,28},{16,0},{20,4},{24,8},{28,12},{1,17},{... | collective-permute-start | bytes 786440 | tf_op jit(solution)/shard_map/ppermute | solution.py:228
  11.9 4.1 %collective-permute-done.1.refs_0_ = bf16[2,4,16,1024]{3,2,1,0:T(8,128)(2,1)S(1)} collective-permute-done((bf16[2,4,16,1024]{3,2,1,0:T(8,128)(2,1)S(1)}, bf16[2,4,16,1024]{3,2,1,0:T(8,128)(2,1)S(1)}, u32[]{:S(2)}, u32[]{:S(2)}) %collective-permute-start.1) | collective-permute-done | bytes 262176 | tf_op jit(solution)/shard_map/ppermute | solution.py:228
  16.0 2.1 %collective-permute-done.2.refs_1_ = bf16[2,4,16,1024]{3,2,1,0:T(8,128)(2,1)S(1)} collective-permute-done((bf16[2,4,16,1024]{3,2,1,0:T(8,128)(2,1)S(1)}, bf16[2,4,16,1024]{3,2,1,0:T(8,128)(2,1)S(1)}, u32[]{:S(2)}, u32[]{:S(2)}) %collective-permute-start.2) | collective-permute-done | bytes 262176 | tf_op jit(solution)/shard_map/ppermute | solution.py:228
  18.2 1.6 %collective-permute-start.3 = (bf16[4,16,1024]{2,1,0:T(8,128)(2,1)S(1)}, bf16[4,16,1024]{2,1,0:T(8,128)(2,1)S(1)}, u32[]{:S(2)}, u32[]{:S(2)}) collective-permute-start(bf16[4,16,1024]{2,1,0:T(8,128)(2,1)S(1)} %get-tuple-element.25), channel_id=1, source_target_pairs={{0,16},{4,20},{8,24},{12,28},{16,0},{20,4},{24,8},{28,12},{1,17},{... | collective-permute-start | bytes 393224 | tf_op jit(solution)/shard_map/ppermute | solution.py:228
  20.3 1.2 %collective-permute-done.9.refs_0_ = bf16[2,4,16,1024]{3,2,1,0:T(8,128)(2,1)S(1)} collective-permute-done((bf16[2,4,16,1024]{3,2,1,0:T(8,128)(2,1)S(1)}, bf16[2,4,16,1024]{3,2,1,0:T(8,128)(2,1)S(1)}, u32[]{:S(2)}, u32[]{:S(2)}) %collective-permute-start.9) | collective-permute-done | bytes 262176 | tf_op jit(solution)/shard_map/ppermute | solution.py:228
  21.6 2.1 %collective-permute-done.10.refs_1_ = bf16[2,4,16,1024]{3,2,1,0:T(8,128)(2,1)S(1)} collective-permute-done((bf16[2,4,16,1024]{3,2,1,0:T(8,128)(2,1)S(1)}, bf16[2,4,16,1024]{3,2,1,0:T(8,128)(2,1)S(1)}, u32[]{:S(2)}, u32[]{:S(2)}) %collective-permute-start.10) | collective-permute-done | bytes 262176 | tf_op jit(solution)/shard_map/ppermute | solution.py:228
  23.8 1.6 %collective-permute-start.11 = (bf16[4,16,1024]{2,1,0:T(8,128)(2,1)S(1)}, bf16[4,16,1024]{2,1,0:T(8,128)(2,1)S(1)}, u32[]{:S(2)}, u32[]{:S(2)}) collective-permute-start(bf16[4,16,1024]{2,1,0:T(8,128)(2,1)S(1)} %get-tuple-element.33), channel_id=1, source_target_pairs={{0,16},{4,20},{8,24},{12,28},{16,0},{20,4},{24,8},{28,12},{1,17},{... | collective-permute-start | bytes 393224 | tf_op jit(solution)/shard_map/ppermute | solution.py:228
  26.5 1.6 %collective-permute-start.5 = (bf16[32,1024]{1,0:T(8,128)(2,1)S(1)}, bf16[32,1024]{1,0:T(8,128)(2,1)S(1)}, u32[]{:S(2)}, u32[]{:S(2)}) collective-permute-start(bf16[32,1024]{1,0:T(8,128)(2,1)S(1)} %get-tuple-element.28), channel_id=1, source_target_pairs={{0,1},{1,2},{2,3},{3,0},{4,5},{5,6},{6,7},{7,4},{8,9},{9,10},{10,1... | collective-permute-start | bytes 196616 | tf_op jit(solution)/shard_map/ppermute | solution.py:232
  28.1 2.6 %collective-permute-start.6 = (bf16[32,1024]{1,0:T(8,128)(2,1)S(1)}, bf16[32,1024]{1,0:T(8,128)(2,1)S(1)}, u32[]{:S(2)}, u32[]{:S(2)}) collective-permute-start(bf16[32,1024]{1,0:T(8,128)(2,1)S(1)} %get-tuple-element.29), channel_id=1, source_target_pairs={{0,2},{1,3},{2,0},{3,1},{4,6},{5,7},{6,4},{7,5},{8,10},{9,11},{10,... | collective-permute-start | bytes 196616 | tf_op jit(solution)/shard_map/ppermute | solution.py:232
  30.7 1.3 %collective-permute-start.7 = (bf16[32,1024]{1,0:T(8,128)(2,1)S(1)}, bf16[32,1024]{1,0:T(8,128)(2,1)S(1)}, u32[]{:S(2)}, u32[]{:S(2)}) collective-permute-start(bf16[32,1024]{1,0:T(8,128)(2,1)S(1)} %get-tuple-element.30), channel_id=1, source_target_pairs={{0,3},{1,0},{2,1},{3,2},{4,7},{5,4},{6,5},{7,6},{8,11},{9,8},{10,9... | collective-permute-start | bytes 196616 | tf_op jit(solution)/shard_map/ppermute | solution.py:232
  32.2 0.7 %collective-permute-start.13 = (bf16[32,1024]{1,0:T(8,128)(2,1)S(1)}, bf16[32,1024]{1,0:T(8,128)(2,1)S(1)}, u32[]{:S(2)}, u32[]{:S(2)}) collective-permute-start(bf16[32,1024]{1,0:T(8,128)(2,1)S(1)} %get-tuple-element.36), channel_id=1, source_target_pairs={{0,1},{1,2},{2,3},{3,0},{4,5},{5,6},{6,7},{7,4},{8,9},{9,10},{10,1... | collective-permute-start | bytes 196616 | tf_op jit(solution)/shard_map/ppermute | solution.py:232
  32.9 1.8 %collective-permute-start.14 = (bf16[32,1024]{1,0:T(8,128)(2,1)S(1)}, bf16[32,1024]{1,0:T(8,128)(2,1)S(1)}, u32[]{:S(2)}, u32[]{:S(2)}) collective-permute-start(bf16[32,1024]{1,0:T(8,128)(2,1)S(1)} %get-tuple-element.37), channel_id=1, source_target_pairs={{0,2},{1,3},{2,0},{3,1},{4,6},{5,7},{6,4},{7,5},{8,10},{9,11},{10,... | collective-permute-start | bytes 196616 | tf_op jit(solution)/shard_map/ppermute | solution.py:232
  34.7 1.3 %collective-permute-start.15 = (bf16[32,1024]{1,0:T(8,128)(2,1)S(1)}, bf16[32,1024]{1,0:T(8,128)(2,1)S(1)}, u32[]{:S(2)}, u32[]{:S(2)}) collective-permute-start(bf16[32,1024]{1,0:T(8,128)(2,1)S(1)} %get-tuple-element.38), channel_id=1, source_target_pairs={{0,3},{1,0},{2,1},{3,2},{4,7},{5,4},{6,5},{7,6},{8,11},{9,8},{10,9... | collective-permute-start | bytes 196616 | tf_op jit(solution)/shard_map/ppermute | solution.py:232
  36.6 1.3 %collective-permute-start.16 = (bf16[32,1024]{1,0:T(8,128)(2,1)S(1)}, bf16[32,1024]{1,0:T(8,128)(2,1)S(1)}, u32[]{:S(2)}, u32[]{:S(2)}) collective-permute-start(bf16[32,1024]{1,0:T(8,128)(2,1)S(1)} %weights.2.refs_0_), channel_id=1, source_target_pairs={{0,1},{1,2},{2,3},{3,0},{4,5},{5,6},{6,7},{7,4},{8,9},{9,10},{10,1... | collective-permute-start | bytes 196616 | tf_op jit(solution)/shard_map/ppermute | solution.py:232
  37.9 2.7 %collective-permute-start.17 = (bf16[32,1024]{1,0:T(8,128)(2,1)S(1)}, bf16[32,1024]{1,0:T(8,128)(2,1)S(1)}, u32[]{:S(2)}, u32[]{:S(2)}) collective-permute-start(bf16[32,1024]{1,0:T(8,128)(2,1)S(1)} %weights.2.refs_0_), channel_id=1, source_target_pairs={{0,2},{1,3},{2,0},{3,1},{4,6},{5,7},{6,4},{7,5},{8,10},{9,11},{10,... | collective-permute-start | bytes 196616 | tf_op jit(solution)/shard_map/ppermute | solution.py:232
  40.6 0.7 %collective-permute-start.18 = (bf16[32,1024]{1,0:T(8,128)(2,1)S(1)}, bf16[32,1024]{1,0:T(8,128)(2,1)S(1)}, u32[]{:S(2)}, u32[]{:S(2)}) collective-permute-start(bf16[32,1024]{1,0:T(8,128)(2,1)S(1)} %weights.2.refs_0_), channel_id=1, source_target_pairs={{0,3},{1,0},{2,1},{3,2},{4,7},{5,4},{6,5},{7,6},{8,11},{9,8},{10,9... | collective-permute-start | bytes 196616 | tf_op jit(solution)/shard_map/ppermute | solution.py:232
  41.9 4.7 %collective-permute-start.19 = (bf16[32,1024]{1,0:T(8,128)(2,1)S(1)}, bf16[32,1024]{1,0:T(8,128)(2,1)S(1)}, u32[]{:S(2)}, u32[]{:S(2)}) collective-permute-start(bf16[32,1024]{1,0:T(8,128)(2,1)S(1)} %weights.3.refs_4_), channel_id=1, source_target_pairs={{0,1},{1,2},{2,3},{3,0},{4,5},{5,6},{6,7},{7,4},{8,9},{9,10},{10,1... | collective-permute-start | bytes 196616 | tf_op jit(solution)/shard_map/ppermute | solution.py:232
  46.6 2.4 %collective-permute-start.21 = (bf16[32,1024]{1,0:T(8,128)(2,1)S(1)}, bf16[32,1024]{1,0:T(8,128)(2,1)S(1)}, u32[]{:S(2)}, u32[]{:S(2)}) collective-permute-start(bf16[32,1024]{1,0:T(8,128)(2,1)S(1)} %weights.3.refs_4_), channel_id=1, source_target_pairs={{0,3},{1,0},{2,1},{3,2},{4,7},{5,4},{6,5},{7,6},{8,11},{9,8},{10,9... | collective-permute-start | bytes 196616 | tf_op jit(solution)/shard_map/ppermute | solution.py:232
  49.1 1.2 %finish.1 = (f32[64,1024]{1,0:T(8,128)}, f32[64,1024]{1,0:T(8,128)}, f32[64,1024]{1,0:T(8,128)}) custom-call(f32[32,1024]{1,0:T(8,128)S(1)} %get-tuple-element.27.refs_0_, bf16[32,1024]{1,0:T(8,128)(2,1)S(1)} %collective-permute-done.5.refs_1_, bf16[32,1024]{1,0:T(8,128)(2,1)S(1)} %collective-permute-done.6.refs_2_, ...), custom_call_target="tpu_custom_call" | custom-call | flops 2359296 | bytes 2359296 | tf_op jit(solution)/shard_map/finish/pallas_call | solution.py:31
  50.2 1.8 %collective-permute-done.20.refs_6_ = bf16[32,1024]{1,0:T(8,128)(2,1)S(1)} collective-permute-done((bf16[32,1024]{1,0:T(8,128)(2,1)S(1)}, bf16[32,1024]{1,0:T(8,128)(2,1)S(1)}, u32[]{:S(2)}, u32[]{:S(2)}) %collective-permute-start.20) | collective-permute-done | bytes 65568 | tf_op jit(solution)/shard_map/ppermute | solution.py:232
  52.0 0.8 %assemble.1 = bf16[4,64,1024]{2,1,0:T(8,128)(2,1)} custom-call(bf16[32,1024]{1,0:T(8,128)(2,1)S(1)} %weights.2.refs_0_, bf16[32,1024]{1,0:T(8,128)(2,1)S(1)} %collective-permute-done.16.refs_1_, bf16[32,1024]{1,0:T(8,128)(2,1)S(1)} %collective-permute-done.17.refs_2_, bf16[32,1024]{1,0:T(8,128)(2,1)S(1)} %collective-permute-done.18.refs_3_, ...), custom_call_target="tpu_custom_call" | custom-call | flops 1572864 | bytes 1572864 | tf_op jit(solution)/shard_map/assemble/pallas_call | solution.py:31
  (44 shorter events, 5.8 us)
Async XLA Ops:
  2.9 2.8 %collective-permute-start = (bf16[4,4,32,1024]{3,2,1,0:T(8,128)(2,1)S(1)}, bf16[4,4,32,1024]{3,2,1,0:T(8,128)(2,1)S(1)}, u32[]{:S(2)}, u32[]{:S(2)}) collective-permute-start(bf16[4,4,32,1024]{3,2,1,0:T(8,128)(2,1)S(1)} %load_theirs.2), channel_id=1, source_target_pairs={{0,4},{4,0},{8,12},{12,8},{16,20},{20,16},{24,28},{28,24},{1,5},{5... | collective-permute-start | bytes 3145736 | tf_op jit(solution)/shard_map/ppermute | solution.py:256
  3.6 6.9 %collective-permute-start.8 = (bf16[4,4,32,1024]{3,2,1,0:T(8,128)(2,1)S(1)}, bf16[4,4,32,1024]{3,2,1,0:T(8,128)(2,1)S(1)}, u32[]{:S(2)}, u32[]{:S(2)}) collective-permute-start(bf16[4,4,32,1024]{3,2,1,0:T(8,128)(2,1)S(1)} %load_theirs.3), channel_id=1, source_target_pairs={{0,4},{4,0},{8,12},{12,8},{16,20},{20,16},{24,28},{28,24},{1,5},{5... | collective-permute-start | bytes 3145736 | tf_op jit(solution)/shard_map/ppermute | solution.py:256
  6.0 10.0 %collective-permute-start.1 = (bf16[2,4,16,1024]{3,2,1,0:T(8,128)(2,1)S(1)}, bf16[2,4,16,1024]{3,2,1,0:T(8,128)(2,1)S(1)}, u32[]{:S(2)}, u32[]{:S(2)}) collective-permute-start(bf16[2,4,16,1024]{3,2,1,0:T(8,128)(2,1)S(1)} %get-tuple-element.23), channel_id=1, source_target_pairs={{0,8},{4,12},{8,0},{12,4},{16,24},{20,28},{24,16},{28,20},{1,9},{5... | collective-permute-start | bytes 786440 | tf_op jit(solution)/shard_map/ppermute | solution.py:228
  8.9 9.2 %collective-permute-start.2 = (bf16[2,4,16,1024]{3,2,1,0:T(8,128)(2,1)S(1)}, bf16[2,4,16,1024]{3,2,1,0:T(8,128)(2,1)S(1)}, u32[]{:S(2)}, u32[]{:S(2)}) collective-permute-start(bf16[2,4,16,1024]{3,2,1,0:T(8,128)(2,1)S(1)} %get-tuple-element.24), channel_id=1, source_target_pairs={{0,16},{4,20},{8,24},{12,28},{16,0},{20,4},{24,8},{28,12},{1,17},{... | collective-permute-start | bytes 786440 | tf_op jit(solution)/shard_map/ppermute | solution.py:228
  10.8 10.8 %collective-permute-start.9 = (bf16[2,4,16,1024]{3,2,1,0:T(8,128)(2,1)S(1)}, bf16[2,4,16,1024]{3,2,1,0:T(8,128)(2,1)S(1)}, u32[]{:S(2)}, u32[]{:S(2)}) collective-permute-start(bf16[2,4,16,1024]{3,2,1,0:T(8,128)(2,1)S(1)} %get-tuple-element.31), channel_id=1, source_target_pairs={{0,8},{4,12},{8,0},{12,4},{16,24},{20,28},{24,16},{28,20},{1,9},{5... | collective-permute-start | bytes 786440 | tf_op jit(solution)/shard_map/ppermute | solution.py:228
  11.4 12.3 %collective-permute-start.10 = (bf16[2,4,16,1024]{3,2,1,0:T(8,128)(2,1)S(1)}, bf16[2,4,16,1024]{3,2,1,0:T(8,128)(2,1)S(1)}, u32[]{:S(2)}, u32[]{:S(2)}) collective-permute-start(bf16[2,4,16,1024]{3,2,1,0:T(8,128)(2,1)S(1)} %get-tuple-element.32), channel_id=1, source_target_pairs={{0,16},{4,20},{8,24},{12,28},{16,0},{20,4},{24,8},{28,12},{1,17},{... | collective-permute-start | bytes 786440 | tf_op jit(solution)/shard_map/ppermute | solution.py:228
  18.2 8.1 %collective-permute-start.3 = (bf16[4,16,1024]{2,1,0:T(8,128)(2,1)S(1)}, bf16[4,16,1024]{2,1,0:T(8,128)(2,1)S(1)}, u32[]{:S(2)}, u32[]{:S(2)}) collective-permute-start(bf16[4,16,1024]{2,1,0:T(8,128)(2,1)S(1)} %get-tuple-element.25), channel_id=1, source_target_pairs={{0,16},{4,20},{8,24},{12,28},{16,0},{20,4},{24,8},{28,12},{1,17},{... | collective-permute-start | bytes 393224 | tf_op jit(solution)/shard_map/ppermute | solution.py:228
  19.8 16.6 %copy-start.3 = (f32[64,1024]{1,0:T(8,128)S(1)}, f32[64,1024]{1,0:T(8,128)}, u32[]{:S(2)}) copy-start(f32[64,1024]{1,0:T(8,128)} %refs_5_.3) | copy-start | bytes 786436
  19.8 16.6 %copy-start.4 = (f32[64,1024]{1,0:T(8,128)S(1)}, f32[64,1024]{1,0:T(8,128)}, u32[]{:S(2)}) copy-start(f32[64,1024]{1,0:T(8,128)} %refs_6_.3) | copy-start | bytes 786436
  19.8 6.5 %collective-permute-start.4 = (bf16[4,16,1024]{2,1,0:T(8,128)(2,1)S(1)}, bf16[4,16,1024]{2,1,0:T(8,128)(2,1)S(1)}, u32[]{:S(2)}, u32[]{:S(2)}) collective-permute-start(bf16[4,16,1024]{2,1,0:T(8,128)(2,1)S(1)} %get-tuple-element.26), channel_id=1, source_target_pairs={{0,8},{4,12},{8,0},{12,4},{16,24},{20,28},{24,16},{28,20},{1,9},{5... | collective-permute-start | bytes 393224 | tf_op jit(solution)/shard_map/ppermute | solution.py:228
  23.8 8.2 %collective-permute-start.11 = (bf16[4,16,1024]{2,1,0:T(8,128)(2,1)S(1)}, bf16[4,16,1024]{2,1,0:T(8,128)(2,1)S(1)}, u32[]{:S(2)}, u32[]{:S(2)}) collective-permute-start(bf16[4,16,1024]{2,1,0:T(8,128)(2,1)S(1)} %get-tuple-element.33), channel_id=1, source_target_pairs={{0,16},{4,20},{8,24},{12,28},{16,0},{20,4},{24,8},{28,12},{1,17},{... | collective-permute-start | bytes 393224 | tf_op jit(solution)/shard_map/ppermute | solution.py:228
  25.4 6.6 %collective-permute-start.12 = (bf16[4,16,1024]{2,1,0:T(8,128)(2,1)S(1)}, bf16[4,16,1024]{2,1,0:T(8,128)(2,1)S(1)}, u32[]{:S(2)}, u32[]{:S(2)}) collective-permute-start(bf16[4,16,1024]{2,1,0:T(8,128)(2,1)S(1)} %get-tuple-element.34), channel_id=1, source_target_pairs={{0,8},{4,12},{8,0},{12,4},{16,24},{20,28},{24,16},{28,20},{1,9},{5... | collective-permute-start | bytes 393224 | tf_op jit(solution)/shard_map/ppermute | solution.py:228
  26.5 8.3 %collective-permute-start.5 = (bf16[32,1024]{1,0:T(8,128)(2,1)S(1)}, bf16[32,1024]{1,0:T(8,128)(2,1)S(1)}, u32[]{:S(2)}, u32[]{:S(2)}) collective-permute-start(bf16[32,1024]{1,0:T(8,128)(2,1)S(1)} %get-tuple-element.28), channel_id=1, source_target_pairs={{0,1},{1,2},{2,3},{3,0},{4,5},{5,6},{6,7},{7,4},{8,9},{9,10},{10,1... | collective-permute-start | bytes 196616 | tf_op jit(solution)/shard_map/ppermute | solution.py:232
  28.1 8.0 %collective-permute-start.6 = (bf16[32,1024]{1,0:T(8,128)(2,1)S(1)}, bf16[32,1024]{1,0:T(8,128)(2,1)S(1)}, u32[]{:S(2)}, u32[]{:S(2)}) collective-permute-start(bf16[32,1024]{1,0:T(8,128)(2,1)S(1)} %get-tuple-element.29), channel_id=1, source_target_pairs={{0,2},{1,3},{2,0},{3,1},{4,6},{5,7},{6,4},{7,5},{8,10},{9,11},{10,... | collective-permute-start | bytes 196616 | tf_op jit(solution)/shard_map/ppermute | solution.py:232
  30.7 5.7 %collective-permute-start.7 = (bf16[32,1024]{1,0:T(8,128)(2,1)S(1)}, bf16[32,1024]{1,0:T(8,128)(2,1)S(1)}, u32[]{:S(2)}, u32[]{:S(2)}) collective-permute-start(bf16[32,1024]{1,0:T(8,128)(2,1)S(1)} %get-tuple-element.30), channel_id=1, source_target_pairs={{0,3},{1,0},{2,1},{3,2},{4,7},{5,4},{6,5},{7,6},{8,11},{9,8},{10,9... | collective-permute-start | bytes 196616 | tf_op jit(solution)/shard_map/ppermute | solution.py:232
  32.2 8.4 %collective-permute-start.13 = (bf16[32,1024]{1,0:T(8,128)(2,1)S(1)}, bf16[32,1024]{1,0:T(8,128)(2,1)S(1)}, u32[]{:S(2)}, u32[]{:S(2)}) collective-permute-start(bf16[32,1024]{1,0:T(8,128)(2,1)S(1)} %get-tuple-element.36), channel_id=1, source_target_pairs={{0,1},{1,2},{2,3},{3,0},{4,5},{5,6},{6,7},{7,4},{8,9},{9,10},{10,1... | collective-permute-start | bytes 196616 | tf_op jit(solution)/shard_map/ppermute | solution.py:232
  32.9 8.9 %collective-permute-start.14 = (bf16[32,1024]{1,0:T(8,128)(2,1)S(1)}, bf16[32,1024]{1,0:T(8,128)(2,1)S(1)}, u32[]{:S(2)}, u32[]{:S(2)}) collective-permute-start(bf16[32,1024]{1,0:T(8,128)(2,1)S(1)} %get-tuple-element.37), channel_id=1, source_target_pairs={{0,2},{1,3},{2,0},{3,1},{4,6},{5,7},{6,4},{7,5},{8,10},{9,11},{10,... | collective-permute-start | bytes 196616 | tf_op jit(solution)/shard_map/ppermute | solution.py:232
  34.7 7.0 %collective-permute-start.15 = (bf16[32,1024]{1,0:T(8,128)(2,1)S(1)}, bf16[32,1024]{1,0:T(8,128)(2,1)S(1)}, u32[]{:S(2)}, u32[]{:S(2)}) collective-permute-start(bf16[32,1024]{1,0:T(8,128)(2,1)S(1)} %get-tuple-element.38), channel_id=1, source_target_pairs={{0,3},{1,0},{2,1},{3,2},{4,7},{5,4},{6,5},{7,6},{8,11},{9,8},{10,9... | collective-permute-start | bytes 196616 | tf_op jit(solution)/shard_map/ppermute | solution.py:232
  36.6 10.0 %collective-permute-start.16 = (bf16[32,1024]{1,0:T(8,128)(2,1)S(1)}, bf16[32,1024]{1,0:T(8,128)(2,1)S(1)}, u32[]{:S(2)}, u32[]{:S(2)}) collective-permute-start(bf16[32,1024]{1,0:T(8,128)(2,1)S(1)} %weights.2.refs_0_), channel_id=1, source_target_pairs={{0,1},{1,2},{2,3},{3,0},{4,5},{5,6},{6,7},{7,4},{8,9},{9,10},{10,1... | collective-permute-start | bytes 196616 | tf_op jit(solution)/shard_map/ppermute | solution.py:232
  37.9 12.3 %collective-permute-start.17 = (bf16[32,1024]{1,0:T(8,128)(2,1)S(1)}, bf16[32,1024]{1,0:T(8,128)(2,1)S(1)}, u32[]{:S(2)}, u32[]{:S(2)}) collective-permute-start(bf16[32,1024]{1,0:T(8,128)(2,1)S(1)} %weights.2.refs_0_), channel_id=1, source_target_pairs={{0,2},{1,3},{2,0},{3,1},{4,6},{5,7},{6,4},{7,5},{8,10},{9,11},{10,... | collective-permute-start | bytes 196616 | tf_op jit(solution)/shard_map/ppermute | solution.py:232
  40.6 9.6 %collective-permute-start.18 = (bf16[32,1024]{1,0:T(8,128)(2,1)S(1)}, bf16[32,1024]{1,0:T(8,128)(2,1)S(1)}, u32[]{:S(2)}, u32[]{:S(2)}) collective-permute-start(bf16[32,1024]{1,0:T(8,128)(2,1)S(1)} %weights.2.refs_0_), channel_id=1, source_target_pairs={{0,3},{1,0},{2,1},{3,2},{4,7},{5,4},{6,5},{7,6},{8,11},{9,8},{10,9... | collective-permute-start | bytes 196616 | tf_op jit(solution)/shard_map/ppermute | solution.py:232
  41.9 8.3 %collective-permute-start.19 = (bf16[32,1024]{1,0:T(8,128)(2,1)S(1)}, bf16[32,1024]{1,0:T(8,128)(2,1)S(1)}, u32[]{:S(2)}, u32[]{:S(2)}) collective-permute-start(bf16[32,1024]{1,0:T(8,128)(2,1)S(1)} %weights.3.refs_4_), channel_id=1, source_target_pairs={{0,1},{1,2},{2,3},{3,0},{4,5},{5,6},{6,7},{7,4},{8,9},{9,10},{10,1... | collective-permute-start | bytes 196616 | tf_op jit(solution)/shard_map/ppermute | solution.py:232
  46.6 5.4 %collective-permute-start.20 = (bf16[32,1024]{1,0:T(8,128)(2,1)S(1)}, bf16[32,1024]{1,0:T(8,128)(2,1)S(1)}, u32[]{:S(2)}, u32[]{:S(2)}) collective-permute-start(bf16[32,1024]{1,0:T(8,128)(2,1)S(1)} %weights.3.refs_4_), channel_id=1, source_target_pairs={{0,2},{1,3},{2,0},{3,1},{4,6},{5,7},{6,4},{7,5},{8,10},{9,11},{10,... | collective-permute-start | bytes 196616 | tf_op jit(solution)/shard_map/ppermute | solution.py:232
  46.6 5.4 %collective-permute-start.21 = (bf16[32,1024]{1,0:T(8,128)(2,1)S(1)}, bf16[32,1024]{1,0:T(8,128)(2,1)S(1)}, u32[]{:S(2)}, u32[]{:S(2)}) collective-permute-start(bf16[32,1024]{1,0:T(8,128)(2,1)S(1)} %weights.3.refs_4_), channel_id=1, source_target_pairs={{0,3},{1,0},{2,1},{3,2},{4,7},{5,4},{6,5},{7,6},{8,11},{9,8},{10,9... | collective-permute-start | bytes 196616 | tf_op jit(solution)/shard_map/ppermute | solution.py:232
  (3 other events, 25.6 us)

commit v3 on v0

v3 whole, which is shorter than its diff:
```python
import functools

import jax
import jax.numpy as jnp
from jax import lax
from jax.experimental import pallas as pl
from jax.experimental.pallas import tpu as pltpu
from jax.sharding import PartitionSpec as P

beta_first = 0.9
beta_second = 0.95
learn_rate = 0.05
decay_rate = 0.1
adam_eps = 1e-05
bias_first = 1.0 - 0.9**10
bias_second = 1.0 - 0.95**10

CORES = 2
STEP = 16
LANES = 128
EIGHTHS = ((2, 2), (2, 2))
HALVE = (True, False)
ANY = pl.BlockSpec(memory_space=pl.ANY)
VMEM = pl.BlockSpec(memory_space=pltpu.VMEM)


def local_kernel(kernel, out_shape, operands, name, in_specs=None, out_specs=None, sems=0, after=(), grant=4):
    if in_specs is None:
        in_specs = [VMEM] * len(operands)
    if out_specs is None:
        out_specs = jax.tree.map(lambda _: VMEM, out_shape)
    n = len(operands)

    def ordered(*refs):
        kernel(*refs[:n], *refs[n + len(after) :])

    nbytes = sum(s.size * s.dtype.itemsize for s in jax.tree.leaves(out_shape)) * 3
    return pl.pallas_call(
        ordered,
        out_shape=out_shape,
        in_specs=in_specs + [ANY] * len(after),
        out_specs=out_specs,
        scratch_shapes=[pltpu.SemaphoreType.DMA((sems,))] if sems else [],
        compiler_params=pltpu.CompilerParams(vmem_limit_bytes=grant << 20),
        cost_estimate=pl.CostEstimate(flops=nbytes, bytes_accessed=nbytes, transcendentals=0),
        name=name,
    )(*operands, *after)


def bf16(*shape):
    return jax.ShapeDtypeStruct(shape, jnp.bfloat16)


def f32(*shape):
    return jax.ShapeDtypeStruct(shape, jnp.float32)


def place():
    me = lax.axis_index("inner")
    return me // CORES, lax.rem(me, CORES), lax.axis_index("outer")


def transfer(sources, targets, sems):
    copies = [pltpu.make_async_copy(s, d, sems.at[i]) for i, (s, d) in enumerate(zip(sources, targets))]
    for copy in copies:
        copy.start()
    for copy in copies:
        copy.wait()


def load(grads, span, side, width, chips, name, after=(), grant=4):
    outer, owned, _ = grads.shape
    base, size = span

    def kernel(grad_ref, out, sems):
        core = place()[1]
        sources = []
        for chip in range(chips):
            block = CORES * chip + (1 - core if side else core)
            sources.append(grad_ref.at[:, :, pl.ds(pl.multiple_of(block * width + base, LANES), size)])
        transfer(sources, [out.at[chip] for chip in range(chips)], sems)

    shape = bf16(chips, outer, owned, size)
    return local_kernel(kernel, shape, [grads], name, in_specs=[ANY], sems=chips, after=after, grant=grant)


def rows_at(start):
    return pl.ds(pl.multiple_of(start, STEP), STEP)


def each_step(depth, do):
    lax.fori_loop(0, depth // STEP, lambda i, carry: (do(rows_at(i * STEP)), carry)[1], 0, unroll=True)


def sum_of(terms, rows):
    value = None
    for ref, index in terms:
        term = ref[(*index, rows)].astype(jnp.float32)
        value = term if value is None else value + term
    return value


def sums(operands, shapes, plan, name, after=()):
    def kernel(*refs):
        outs = refs[len(operands) :]
        for out, pieces in zip(outs, plan(refs[: len(operands)], *place())):
            for index, columns, terms in pieces:

                def do(rows, out=out, index=index, columns=columns, terms=terms):
                    out[(*index, rows, columns)] = sum_of(terms, rows).astype(out.dtype)

                each_step(out.shape[-2], do)

    return local_kernel(kernel, shapes, operands, name, after=after)


def adam(total, master, first, second):
    new_first = beta_first * first + (1.0 - beta_first) * total
    new_second = beta_second * second + (1.0 - beta_second) * total * total
    update = new_first / bias_first / (jnp.sqrt(new_second / bias_second) + adam_eps) + decay_rate * master
    return master - learn_rate * update, new_first, new_second


def weights(total, span, state, name, after=()):
    arrays, indices = zip(*total)
    shape = arrays[0].shape[-2:]
    columns = pl.ds(*span)

    def kernel(*refs):
        *terms, master_ref, first_ref, second_ref, out = refs

        def do(rows):
            value = sum_of(list(zip(terms, indices)), rows)
            value, _, _ = adam(value, master_ref[rows, columns], first_ref[rows, columns], second_ref[rows, columns])
            out[rows] = value.astype(out.dtype)

        each_step(shape[0], do)

    return local_kernel(kernel, bf16(*shape), [*arrays, *state], name, after=after)


def finish(totals, spans, state):
    arrays = [array for total in totals for array, _ in total]
    n = len(arrays)

    def kernel(*refs):
        state_refs, outs = refs[n : n + 3], refs[n + 3 :]
        at = 0
        for span, total in zip(spans, totals):
            columns = pl.ds(*span)
            terms = [(ref, index) for ref, (_, index) in zip(refs[at : at + len(total)], total)]
            at += len(total)

            def do(rows, terms=terms, columns=columns):
                values = adam(sum_of(terms, rows), *[ref[rows, columns] for ref in state_refs])
                for out, value in zip(outs, values):
                    out[rows, columns] = value

            each_step(state[0].shape[0], do)

    return local_kernel(kernel, [f32(*state[0].shape)] * 3, arrays + list(state), "finish")


def assemble(groups, sources, spans, outer, width):
    def kernel(*refs):
        *pieces, out, sems = refs
        here = lax.axis_index("outer")
        targets = [out.at[source(here), :, pl.ds(*span)] for span in spans for source in sources]
        transfer(pieces, targets, sems)

    operands = [piece for group in groups for piece in group]
    shape = bf16(outer, operands[0].shape[0], width)
    return local_kernel(kernel, shape, operands, "assemble", out_specs=ANY, sems=len(operands))


def to_core(x, inner):
    return lax.ppermute(x, "inner", [(i, i ^ 1) for i in range(inner)])


def to_chip(x, target, chips):
    pairs = [(CORES * c + k, CORES * target(c, k) + k) for c in range(chips) for k in range(CORES)]
    return lax.ppermute(x, "inner", pairs)


def to_group(x, target, inner, outer):
    pairs = [(i * outer + z, i * outer + target(z, i % CORES)) for i in range(inner) for z in range(outer)]
    return lax.ppermute(x, ("inner", "outer"), pairs)


def local(mine, core_in, chip, block):
    return [(mine, (chip, block)), (core_in, (chip, block))]


EVERY = slice(None)


def plain_total(mine, core_in, inner, outer):
    chips, _, depth, width = mine.shape
    moves = [lambda chip, core, m=m: (chip + m) % chips for m in range(1, chips)]
    steps = [lambda z, core, s=s: (z + s) % outer for s in range(1, outer)]

    def first(refs, chip, core, here):
        return [[((z,), EVERY, local(*refs, move(chip, core), z)) for z in range(outer)] for move in moves]

    made = sums([mine, core_in], [bf16(outer, depth, width)] * len(moves), first, "first_sum")
    got = [to_chip(x, move, chips) for x, move in zip(made, moves)]

    def group(refs, chip, core, here):
        blocks = [here] + [step(here, core) for step in steps]
        return [[((), EVERY, local(*refs[:2], chip, z) + [(ref, (z,)) for ref in refs[2:]])] for z in blocks]

    shapes = [f32(depth, width)] + [bf16(depth, width)] * len(steps)
    kept, *sends = sums([mine, core_in, *got], shapes, group, "group_sum")
    return [(kept, ())] + [(to_group(x, step, inner, outer), ()) for x, step in zip(sends, steps)]


CHIP_STEPS = [lambda chip, core: chip ^ (1 + core), lambda chip, core: chip ^ (2 - core)]
OUTER_STEPS = [lambda z, core: z ^ 1, lambda z, core: z ^ 3]


def over_group(mine, core_in, chips):
    _, outer, depth, width = mine.shape

    def first(refs, chip, core, here):
        targets = [CHIP_STEPS[0](chip, core), chip ^ 3]
        return [[((i, z), EVERY, local(*refs, to, z)) for i, to in enumerate(targets) for z in range(outer)]]

    [made] = sums([mine, core_in], [bf16(2, outer, depth, width)], first, "first_sum")
    got = to_chip(made, CHIP_STEPS[0], chips)

    def second(refs, chip, core, here):
        to = CHIP_STEPS[1](chip, core)
        return [[((z,), EVERY, local(*refs[:2], to, z) + [(refs[2], (1, z))]) for z in range(outer)]]

    after = yield
    [made] = sums([mine, core_in, got], [bf16(outer, depth, width)], second, "second_sum", after)
    yield mine, core_in, got, to_chip(made, CHIP_STEPS[1], chips)


def group_pieces(pieces, refs, chip, z, index, more=()):
    out, at = [], 0
    for k in range(len(pieces)):
        mine, core_in, got, last = refs[4 * k : 4 * k + 4]
        columns = pl.ds(at, mine.shape[-1])
        at += mine.shape[-1]
        terms = local(mine, core_in, chip, z) + [(got, (0, z)), (last, (z,))]
        out.append((index, columns, terms + [(ref.at[..., columns], lead) for ref, lead in more]))
    return out


def halve_groups(pieces, inner, outer):
    depth, width = pieces[0][0].shape[2], sum(piece[0].shape[3] for piece in pieces)
    arrays = [array for piece in pieces for array in piece]

    def first(refs, chip, core, here):
        targets = [OUTER_STEPS[0](here, core), here ^ 2]
        return [[p for i, to in enumerate(targets) for p in group_pieces(pieces, refs, chip, to, (i,))]]

    [begun] = sums(arrays, [bf16(2, depth, width)], first, "halve")
    got = to_group(begun, OUTER_STEPS[0], inner, outer)

    def second(refs, chip, core, here):
        to = OUTER_STEPS[1](here, core)
        return [
            group_pieces(pieces, refs, chip, here, (), [(refs[-1], (0,))]),
            group_pieces(pieces, refs, chip, to, (), [(refs[-1], (1,))]),
        ]

    kept, made = sums([*arrays, got], [f32(depth, width), bf16(depth, width)], second, "halve_again")
    return [(kept, ()), (to_group(made, OUTER_STEPS[1], inner, outer), ())], begun


def direct_groups(pieces, inner, outer):
    depth, width = pieces[0][0].shape[2], sum(piece[0].shape[3] for piece in pieces)
    arrays = [array for piece in pieces for array in piece]
    masks = [2, 3, 1]

    def group(refs, chip, core, here):
        return [group_pieces(pieces, refs, chip, here ^ m, ()) for m in [0] + masks]

    shapes = [f32(depth, width)] + [bf16(depth, width)] * len(masks)
    kept, *sends = sums(arrays, shapes, group, "group_sum")
    return [(kept, ())] + [(to_group(x, lambda z, _, m=m: z ^ m, inner, outer), ()) for x, m in zip(sends, masks)], kept


def gather(own, inner, outer):
    if outer == 4:
        far, diag, near = [to_group(own, lambda z, _, m=m: z ^ m, inner, outer) for m in (2, 3, 1)]
        return own, near, far, diag
    return own, *[to_group(own, lambda z, _, s=s: (z + s) % outer, inner, outer) for s in range(1, outer)]


def body(gradients, master, first, second, *, inner, outer):
    depth, columns = gradients.shape[2:]
    chips, owned, width = inner // CORES, depth // outer, columns // inner
    grads = gradients.reshape(outer, owned, columns)
    state = (master, first, second)

    if chips == 4 and outer == 4 and width % (8 * LANES) == 0:
        sizes = [n * width // 8 for span in EIGHTHS for n in span]
        parts = [(sum(sizes[:k]), size) for k, size in enumerate(sizes)]
        theirs = [load(grads, part, 1, width, chips, "load_theirs", grant=4 if k else 52) for k, part in enumerate(parts)]
        core_in = [to_core(x, inner) for x in theirs]
        mine = [load(grads, part, 0, width, chips, "load_mine") for part in parts]
        ways = [over_group(m, c, chips) for m, c in zip(mine, core_in)]
        for way in ways:
            next(way)
        sources = [lambda z, m=m: z ^ m for m in range(4)]
        spans, totals, at, begun = [], [], 0, []
        for k, span in enumerate(EIGHTHS):
            after = [[]] * (len(span) - 1) + [begun]
            some = [way.send(after[n]) for n, way in enumerate(ways[at : at + len(span)])]
            spans.append((parts[at][0], sum(sizes[at : at + len(span)])))
            at += len(span)
            total, first_made = (halve_groups if HALVE[k] else direct_groups)(some, inner, outer)
            totals.append(total)
            begun = [first_made]
    else:
        spans = [(0, width)]
        sources = [lambda z, s=s: (z + outer - s) % outer for s in range(outer)]
        theirs, mine = [load(grads, spans[0], side, width, chips, "load") for side in (1, 0)]
        totals = [plain_total(mine, to_core(theirs, inner), inner, outer)]

    made = [weights(total, span, state, "weights") for total, span in zip(totals, spans)]
    copy = assemble([gather(new, inner, outer) for new in made], sources, spans, outer, width)
    return (*finish(totals, spans, state), copy.reshape(depth, width))


def solution(mesh):
    return jax.shard_map(
        functools.partial(body, inner=mesh.shape["inner"], outer=mesh.shape["outer"]),
        mesh=mesh,
        in_specs=(
            P("inner", "outer", None, None),
            P("outer", "inner"),
            P("outer", "inner"),
            P("outer", "inner"),
        ),
        out_specs=(P("outer", "inner"), P("outer", "inner"), P("outer", "inner"), P(None, "inner")),
        check_vma=False,
    )
```

time: 186 us -> 50.4 us (0.27)
  blocking collectives: 89.3 us -> 0 us
  other arithmetic: 51.4 us -> 0 us
  local copies, waits for them, and re-layouts: 43.1 us -> 0.63 us
  starting transfers between devices: 0 us -> 34.5 us
  waiting for transfers between devices: 0 us -> 9.15 us
  Pallas kernels: 0 us -> 5.1 us
    all_to_all x2 -> x0, blocking collectives: 73.5 us -> none  [the longest x1 54.3 us: body(): lax.all_to_all(local, 'inner', split_axis=2, concat_axis=0, tiled=True)]
    unnamed x2 -> x0, other arithmetic: 47.3 us -> none
    ppermute x0 -> x23, starting transfers between devices: none -> 34.5 us  [the longest x11 20.8 us: to_group(): return lax.ppermute(x, ('inner', 'outer'), pairs)]
    unnamed x14 -> x8, local copies, waits for them, and re-layouts: 24.3 us -> 0.63 us
    reshape x1 -> x0, local copies, waits for them, and re-layouts: 17.9 us -> none  [body(): local = gradients.reshape(1, gradients.shape[2], gradients.shape[3])]
    all_gather x1 -> x0, blocking collectives: 15.8 us -> none  [body(): lax.all_gather(new_master.astype(jnp.bfloat16), 'outer', axis=0, tiled=True)]
    ppermute x0 -> x23, waiting for transfers between devices: none -> 9.15 us  [the longest x8 6.23 us: to_chip(): return lax.ppermute(x, 'inner', pairs)]
    pallas_call x0 -> x23, Pallas kernels: none -> 5.1 us  [local_kernel(): pl.pallas_call(ordered, out_shape=out_shape, in_specs=in_specs + [ANY] *...]
  transfers between devices with their start and end apart: 0 -> 23, of which waited for: 0 -> 6; matrix products, arithmetic and copies ran while one was open for 0% -> 0% of each run, Pallas kernels for 0% -> 6%
where the time goes in v3:
time: 50.4 us; the launch traced here: 50.2 us
  starting transfers between devices  34.5 us (68%)
  waiting for transfers between devices  9.15 us (18%)
  Pallas kernels  5.1 us (10%)
  between operations  0.84 us (2%)
  local copies, waits for them, and re-layouts  0.63 us (1%)
    ppermute x11, starting transfers between devices, to_group(): return lax.ppermute(x, ('inner', 'outer'), pairs)  20.8 us
    ppermute x8, starting transfers between devices, to_chip(): return lax.ppermute(x, 'inner', pairs)  12 us
    ppermute x8, waiting for transfers between devices, to_chip(): return lax.ppermute(x, 'inner', pairs)  6.23 us
    pallas_call x23, Pallas kernels, local_kernel(): pl.pallas_call(ordered, out_shape=out_shape, in_specs=in_specs + [ANY] *...  5.1 us
    ppermute x11, waiting for transfers between devices, to_group(): return lax.ppermute(x, ('inner', 'outer'), pairs)  2.91 us
    ppermute x4, starting transfers between devices, to_core(): return lax.ppermute(x, 'inner', [(i, i ^ 1) for i in range(inner)])  1.67 us
  transfers between devices with their start and end apart: 23, of which 6 were waited for; matrix products, arithmetic and copies ran while one was open for 0% of the time, Pallas kernels for 6%

profile of v3, /device:TPU:0, one launch (start us, length us, event | category | flops | bytes accessed | tf_op | source)
XLA Modules:
  0.0 50.2 jit_solution(15191976944023111798)
XLA Ops:
  0.6 1.3 %load_theirs.4 = bf16[4,4,64,256]{3,2,1,0:T(8,128)(2,1)S(1)} custom-call(bf16[4,64,8192]{2,1,0:T(8,128)(2,1)} %bitcast.2), custom_call_target="tpu_custom_call" | custom-call | flops 1572864 | bytes 1572864 | tf_op jit(solution)/shard_map/load_theirs/pallas_call | solution.py:38
  2.5 0.6 %copy-done = bf16[1,1,256,8192]{3,2,1,0:T(8,128)(2,1)S(1)} copy-done((bf16[1,1,256,8192]{3,2,1,0:T(8,128)(2,1)S(1)}, bf16[1,1,256,8192]{3,2,1,0:T(8,128)(2,1)}, u32[]{:S(2)}) %copy-start) | copy-done | bytes 4194328
  5.0 2.6 %collective-permute-start.1 = (bf16[2,4,64,256]{3,2,1,0:T(8,128)(2,1)S(1)}, bf16[2,4,64,256]{3,2,1,0:T(8,128)(2,1)S(1)}, u32[]{:S(2)}, u32[]{:S(2)}) collective-permute-start(bf16[2,4,64,256]{3,2,1,0:T(8,128)(2,1)S(1)} %first_sum.4), channel_id=1, source_target_pairs={{0,8},{4,20},{8,0},{12,28},{16,24},{20,4},{24,16},{28,12},{1,9},{5... | collective-permute-start | bytes 786440 | tf_op jit(solution)/shard_map/ppermute | solution.py:182
  8.6 1.5 %collective-permute-start.9 = (bf16[2,4,64,256]{3,2,1,0:T(8,128)(2,1)S(1)}, bf16[2,4,64,256]{3,2,1,0:T(8,128)(2,1)S(1)}, u32[]{:S(2)}, u32[]{:S(2)}) collective-permute-start(bf16[2,4,64,256]{3,2,1,0:T(8,128)(2,1)S(1)} %first_sum.6), channel_id=1, source_target_pairs={{0,8},{4,20},{8,0},{12,28},{16,24},{20,4},{24,16},{28,12},{1,9},{5... | collective-permute-start | bytes 786440 | tf_op jit(solution)/shard_map/ppermute | solution.py:182
  10.8 1.1 %collective-permute-done.1.refs_2_ = bf16[2,4,64,256]{3,2,1,0:T(8,128)(2,1)S(1)} collective-permute-done((bf16[2,4,64,256]{3,2,1,0:T(8,128)(2,1)S(1)}, bf16[2,4,64,256]{3,2,1,0:T(8,128)(2,1)S(1)}, u32[]{:S(2)}, u32[]{:S(2)}) %collective-permute-start.1) | collective-permute-done | bytes 262176 | tf_op jit(solution)/shard_map/ppermute | solution.py:182
  12.0 2.1 %collective-permute-start.2 = (bf16[4,64,256]{2,1,0:T(8,128)(2,1)S(1)}, bf16[4,64,256]{2,1,0:T(8,128)(2,1)S(1)}, u32[]{:S(2)}, u32[]{:S(2)}) collective-permute-start(bf16[4,64,256]{2,1,0:T(8,128)(2,1)S(1)} %second_sum.4), channel_id=1, source_target_pairs={{0,16},{4,12},{8,24},{12,4},{16,0},{20,28},{24,8},{28,20},{1,17},{... | collective-permute-start | bytes 393224 | tf_op jit(solution)/shard_map/ppermute | solution.py:182
  14.1 0.7 %collective-permute-done.4.refs_2_.refs_6_ = bf16[2,4,64,256]{3,2,1,0:T(8,128)(2,1)S(1)} collective-permute-done((bf16[2,4,64,256]{3,2,1,0:T(8,128)(2,1)S(1)}, bf16[2,4,64,256]{3,2,1,0:T(8,128)(2,1)S(1)}, u32[]{:S(2)}, u32[]{:S(2)}) %collective-permute-start.4) | collective-permute-done | bytes 262176 | tf_op jit(solution)/shard_map/ppermute | solution.py:182
  14.9 2.4 %collective-permute-start.5 = (bf16[4,64,256]{2,1,0:T(8,128)(2,1)S(1)}, bf16[4,64,256]{2,1,0:T(8,128)(2,1)S(1)}, u32[]{:S(2)}, u32[]{:S(2)}) collective-permute-start(bf16[4,64,256]{2,1,0:T(8,128)(2,1)S(1)} %second_sum.5), channel_id=1, source_target_pairs={{0,16},{4,12},{8,24},{12,4},{16,0},{20,28},{24,8},{28,20},{1,17},{... | collective-permute-start | bytes 393224 | tf_op jit(solution)/shard_map/ppermute | solution.py:182
  17.3 1.2 %collective-permute-done.2.refs_3_ = bf16[4,64,256]{2,1,0:T(8,128)(2,1)S(1)} collective-permute-done((bf16[4,64,256]{2,1,0:T(8,128)(2,1)S(1)}, bf16[4,64,256]{2,1,0:T(8,128)(2,1)S(1)}, u32[]{:S(2)}, u32[]{:S(2)}) %collective-permute-start.2) | collective-permute-done | bytes 131104 | tf_op jit(solution)/shard_map/ppermute | solution.py:182
  18.5 3.2 %collective-permute-done.5.refs_7_ = bf16[4,64,256]{2,1,0:T(8,128)(2,1)S(1)} collective-permute-done((bf16[4,64,256]{2,1,0:T(8,128)(2,1)S(1)}, bf16[4,64,256]{2,1,0:T(8,128)(2,1)S(1)}, u32[]{:S(2)}, u32[]{:S(2)}) %collective-permute-start.5) | collective-permute-done | bytes 131104 | tf_op jit(solution)/shard_map/ppermute | solution.py:182
  21.8 2.1 %collective-permute-start.6 = (bf16[2,64,512]{2,1,0:T(8,128)(2,1)S(1)}, bf16[2,64,512]{2,1,0:T(8,128)(2,1)S(1)}, u32[]{:S(2)}, u32[]{:S(2)}) collective-permute-start(bf16[2,64,512]{2,1,0:T(8,128)(2,1)S(1)} %halve.1.refs_3_), channel_id=1, source_target_pairs={{0,1},{1,0},{2,3},{3,2},{4,5},{5,4},{6,7},{7,6},{8,9},{9,8},{10,11... | collective-permute-start | bytes 393224 | tf_op jit(solution)/shard_map/ppermute | solution.py:187
  24.1 1.6 %collective-permute-start.10 = (bf16[4,64,256]{2,1,0:T(8,128)(2,1)S(1)}, bf16[4,64,256]{2,1,0:T(8,128)(2,1)S(1)}, u32[]{:S(2)}, u32[]{:S(2)}) collective-permute-start(bf16[4,64,256]{2,1,0:T(8,128)(2,1)S(1)} %second_sum.6), channel_id=1, source_target_pairs={{0,16},{4,12},{8,24},{12,4},{16,0},{20,28},{24,8},{28,20},{1,17},{... | collective-permute-start | bytes 393224 | tf_op jit(solution)/shard_map/ppermute | solution.py:182
  26.3 0.6 %collective-permute-done.6.refs_8_ = bf16[2,64,512]{2,1,0:T(8,128)(2,1)S(1)} collective-permute-done((bf16[2,64,512]{2,1,0:T(8,128)(2,1)S(1)}, bf16[2,64,512]{2,1,0:T(8,128)(2,1)S(1)}, u32[]{:S(2)}, u32[]{:S(2)}) %collective-permute-start.6) | collective-permute-done | bytes 131104 | tf_op jit(solution)/shard_map/ppermute | solution.py:187
  27.0 4.1 %collective-permute-start.7 = (bf16[64,512]{1,0:T(8,128)(2,1)S(1)}, bf16[64,512]{1,0:T(8,128)(2,1)S(1)}, u32[]{:S(2)}, u32[]{:S(2)}) collective-permute-start(bf16[64,512]{1,0:T(8,128)(2,1)S(1)} %get-tuple-element.14), channel_id=1, source_target_pairs={{0,3},{1,2},{2,1},{3,0},{4,7},{5,6},{6,5},{7,4},{8,11},{9,10},{10,... | collective-permute-start | bytes 196616 | tf_op jit(solution)/shard_map/ppermute | solution.py:187
  31.3 2.2 %collective-permute-start.14 = (bf16[64,512]{1,0:T(8,128)(2,1)S(1)}, bf16[64,512]{1,0:T(8,128)(2,1)S(1)}, u32[]{:S(2)}, u32[]{:S(2)}) collective-permute-start(bf16[64,512]{1,0:T(8,128)(2,1)S(1)} %get-tuple-element.16), channel_id=1, source_target_pairs={{0,2},{1,3},{2,0},{3,1},{4,6},{5,7},{6,4},{7,5},{8,10},{9,11},{10,... | collective-permute-start | bytes 196616 | tf_op jit(solution)/shard_map/ppermute | solution.py:187
  33.8 1.1 %collective-permute-start.16 = (bf16[64,512]{1,0:T(8,128)(2,1)S(1)}, bf16[64,512]{1,0:T(8,128)(2,1)S(1)}, u32[]{:S(2)}, u32[]{:S(2)}) collective-permute-start(bf16[64,512]{1,0:T(8,128)(2,1)S(1)} %get-tuple-element.18), channel_id=1, source_target_pairs={{0,1},{1,0},{2,3},{3,2},{4,5},{5,4},{6,7},{7,6},{8,9},{9,8},{10,11... | collective-permute-start | bytes 196616 | tf_op jit(solution)/shard_map/ppermute | solution.py:187
  35.0 1.7 %collective-permute-start.17 = (bf16[64,512]{1,0:T(8,128)(2,1)S(1)}, bf16[64,512]{1,0:T(8,128)(2,1)S(1)}, u32[]{:S(2)}, u32[]{:S(2)}) collective-permute-start(bf16[64,512]{1,0:T(8,128)(2,1)S(1)} %weights.2.refs_0_), channel_id=1, source_target_pairs={{0,1},{1,0},{2,3},{3,2},{4,5},{5,4},{6,7},{7,6},{8,9},{9,8},{10,11... | collective-permute-start | bytes 196616 | tf_op jit(solution)/shard_map/ppermute | solution.py:187
  36.7 1.9 %collective-permute-start.18 = (bf16[64,512]{1,0:T(8,128)(2,1)S(1)}, bf16[64,512]{1,0:T(8,128)(2,1)S(1)}, u32[]{:S(2)}, u32[]{:S(2)}) collective-permute-start(bf16[64,512]{1,0:T(8,128)(2,1)S(1)} %weights.2.refs_0_), channel_id=1, source_target_pairs={{0,2},{1,3},{2,0},{3,1},{4,6},{5,7},{6,4},{7,5},{8,10},{9,11},{10,... | collective-permute-start | bytes 196616 | tf_op jit(solution)/shard_map/ppermute | solution.py:187
  38.6 2.9 %collective-permute-start.19 = (bf16[64,512]{1,0:T(8,128)(2,1)S(1)}, bf16[64,512]{1,0:T(8,128)(2,1)S(1)}, u32[]{:S(2)}, u32[]{:S(2)}) collective-permute-start(bf16[64,512]{1,0:T(8,128)(2,1)S(1)} %weights.2.refs_0_), channel_id=1, source_target_pairs={{0,3},{1,2},{2,1},{3,0},{4,7},{5,6},{6,5},{7,4},{8,11},{9,10},{10,... | collective-permute-start | bytes 196616 | tf_op jit(solution)/shard_map/ppermute | solution.py:187
  42.0 1.2 %collective-permute-start.21 = (bf16[64,512]{1,0:T(8,128)(2,1)S(1)}, bf16[64,512]{1,0:T(8,128)(2,1)S(1)}, u32[]{:S(2)}, u32[]{:S(2)}) collective-permute-start(bf16[64,512]{1,0:T(8,128)(2,1)S(1)} %weights.3.refs_4_), channel_id=1, source_target_pairs={{0,2},{1,3},{2,0},{3,1},{4,6},{5,7},{6,4},{7,5},{8,10},{9,11},{10,... | collective-permute-start | bytes 196616 | tf_op jit(solution)/shard_map/ppermute | solution.py:187
  43.2 2.9 %collective-permute-start.22 = (bf16[64,512]{1,0:T(8,128)(2,1)S(1)}, bf16[64,512]{1,0:T(8,128)(2,1)S(1)}, u32[]{:S(2)}, u32[]{:S(2)}) collective-permute-start(bf16[64,512]{1,0:T(8,128)(2,1)S(1)} %weights.3.refs_4_), channel_id=1, source_target_pairs={{0,3},{1,2},{2,1},{3,0},{4,7},{5,6},{6,5},{7,4},{8,11},{9,10},{10,... | collective-permute-start | bytes 196616 | tf_op jit(solution)/shard_map/ppermute | solution.py:187
  46.2 1.0 %finish.1 = (f32[64,1024]{1,0:T(8,128)}, f32[64,1024]{1,0:T(8,128)}, f32[64,1024]{1,0:T(8,128)}) custom-call(f32[64,512]{1,0:T(8,128)S(1)} %get-tuple-element.13.refs_0_, bf16[64,512]{1,0:T(8,128)(2,1)S(1)} %collective-permute-done.7.refs_1_, f32[64,512]{1,0:T(8,128)S(1)} %get-tuple-element.15.refs_2_.refs_0_, ...), custom_call_target="tpu_custom_call" | custom-call | flops 2359296 | bytes 2359296 | tf_op jit(solution)/shard_map/finish/pallas_call | solution.py:38
  47.2 2.2 %collective-permute-done.21.refs_6_ = bf16[64,512]{1,0:T(8,128)(2,1)S(1)} collective-permute-done((bf16[64,512]{1,0:T(8,128)(2,1)S(1)}, bf16[64,512]{1,0:T(8,128)(2,1)S(1)}, u32[]{:S(2)}, u32[]{:S(2)}) %collective-permute-start.21) | collective-permute-done | bytes 65568 | tf_op jit(solution)/shard_map/ppermute | solution.py:187
  49.4 0.8 %assemble.1 = bf16[4,64,1024]{2,1,0:T(8,128)(2,1)} custom-call(bf16[64,512]{1,0:T(8,128)(2,1)S(1)} %weights.2.refs_0_, bf16[64,512]{1,0:T(8,128)(2,1)S(1)} %collective-permute-done.17.refs_1_, bf16[64,512]{1,0:T(8,128)(2,1)S(1)} %collective-permute-done.18.refs_2_, bf16[64,512]{1,0:T(8,128)(2,1)S(1)} %collective-permute-done.19.refs_3_, ...), custom_call_target="tpu_custom_call" | custom-call | flops 1572864 | bytes 1572864 | tf_op jit(solution)/shard_map/assemble/pallas_call | solution.py:38
  (53 shorter events, 6.0 us)
Async XLA Ops:
  1.9 2.9 %collective-permute-start = (bf16[4,4,64,256]{3,2,1,0:T(8,128)(2,1)S(1)}, bf16[4,4,64,256]{3,2,1,0:T(8,128)(2,1)S(1)}, u32[]{:S(2)}, u32[]{:S(2)}) collective-permute-start(bf16[4,4,64,256]{3,2,1,0:T(8,128)(2,1)S(1)} %load_theirs.4), channel_id=1, source_target_pairs={{0,4},{4,0},{8,12},{12,8},{16,20},{20,16},{24,28},{28,24},{1,5},{5... | collective-permute-start | bytes 1572872 | tf_op jit(solution)/shard_map/ppermute | solution.py:177
  3.2 4.4 %collective-permute-start.3 = (bf16[4,4,64,256]{3,2,1,0:T(8,128)(2,1)S(1)}, bf16[4,4,64,256]{3,2,1,0:T(8,128)(2,1)S(1)}, u32[]{:S(2)}, u32[]{:S(2)}) collective-permute-start(bf16[4,4,64,256]{3,2,1,0:T(8,128)(2,1)S(1)} %load_theirs.5), channel_id=1, source_target_pairs={{0,4},{4,0},{8,12},{12,8},{16,20},{20,16},{24,28},{28,24},{1,5},{5... | collective-permute-start | bytes 1572872 | tf_op jit(solution)/shard_map/ppermute | solution.py:177
  3.8 4.7 %collective-permute-start.8 = (bf16[4,4,64,256]{3,2,1,0:T(8,128)(2,1)S(1)}, bf16[4,4,64,256]{3,2,1,0:T(8,128)(2,1)S(1)}, u32[]{:S(2)}, u32[]{:S(2)}) collective-permute-start(bf16[4,4,64,256]{3,2,1,0:T(8,128)(2,1)S(1)} %load_theirs.6), channel_id=1, source_target_pairs={{0,4},{4,0},{8,12},{12,8},{16,20},{20,16},{24,28},{28,24},{1,5},{5... | collective-permute-start | bytes 1572872 | tf_op jit(solution)/shard_map/ppermute | solution.py:177
  4.1 6.1 %collective-permute-start.11 = (bf16[4,4,64,256]{3,2,1,0:T(8,128)(2,1)S(1)}, bf16[4,4,64,256]{3,2,1,0:T(8,128)(2,1)S(1)}, u32[]{:S(2)}, u32[]{:S(2)}) collective-permute-start(bf16[4,4,64,256]{3,2,1,0:T(8,128)(2,1)S(1)} %load_theirs.7), channel_id=1, source_target_pairs={{0,4},{4,0},{8,12},{12,8},{16,20},{20,16},{24,28},{28,24},{1,5},{5... | collective-permute-start | bytes 1572872 | tf_op jit(solution)/shard_map/ppermute | solution.py:177
  5.0 6.9 %collective-permute-start.1 = (bf16[2,4,64,256]{3,2,1,0:T(8,128)(2,1)S(1)}, bf16[2,4,64,256]{3,2,1,0:T(8,128)(2,1)S(1)}, u32[]{:S(2)}, u32[]{:S(2)}) collective-permute-start(bf16[2,4,64,256]{3,2,1,0:T(8,128)(2,1)S(1)} %first_sum.4), channel_id=1, source_target_pairs={{0,8},{4,20},{8,0},{12,28},{16,24},{20,4},{24,16},{28,12},{1,9},{5... | collective-permute-start | bytes 786440 | tf_op jit(solution)/shard_map/ppermute | solution.py:182
  7.6 7.2 %collective-permute-start.4 = (bf16[2,4,64,256]{3,2,1,0:T(8,128)(2,1)S(1)}, bf16[2,4,64,256]{3,2,1,0:T(8,128)(2,1)S(1)}, u32[]{:S(2)}, u32[]{:S(2)}) collective-permute-start(bf16[2,4,64,256]{3,2,1,0:T(8,128)(2,1)S(1)} %first_sum.5), channel_id=1, source_target_pairs={{0,8},{4,20},{8,0},{12,28},{16,24},{20,4},{24,16},{28,12},{1,9},{5... | collective-permute-start | bytes 786440 | tf_op jit(solution)/shard_map/ppermute | solution.py:182
  8.6 15.4 %collective-permute-start.9 = (bf16[2,4,64,256]{3,2,1,0:T(8,128)(2,1)S(1)}, bf16[2,4,64,256]{3,2,1,0:T(8,128)(2,1)S(1)}, u32[]{:S(2)}, u32[]{:S(2)}) collective-permute-start(bf16[2,4,64,256]{3,2,1,0:T(8,128)(2,1)S(1)} %first_sum.6), channel_id=1, source_target_pairs={{0,8},{4,20},{8,0},{12,28},{16,24},{20,4},{24,16},{28,12},{1,9},{5... | collective-permute-start | bytes 786440 | tf_op jit(solution)/shard_map/ppermute | solution.py:182
  10.2 15.4 %collective-permute-start.12 = (bf16[2,4,64,256]{3,2,1,0:T(8,128)(2,1)S(1)}, bf16[2,4,64,256]{3,2,1,0:T(8,128)(2,1)S(1)}, u32[]{:S(2)}, u32[]{:S(2)}) collective-permute-start(bf16[2,4,64,256]{3,2,1,0:T(8,128)(2,1)S(1)} %first_sum.7), channel_id=1, source_target_pairs={{0,8},{4,20},{8,0},{12,28},{16,24},{20,4},{24,16},{28,12},{1,9},{5... | collective-permute-start | bytes 786440 | tf_op jit(solution)/shard_map/ppermute | solution.py:182
  12.0 6.5 %collective-permute-start.2 = (bf16[4,64,256]{2,1,0:T(8,128)(2,1)S(1)}, bf16[4,64,256]{2,1,0:T(8,128)(2,1)S(1)}, u32[]{:S(2)}, u32[]{:S(2)}) collective-permute-start(bf16[4,64,256]{2,1,0:T(8,128)(2,1)S(1)} %second_sum.4), channel_id=1, source_target_pairs={{0,16},{4,12},{8,24},{12,4},{16,0},{20,28},{24,8},{28,20},{1,17},{... | collective-permute-start | bytes 393224 | tf_op jit(solution)/shard_map/ppermute | solution.py:182
  14.9 6.8 %collective-permute-start.5 = (bf16[4,64,256]{2,1,0:T(8,128)(2,1)S(1)}, bf16[4,64,256]{2,1,0:T(8,128)(2,1)S(1)}, u32[]{:S(2)}, u32[]{:S(2)}) collective-permute-start(bf16[4,64,256]{2,1,0:T(8,128)(2,1)S(1)} %second_sum.5), channel_id=1, source_target_pairs={{0,16},{4,12},{8,24},{12,4},{16,0},{20,28},{24,8},{28,20},{1,17},{... | collective-permute-start | bytes 393224 | tf_op jit(solution)/shard_map/ppermute | solution.py:182
  21.8 13.0 %copy-start.1 = (f32[64,1024]{1,0:T(8,128)S(1)}, f32[64,1024]{1,0:T(8,128)}, u32[]{:S(2)}) copy-start(f32[64,1024]{1,0:T(8,128)} %refs_4_.3) | copy-start | bytes 786436
  21.8 5.1 %collective-permute-start.6 = (bf16[2,64,512]{2,1,0:T(8,128)(2,1)S(1)}, bf16[2,64,512]{2,1,0:T(8,128)(2,1)S(1)}, u32[]{:S(2)}, u32[]{:S(2)}) collective-permute-start(bf16[2,64,512]{2,1,0:T(8,128)(2,1)S(1)} %halve.1.refs_3_), channel_id=1, source_target_pairs={{0,1},{1,0},{2,3},{3,2},{4,5},{5,4},{6,7},{7,6},{8,9},{9,8},{10,11... | collective-permute-start | bytes 393224 | tf_op jit(solution)/shard_map/ppermute | solution.py:187
  24.1 7.1 %collective-permute-start.10 = (bf16[4,64,256]{2,1,0:T(8,128)(2,1)S(1)}, bf16[4,64,256]{2,1,0:T(8,128)(2,1)S(1)}, u32[]{:S(2)}, u32[]{:S(2)}) collective-permute-start(bf16[4,64,256]{2,1,0:T(8,128)(2,1)S(1)} %second_sum.6), channel_id=1, source_target_pairs={{0,16},{4,12},{8,24},{12,4},{16,0},{20,28},{24,8},{28,20},{1,17},{... | collective-permute-start | bytes 393224 | tf_op jit(solution)/shard_map/ppermute | solution.py:182
  25.7 5.4 %collective-permute-start.13 = (bf16[4,64,256]{2,1,0:T(8,128)(2,1)S(1)}, bf16[4,64,256]{2,1,0:T(8,128)(2,1)S(1)}, u32[]{:S(2)}, u32[]{:S(2)}) collective-permute-start(bf16[4,64,256]{2,1,0:T(8,128)(2,1)S(1)} %second_sum.7), channel_id=1, source_target_pairs={{0,16},{4,12},{8,24},{12,4},{16,0},{20,28},{24,8},{28,20},{1,17},{... | collective-permute-start | bytes 393224 | tf_op jit(solution)/shard_map/ppermute | solution.py:182
  27.0 7.8 %collective-permute-start.7 = (bf16[64,512]{1,0:T(8,128)(2,1)S(1)}, bf16[64,512]{1,0:T(8,128)(2,1)S(1)}, u32[]{:S(2)}, u32[]{:S(2)}) collective-permute-start(bf16[64,512]{1,0:T(8,128)(2,1)S(1)} %get-tuple-element.14), channel_id=1, source_target_pairs={{0,3},{1,2},{2,1},{3,0},{4,7},{5,6},{6,5},{7,4},{8,11},{9,10},{10,... | collective-permute-start | bytes 196616 | tf_op jit(solution)/shard_map/ppermute | solution.py:187
  31.3 7.3 %collective-permute-start.14 = (bf16[64,512]{1,0:T(8,128)(2,1)S(1)}, bf16[64,512]{1,0:T(8,128)(2,1)S(1)}, u32[]{:S(2)}, u32[]{:S(2)}) collective-permute-start(bf16[64,512]{1,0:T(8,128)(2,1)S(1)} %get-tuple-element.16), channel_id=1, source_target_pairs={{0,2},{1,3},{2,0},{3,1},{4,6},{5,7},{6,4},{7,5},{8,10},{9,11},{10,... | collective-permute-start | bytes 196616 | tf_op jit(solution)/shard_map/ppermute | solution.py:187
  33.5 8.0 %collective-permute-start.15 = (bf16[64,512]{1,0:T(8,128)(2,1)S(1)}, bf16[64,512]{1,0:T(8,128)(2,1)S(1)}, u32[]{:S(2)}, u32[]{:S(2)}) collective-permute-start(bf16[64,512]{1,0:T(8,128)(2,1)S(1)} %get-tuple-element.17), channel_id=1, source_target_pairs={{0,3},{1,2},{2,1},{3,0},{4,7},{5,6},{6,5},{7,4},{8,11},{9,10},{10,... | collective-permute-start | bytes 196616 | tf_op jit(solution)/shard_map/ppermute | solution.py:187
  33.8 7.8 %collective-permute-start.16 = (bf16[64,512]{1,0:T(8,128)(2,1)S(1)}, bf16[64,512]{1,0:T(8,128)(2,1)S(1)}, u32[]{:S(2)}, u32[]{:S(2)}) collective-permute-start(bf16[64,512]{1,0:T(8,128)(2,1)S(1)} %get-tuple-element.18), channel_id=1, source_target_pairs={{0,1},{1,0},{2,3},{3,2},{4,5},{5,4},{6,7},{7,6},{8,9},{9,8},{10,11... | collective-permute-start | bytes 196616 | tf_op jit(solution)/shard_map/ppermute | solution.py:187
  35.0 8.2 %collective-permute-start.17 = (bf16[64,512]{1,0:T(8,128)(2,1)S(1)}, bf16[64,512]{1,0:T(8,128)(2,1)S(1)}, u32[]{:S(2)}, u32[]{:S(2)}) collective-permute-start(bf16[64,512]{1,0:T(8,128)(2,1)S(1)} %weights.2.refs_0_), channel_id=1, source_target_pairs={{0,1},{1,0},{2,3},{3,2},{4,5},{5,4},{6,7},{7,6},{8,9},{9,8},{10,11... | collective-permute-start | bytes 196616 | tf_op jit(solution)/shard_map/ppermute | solution.py:187
  36.7 10.4 %collective-permute-start.18 = (bf16[64,512]{1,0:T(8,128)(2,1)S(1)}, bf16[64,512]{1,0:T(8,128)(2,1)S(1)}, u32[]{:S(2)}, u32[]{:S(2)}) collective-permute-start(bf16[64,512]{1,0:T(8,128)(2,1)S(1)} %weights.2.refs_0_), channel_id=1, source_target_pairs={{0,2},{1,3},{2,0},{3,1},{4,6},{5,7},{6,4},{7,5},{8,10},{9,11},{10,... | collective-permute-start | bytes 196616 | tf_op jit(solution)/shard_map/ppermute | solution.py:187
  38.6 8.5 %collective-permute-start.19 = (bf16[64,512]{1,0:T(8,128)(2,1)S(1)}, bf16[64,512]{1,0:T(8,128)(2,1)S(1)}, u32[]{:S(2)}, u32[]{:S(2)}) collective-permute-start(bf16[64,512]{1,0:T(8,128)(2,1)S(1)} %weights.2.refs_0_), channel_id=1, source_target_pairs={{0,3},{1,2},{2,1},{3,0},{4,7},{5,6},{6,5},{7,4},{8,11},{9,10},{10,... | collective-permute-start | bytes 196616 | tf_op jit(solution)/shard_map/ppermute | solution.py:187
  41.7 5.5 %collective-permute-start.20 = (bf16[64,512]{1,0:T(8,128)(2,1)S(1)}, bf16[64,512]{1,0:T(8,128)(2,1)S(1)}, u32[]{:S(2)}, u32[]{:S(2)}) collective-permute-start(bf16[64,512]{1,0:T(8,128)(2,1)S(1)} %weights.3.refs_4_), channel_id=1, source_target_pairs={{0,1},{1,0},{2,3},{3,2},{4,5},{5,4},{6,7},{7,6},{8,9},{9,8},{10,11... | collective-permute-start | bytes 196616 | tf_op jit(solution)/shard_map/ppermute | solution.py:187
  42.0 7.4 %collective-permute-start.21 = (bf16[64,512]{1,0:T(8,128)(2,1)S(1)}, bf16[64,512]{1,0:T(8,128)(2,1)S(1)}, u32[]{:S(2)}, u32[]{:S(2)}) collective-permute-start(bf16[64,512]{1,0:T(8,128)(2,1)S(1)} %weights.3.refs_4_), channel_id=1, source_target_pairs={{0,2},{1,3},{2,0},{3,1},{4,6},{5,7},{6,4},{7,5},{8,10},{9,11},{10,... | collective-permute-start | bytes 196616 | tf_op jit(solution)/shard_map/ppermute | solution.py:187
  43.2 6.2 %collective-permute-start.22 = (bf16[64,512]{1,0:T(8,128)(2,1)S(1)}, bf16[64,512]{1,0:T(8,128)(2,1)S(1)}, u32[]{:S(2)}, u32[]{:S(2)}) collective-permute-start(bf16[64,512]{1,0:T(8,128)(2,1)S(1)} %weights.3.refs_4_), channel_id=1, source_target_pairs={{0,3},{1,2},{2,1},{3,0},{4,7},{5,6},{6,5},{7,4},{8,11},{9,10},{10,... | collective-permute-start | bytes 196616 | tf_op jit(solution)/shard_map/ppermute | solution.py:187
  (3 other events, 28.5 us)

commit v4 on v3

--- a/solution.py
+++ b/solution.py
@@ -18,8 +18,6 @@
 CORES = 2
 STEP = 16
 LANES = 128
-EIGHTHS = ((2, 2), (2, 2))
-HALVE = (True, False)
 ANY = pl.BlockSpec(memory_space=pl.ANY)
 VMEM = pl.BlockSpec(memory_space=pltpu.VMEM)
 
@@ -121,35 +119,43 @@
     return master - learn_rate * update, new_first, new_second
 
 
+def each_piece(total, refs, base=0):
+    refs = list(refs)
+    for size, terms in total:
+        yield pl.ds(base, size), [(refs.pop(0), index) for _, index in terms]
+        base += size
+
+
+def arrays_of(total):
+    return [array for _, terms in total for array, _ in terms]
+
+
 def weights(total, span, state, name, after=()):
-    arrays, indices = zip(*total)
-    shape = arrays[0].shape[-2:]
-    columns = pl.ds(*span)
+    arrays = arrays_of(total)
+    depth = state[0].shape[0]
 
     def kernel(*refs):
-        *terms, master_ref, first_ref, second_ref, out = refs
-
-        def do(rows):
-            value = sum_of(list(zip(terms, indices)), rows)
-            value, _, _ = adam(value, master_ref[rows, columns], first_ref[rows, columns], second_ref[rows, columns])
-            out[rows] = value.astype(out.dtype)
-
-        each_step(shape[0], do)
-
-    return local_kernel(kernel, bf16(*shape), [*arrays, *state], name, after=after)
-
-
-def finish(totals, spans, state):
-    arrays = [array for total in totals for array, _ in total]
+        state_refs, out = refs[len(arrays) : -1], refs[-1]
+        for columns, terms in each_piece(total, refs, span[0]):
+            here = pl.ds(columns.start - span[0], columns.size)
+
+            def do(rows, terms=terms, columns=columns, here=here):
+                value, _, _ = adam(sum_of(terms, rows), *[ref[rows, columns] for ref in state_refs])
+                out[rows, here] = value.astype(out.dtype)
+
+            each_step(depth, do)
+
+    return local_kernel(kernel, bf16(depth, span[1]), [*arrays, *state], name, after=after)
+
+
+def finish(totals, state):
+    total = [piece for pieces in totals for piece in pieces]
+    arrays = arrays_of(total)
     n = len(arrays)
 
     def kernel(*refs):
         state_refs, outs = refs[n : n + 3], refs[n + 3 :]
-        at = 0
-        for span, total in zip(spans, totals):
-            columns = pl.ds(*span)
-            terms = [(ref, index) for ref, (_, index) in zip(refs[at : at + len(total)], total)]
-            at += len(total)
+        for columns, terms in each_piece(total, refs):
 
             def do(rows, terms=terms, columns=columns):
                 values = adam(sum_of(terms, rows), *[ref[rows, columns] for ref in state_refs])
@@ -216,77 +222,161 @@
 
 CHIP_STEPS = [lambda chip, core: chip ^ (1 + core), lambda chip, core: chip ^ (2 - core)]
 OUTER_STEPS = [lambda z, core: z ^ 1, lambda z, core: z ^ 3]
-
-
-def over_group(mine, core_in, chips):
-    _, outer, depth, width = mine.shape
-
-    def first(refs, chip, core, here):
-        targets = [CHIP_STEPS[0](chip, core), chip ^ 3]
-        return [[((i, z), EVERY, local(*refs, to, z)) for i, to in enumerate(targets) for z in range(outer)]]
-
-    [made] = sums([mine, core_in], [bf16(2, outer, depth, width)], first, "first_sum")
-    got = to_chip(made, CHIP_STEPS[0], chips)
-
-    def second(refs, chip, core, here):
-        to = CHIP_STEPS[1](chip, core)
-        return [[((z,), EVERY, local(*refs[:2], to, z) + [(refs[2], (1, z))]) for z in range(outer)]]
-
-    after = yield
-    [made] = sums([mine, core_in, got], [bf16(outer, depth, width)], second, "second_sum", after)
-    yield mine, core_in, got, to_chip(made, CHIP_STEPS[1], chips)
-
-
-def group_pieces(pieces, refs, chip, z, index, more=()):
+PARTNERS = [2, 3, 1]
+
+
+def group_pieces(parts, refs, chip, z, index, more=()):
     out, at = [], 0
-    for k in range(len(pieces)):
-        mine, core_in, got, last = refs[4 * k : 4 * k + 4]
+    for k, (mine, *_) in enumerate(parts):
+        mine_ref, core_ref, got, last = refs[4 * k : 4 * k + 4]
         columns = pl.ds(at, mine.shape[-1])
         at += mine.shape[-1]
-        terms = local(mine, core_in, chip, z) + [(got, (0, z)), (last, (z,))]
+        terms = local(mine_ref, core_ref, chip, z) + [(got, (0, z)), (last, (z,))]
         out.append((index, columns, terms + [(ref.at[..., columns], lead) for ref, lead in more]))
     return out
 
 
-def halve_groups(pieces, inner, outer):
-    depth, width = pieces[0][0].shape[2], sum(piece[0].shape[3] for piece in pieces)
-    arrays = [array for piece in pieces for array in piece]
-
-    def first(refs, chip, core, here):
-        targets = [OUTER_STEPS[0](here, core), here ^ 2]
-        return [[p for i, to in enumerate(targets) for p in group_pieces(pieces, refs, chip, to, (i,))]]
-
-    [begun] = sums(arrays, [bf16(2, depth, width)], first, "halve")
-    got = to_group(begun, OUTER_STEPS[0], inner, outer)
-
-    def second(refs, chip, core, here):
-        to = OUTER_STEPS[1](here, core)
-        return [
-            group_pieces(pieces, refs, chip, here, (), [(refs[-1], (0,))]),
-            group_pieces(pieces, refs, chip, to, (), [(refs[-1], (1,))]),
-        ]
-
-    kept, made = sums([*arrays, got], [f32(depth, width), bf16(depth, width)], second, "halve_again")
-    return [(kept, ()), (to_group(made, OUTER_STEPS[1], inner, outer), ())], begun
-
-
-def direct_groups(pieces, inner, outer):
-    depth, width = pieces[0][0].shape[2], sum(piece[0].shape[3] for piece in pieces)
-    arrays = [array for piece in pieces for array in piece]
-    masks = [2, 3, 1]
-
-    def group(refs, chip, core, here):
-        return [group_pieces(pieces, refs, chip, here ^ m, ()) for m in [0] + masks]
-
-    shapes = [f32(depth, width)] + [bf16(depth, width)] * len(masks)
-    kept, *sends = sums(arrays, shapes, group, "group_sum")
-    return [(kept, ())] + [(to_group(x, lambda z, _, m=m: z ^ m, inner, outer), ()) for x, m in zip(sends, masks)], kept
-
-
-def gather(own, inner, outer):
+def four_by_four(grads, width, inner, outer):
+    chips = inner // CORES
+    depth = grads.shape[1]
+    widths = [width // 4] * 4
+    wide = widths[0] + widths[1]
+    order, last = [], {}
+    parts = [[None, None] for _ in widths]
+
+    def run(arrays, shapes, plan, name):
+        made = sums(arrays, shapes, plan, name, order[-1:])
+        order.append(made[0])
+        return made
+
+    def chip_targets(chip, core):
+        return list(enumerate([CHIP_STEPS[0](chip, core), chip ^ 3]))
+
+    def outer_targets(here, core):
+        return list(enumerate([OUTER_STEPS[0](here, core), here ^ 2]))
+
+    def over_chips(k):
+        def plan(refs, chip, core, here):
+            return [[((i, z), EVERY, local(*refs, to, z)) for i, to in chip_targets(chip, core) for z in range(outer)]]
+
+        [made] = run(parts[k], [bf16(2, outer, depth, widths[k])], plan, "first_sum")
+        parts[k].append(to_chip(made, CHIP_STEPS[0], chips))
+
+    def over_chips_again(k):
+        def plan(refs, chip, core, here):
+            to = CHIP_STEPS[1](chip, core)
+            return [[((z,), EVERY, local(*refs[:2], to, z) + [(refs[2], (1, z))]) for z in range(outer)]]
+
+        [made] = run(parts[k], [bf16(outer, depth, widths[k])], plan, "second_sum")
+        parts[k].append(to_chip(made, CHIP_STEPS[1], chips))
+
+    def halve():
+        def plan(refs, chip, core, here):
+            return [[p for i, to in outer_targets(here, core) for p in group_pieces(parts[:2], refs, chip, to, (i,))]]
+
+        [made] = run([*parts[0], *parts[1]], [bf16(2, depth, wide)], plan, "halve")
+        last["halve"] = to_group(made, OUTER_STEPS[0], inner, outer)
+
+    def halve_again():
+        def plan(refs, chip, core, here):
+            to = OUTER_STEPS[1](here, core)
+            return [
+                group_pieces(parts[:2], refs, chip, here, (), [(refs[-1], (0,))]),
+                group_pieces(parts[:2], refs, chip, to, (), [(refs[-1], (1,))]),
+            ]
+
+        shapes = [f32(depth, wide), bf16(depth, wide)]
+        kept, made = run([*parts[0], *parts[1], last["halve"]], shapes, plan, "halve_again")
+        last["first"] = [(kept, ()), (to_group(made, OUTER_STEPS[1], inner, outer), ())]
+
+    def group():
+        def plan(refs, chip, core, here):
+            return [group_pieces(parts[2:3], refs, chip, here ^ m, ()) for m in [0] + PARTNERS]
+
+        shapes = [f32(depth, widths[2])] + [bf16(depth, widths[2])] * len(PARTNERS)
+        kept, *sends = run(parts[2], shapes, plan, "group_sum")
+        last["second"] = [(kept, ())]
+        for x, m in zip(sends, PARTNERS):
+            last["second"].append((to_group(x, lambda z, _, m=m: z ^ m, inner, outer), ()))
+
+    def early():
+        def plan(refs, chip, core, here):
+            return [
+                [((i, c), EVERY, local(*refs, c, to)) for i, to in outer_targets(here, core) for c in range(chips)]
+            ]
+
+        [made] = run(parts[3], [bf16(2, chips, depth, widths[3])], plan, "early_first")
+        parts[3].append(to_group(made, OUTER_STEPS[0], inner, outer))
+
+    def early_again():
+        def plan(refs, chip, core, here):
+            to = OUTER_STEPS[1](here, core)
+            return [[((c,), EVERY, local(*refs[:2], c, to) + [(refs[2], (1, c))]) for c in range(chips)]]
+
+        [made] = run(parts[3], [bf16(chips, depth, widths[3])], plan, "early_second")
+        parts[3].append(to_group(made, OUTER_STEPS[1], inner, outer))
+
+    def line(refs, c, here):
+        return local(*refs[:2], c, here) + [(refs[2], (0, c)), (refs[3], (c,))]
+
+    def early_chips():
+        def plan(refs, chip, core, here):
+            return [
+                [((), EVERY, line(refs, chip, here))],
+                [((i,), EVERY, line(refs, to, here)) for i, to in chip_targets(chip, core)],
+            ]
+
+        kept, made = run(parts[3], [f32(depth, widths[3]), bf16(2, depth, widths[3])], plan, "early_third")
+        parts[3].append(to_chip(made, CHIP_STEPS[0], chips))
+        last["third"] = [(kept, ()), (parts[3][4], (0,))]
+
+    def early_chips_again():
+        def plan(refs, chip, core, here):
+            return [[((), EVERY, line(refs, CHIP_STEPS[1](chip, core), here) + [(refs[4], (1,))])]]
+
+        [made] = run(parts[3], [bf16(depth, widths[3])], plan, "early_fourth")
+        last["third"].append((to_chip(made, CHIP_STEPS[1], chips), ()))
+
+    def theirs(k):
+        place, grant = (sum(widths[:k]), widths[k]), 4 if order else 52
+        order.append(load(grads, place, 1, width, chips, "load_theirs", order[-1:], grant))
+        parts[k][1] = to_core(order[-1], inner)
+
+    def ours(k):
+        place = sum(widths[:k]), widths[k]
+        order.append(load(grads, place, 0, width, chips, "load_mine", order[-1:]))
+        parts[k][0] = order[-1]
+
+    for k in (0, 3, 1, 2):
+        theirs(k)
+    ours(0)
+    over_chips(0)
+    ours(3)
+    early()
+    ours(1)
+    over_chips(1)
+    ours(2)
+    over_chips(2)
+    over_chips_again(0)
+    early_again()
+    over_chips_again(1)
+    over_chips_again(2)
+    halve()
+    early_chips()
+    group()
+    halve_again()
+    early_chips_again()
+    return [[(wide, last["first"])], [(widths[2], last["second"]), (widths[3], last["third"])]]
+
+
+def gather(own, inner, outer, straight):
     if outer == 4:
-        far, diag, near = [to_group(own, lambda z, _, m=m: z ^ m, inner, outer) for m in (2, 3, 1)]
-        return own, near, far, diag
+        if straight:
+            pieces = {m: to_group(own, lambda z, _, m=m: z ^ m, inner, outer) for m in (2, 3, 1)}
+        else:
+            pieces = {m: to_group(own, lambda z, _, m=m: z ^ m, inner, outer) for m in (2, 1)}
+            pieces[3] = to_group(pieces[2], lambda z, _: z ^ 1, inner, outer)
+        return own, *[pieces[m] for m in (2, 1, 3)]
     return own, *[to_group(own, lambda z, _, s=s: (z + s) % outer, inner, outer) for s in range(1, outer)]
 
 
@@ -296,34 +386,19 @@
     grads = gradients.reshape(outer, owned, columns)
     state = (master, first, second)
 
-    if chips == 4 and outer == 4 and width % (8 * LANES) == 0:
-        sizes = [n * width // 8 for span in EIGHTHS for n in span]
-        parts = [(sum(sizes[:k]), size) for k, size in enumerate(sizes)]
-        theirs = [load(grads, part, 1, width, chips, "load_theirs", grant=4 if k else 52) for k, part in enumerate(parts)]
-        core_in = [to_core(x, inner) for x in theirs]
-        mine = [load(grads, part, 0, width, chips, "load_mine") for part in parts]
-        ways = [over_group(m, c, chips) for m, c in zip(mine, core_in)]
-        for way in ways:
-            next(way)
-        sources = [lambda z, m=m: z ^ m for m in range(4)]
-        spans, totals, at, begun = [], [], 0, []
-        for k, span in enumerate(EIGHTHS):
-            after = [[]] * (len(span) - 1) + [begun]
-            some = [way.send(after[n]) for n, way in enumerate(ways[at : at + len(span)])]
-            spans.append((parts[at][0], sum(sizes[at : at + len(span)])))
-            at += len(span)
-            total, first_made = (halve_groups if HALVE[k] else direct_groups)(some, inner, outer)
-            totals.append(total)
-            begun = [first_made]
+    if chips == 4 and outer == 4 and width % (4 * LANES) == 0:
+        totals = four_by_four(grads, width, inner, outer)
+        sources = [lambda z, m=m: z ^ m for m in (0, 2, 1, 3)]
     else:
-        spans = [(0, width)]
         sources = [lambda z, s=s: (z + outer - s) % outer for s in range(outer)]
-        theirs, mine = [load(grads, spans[0], side, width, chips, "load") for side in (1, 0)]
-        totals = [plain_total(mine, to_core(theirs, inner), inner, outer)]
-
+        theirs, mine = [load(grads, (0, width), side, width, chips, "load") for side in (1, 0)]
+        totals = [[(width, plain_total(mine, to_core(theirs, inner), inner, outer))]]
+
+    sizes = [sum(size for size, _ in total) for total in totals]
+    spans = [(sum(sizes[:k]), size) for k, size in enumerate(sizes)]
     made = [weights(total, span, state, "weights") for total, span in zip(totals, spans)]
-    copy = assemble([gather(new, inner, outer) for new in made], sources, spans, outer, width)
-    return (*finish(totals, spans, state), copy.reshape(depth, width))
+    copy = assemble([gather(new, inner, outer, k == 0) for k, new in enumerate(made)], sources, spans, outer, width)
+    return (*finish(totals, state), copy.reshape(depth, width))
 
 
 def solution(mesh):

time: 50.4 us -> 49.3 us (0.978)
  starting transfers between devices: 34.5 us -> 32.5 us
  waiting for transfers between devices: 9.15 us -> 9.96 us
    ppermute x11 -> x13, waiting for transfers between devices: 2.91 us -> 8.81 us  [to_group(): return lax.ppermute(x, ('inner', 'outer'), pairs)]
    ppermute x8, waiting for transfers between devices: 6.23 us -> 1.14 us  [to_chip(): return lax.ppermute(x, 'inner', pairs)]
    ppermute x8, starting transfers between devices: 12 us -> 9.33 us  [to_chip(): return lax.ppermute(x, 'inner', pairs)]
    ppermute x11 -> x13, starting transfers between devices: 20.8 us -> 21.5 us  [to_group(): return lax.ppermute(x, ('inner', 'outer'), pairs)]
    pallas_call x23 -> x25, Pallas kernels: 5.1 us -> 5.11 us  [local_kernel(): pl.pallas_call(ordered, out_shape=out_shape, in_specs=in_specs + [ANY] *...]
  transfers between devices with their start and end apart: 23 -> 25, of which waited for: 6 -> 9; matrix products, arithmetic and copies ran while one was open for 0% -> 0% of each run, Pallas kernels for 6% -> 6%
where the time goes in v4:
time: 49.3 us; the launch traced here: 49.1 us
  starting transfers between devices  32.5 us (66%)
  waiting for transfers between devices  9.96 us (20%)
  Pallas kernels  5.11 us (10%)
  between operations  0.88 us (2%)
  local copies, waits for them, and re-layouts  0.63 us (1%)
    ppermute x13, starting transfers between devices, to_group(): return lax.ppermute(x, ('inner', 'outer'), pairs)  21.5 us
    ppermute x8, starting transfers between devices, to_chip(): return lax.ppermute(x, 'inner', pairs)  9.33 us
    ppermute x13, waiting for transfers between devices, to_group(): return lax.ppermute(x, ('inner', 'outer'), pairs)  8.81 us
    pallas_call x25, Pallas kernels, local_kernel(): pl.pallas_call(ordered, out_shape=out_shape, in_specs=in_specs + [ANY] *...  5.11 us
    ppermute x4, starting transfers between devices, to_core(): return lax.ppermute(x, 'inner', [(i, i ^ 1) for i in range(inner)])  1.67 us
    ppermute x8, waiting for transfers between devices, to_chip(): return lax.ppermute(x, 'inner', pairs)  1.14 us
  transfers between devices with their start and end apart: 25, of which 9 were waited for; matrix products, arithmetic and copies ran while one was open for 0% of the time, Pallas kernels for 6%

profile of v4, /device:TPU:0, one launch (start us, length us, event | category | flops | bytes accessed | tf_op | source)
XLA Modules:
  0.0 49.1 jit_solution(2564625693034654653)
XLA Ops:
  0.6 1.3 %load_theirs.4.refs_1_ = bf16[4,4,64,256]{3,2,1,0:T(8,128)(2,1)S(1)} custom-call(bf16[4,64,8192]{2,1,0:T(8,128)(2,1)} %bitcast.2), custom_call_target="tpu_custom_call" | custom-call | flops 1572864 | bytes 1572864 | tf_op jit(solution)/shard_map/load_theirs/pallas_call | solution.py:36
  4.8 2.6 %collective-permute-start.1 = (bf16[2,4,64,256]{3,2,1,0:T(8,128)(2,1)S(1)}, bf16[2,4,64,256]{3,2,1,0:T(8,128)(2,1)S(1)}, u32[]{:S(2)}, u32[]{:S(2)}) collective-permute-start(bf16[2,4,64,256]{3,2,1,0:T(8,128)(2,1)S(1)} %first_sum.3.refs_1_), channel_id=1, source_target_pairs={{0,8},{4,20},{8,0},{12,28},{16,24},{20,4},{24,16},{28,12},{1,9},{5... | collective-permute-start | bytes 786440 | tf_op jit(solution)/shard_map/ppermute | solution.py:188
  7.6 1.6 %collective-permute-start.7 = (bf16[2,4,64,256]{3,2,1,0:T(8,128)(2,1)S(1)}, bf16[2,4,64,256]{3,2,1,0:T(8,128)(2,1)S(1)}, u32[]{:S(2)}, u32[]{:S(2)}) collective-permute-start(bf16[2,4,64,256]{3,2,1,0:T(8,128)(2,1)S(1)} %early_first.1.refs_1_), channel_id=1, source_target_pairs={{0,1},{1,0},{2,3},{3,2},{4,5},{5,4},{6,7},{7,6},{8,9},{9,8},{10,11... | collective-permute-start | bytes 786440 | tf_op jit(solution)/shard_map/ppermute | solution.py:193
  10.3 1.5 %collective-permute-start.9 = (bf16[2,4,64,256]{3,2,1,0:T(8,128)(2,1)S(1)}, bf16[2,4,64,256]{3,2,1,0:T(8,128)(2,1)S(1)}, u32[]{:S(2)}, u32[]{:S(2)}) collective-permute-start(bf16[2,4,64,256]{3,2,1,0:T(8,128)(2,1)S(1)} %first_sum.5.refs_3_), channel_id=1, source_target_pairs={{0,8},{4,20},{8,0},{12,28},{16,24},{20,4},{24,16},{28,12},{1,9},{5... | collective-permute-start | bytes 786440 | tf_op jit(solution)/shard_map/ppermute | solution.py:188
  12.0 4.2 %collective-permute-done.7.refs_2_ = bf16[2,4,64,256]{3,2,1,0:T(8,128)(2,1)S(1)} collective-permute-done((bf16[2,4,64,256]{3,2,1,0:T(8,128)(2,1)S(1)}, bf16[2,4,64,256]{3,2,1,0:T(8,128)(2,1)S(1)}, u32[]{:S(2)}, u32[]{:S(2)}) %collective-permute-start.7) | collective-permute-done | bytes 262176 | tf_op jit(solution)/shard_map/ppermute | solution.py:193
  16.3 1.3 %collective-permute-start.8 = (bf16[4,64,256]{2,1,0:T(8,128)(2,1)S(1)}, bf16[4,64,256]{2,1,0:T(8,128)(2,1)S(1)}, u32[]{:S(2)}, u32[]{:S(2)}) collective-permute-start(bf16[4,64,256]{2,1,0:T(8,128)(2,1)S(1)} %second_sum.4.refs_3_), channel_id=1, source_target_pairs={{0,16},{4,12},{8,24},{12,4},{16,0},{20,28},{24,8},{28,20},{1,17},{... | collective-permute-start | bytes 393224 | tf_op jit(solution)/shard_map/ppermute | solution.py:188
  17.6 0.8 %collective-permute-start.5 = (bf16[4,64,256]{2,1,0:T(8,128)(2,1)S(1)}, bf16[4,64,256]{2,1,0:T(8,128)(2,1)S(1)}, u32[]{:S(2)}, u32[]{:S(2)}) collective-permute-start(bf16[4,64,256]{2,1,0:T(8,128)(2,1)S(1)} %second_sum.3.refs_3_), channel_id=1, source_target_pairs={{0,16},{4,12},{8,24},{12,4},{16,0},{20,28},{24,8},{28,20},{1,17},{... | collective-permute-start | bytes 393224 | tf_op jit(solution)/shard_map/ppermute | solution.py:188
  18.4 3.6 %collective-permute-start.12 = (bf16[4,64,256]{2,1,0:T(8,128)(2,1)S(1)}, bf16[4,64,256]{2,1,0:T(8,128)(2,1)S(1)}, u32[]{:S(2)}, u32[]{:S(2)}) collective-permute-start(bf16[4,64,256]{2,1,0:T(8,128)(2,1)S(1)} %early_second.1.refs_3_), channel_id=1, source_target_pairs={{0,3},{1,2},{2,1},{3,0},{4,7},{5,6},{6,5},{7,4},{8,11},{9,10},{10,... | collective-permute-start | bytes 393224 | tf_op jit(solution)/shard_map/ppermute | solution.py:193
  22.8 1.6 %collective-permute-start.10 = (bf16[2,64,512]{2,1,0:T(8,128)(2,1)S(1)}, bf16[2,64,512]{2,1,0:T(8,128)(2,1)S(1)}, u32[]{:S(2)}, u32[]{:S(2)}) collective-permute-start(bf16[2,64,512]{2,1,0:T(8,128)(2,1)S(1)} %halve.1.refs_4_), channel_id=1, source_target_pairs={{0,1},{1,0},{2,3},{3,2},{4,5},{5,4},{6,7},{7,6},{8,9},{9,8},{10,11... | collective-permute-start | bytes 393224 | tf_op jit(solution)/shard_map/ppermute | solution.py:193
  24.5 1.1 %collective-permute-done.12.refs_3_ = bf16[4,64,256]{2,1,0:T(8,128)(2,1)S(1)} collective-permute-done((bf16[4,64,256]{2,1,0:T(8,128)(2,1)S(1)}, bf16[4,64,256]{2,1,0:T(8,128)(2,1)S(1)}, u32[]{:S(2)}, u32[]{:S(2)}) %collective-permute-start.12) | collective-permute-done | bytes 131104 | tf_op jit(solution)/shard_map/ppermute | solution.py:193
  25.6 1.1 %collective-permute-start.17 = (bf16[2,64,256]{2,1,0:T(8,128)(2,1)S(1)}, bf16[2,64,256]{2,1,0:T(8,128)(2,1)S(1)}, u32[]{:S(2)}, u32[]{:S(2)}) collective-permute-start(bf16[2,64,256]{2,1,0:T(8,128)(2,1)S(1)} %get-tuple-element.22), channel_id=1, source_target_pairs={{0,8},{4,20},{8,0},{12,28},{16,24},{20,4},{24,16},{28,12},{1,9},{5... | collective-permute-start | bytes 196616 | tf_op jit(solution)/shard_map/ppermute | solution.py:188
  26.8 1.0 %collective-permute-done.11.refs_3_ = bf16[4,64,256]{2,1,0:T(8,128)(2,1)S(1)} collective-permute-done((bf16[4,64,256]{2,1,0:T(8,128)(2,1)S(1)}, bf16[4,64,256]{2,1,0:T(8,128)(2,1)S(1)}, u32[]{:S(2)}, u32[]{:S(2)}) %collective-permute-start.11) | collective-permute-done | bytes 131104 | tf_op jit(solution)/shard_map/ppermute | solution.py:188
  27.9 2.4 %collective-permute-start.14 = (bf16[64,256]{1,0:T(8,128)(2,1)S(1)}, bf16[64,256]{1,0:T(8,128)(2,1)S(1)}, u32[]{:S(2)}, u32[]{:S(2)}) collective-permute-start(bf16[64,256]{1,0:T(8,128)(2,1)S(1)} %get-tuple-element.19), channel_id=1, source_target_pairs={{0,2},{1,3},{2,0},{3,1},{4,6},{5,7},{6,4},{7,5},{8,10},{9,11},{10,... | collective-permute-start | bytes 98312 | tf_op jit(solution)/shard_map/ppermute | solution.py:193
  30.3 1.3 %collective-permute-start.15 = (bf16[64,256]{1,0:T(8,128)(2,1)S(1)}, bf16[64,256]{1,0:T(8,128)(2,1)S(1)}, u32[]{:S(2)}, u32[]{:S(2)}) collective-permute-start(bf16[64,256]{1,0:T(8,128)(2,1)S(1)} %get-tuple-element.20), channel_id=1, source_target_pairs={{0,3},{1,2},{2,1},{3,0},{4,7},{5,6},{6,5},{7,4},{8,11},{9,10},{10,... | collective-permute-start | bytes 98312 | tf_op jit(solution)/shard_map/ppermute | solution.py:193
  31.8 0.8 %collective-permute-start.18 = (bf16[64,256]{1,0:T(8,128)(2,1)S(1)}, bf16[64,256]{1,0:T(8,128)(2,1)S(1)}, u32[]{:S(2)}, u32[]{:S(2)}) collective-permute-start(bf16[64,256]{1,0:T(8,128)(2,1)S(1)} %early_fourth.1), channel_id=1, source_target_pairs={{0,16},{4,12},{8,24},{12,4},{16,0},{20,28},{24,8},{28,20},{1,17},{... | collective-permute-start | bytes 98312 | tf_op jit(solution)/shard_map/ppermute | solution.py:188
  32.6 2.9 %collective-permute-start.13 = (bf16[64,512]{1,0:T(8,128)(2,1)S(1)}, bf16[64,512]{1,0:T(8,128)(2,1)S(1)}, u32[]{:S(2)}, u32[]{:S(2)}) collective-permute-start(bf16[64,512]{1,0:T(8,128)(2,1)S(1)} %get-tuple-element.18), channel_id=1, source_target_pairs={{0,3},{1,2},{2,1},{3,0},{4,7},{5,6},{6,5},{7,4},{8,11},{9,10},{10,... | collective-permute-start | bytes 196616 | tf_op jit(solution)/shard_map/ppermute | solution.py:193
  36.7 2.3 %collective-permute-start.22 = (bf16[64,512]{1,0:T(8,128)(2,1)S(1)}, bf16[64,512]{1,0:T(8,128)(2,1)S(1)}, u32[]{:S(2)}, u32[]{:S(2)}) collective-permute-start(bf16[64,512]{1,0:T(8,128)(2,1)S(1)} %weights.3.refs_4_), channel_id=1, source_target_pairs={{0,2},{1,3},{2,0},{3,1},{4,6},{5,7},{6,4},{7,5},{8,10},{9,11},{10,... | collective-permute-start | bytes 196616 | tf_op jit(solution)/shard_map/ppermute | solution.py:193
  39.5 2.3 %collective-permute-start.21 = (bf16[64,512]{1,0:T(8,128)(2,1)S(1)}, bf16[64,512]{1,0:T(8,128)(2,1)S(1)}, u32[]{:S(2)}, u32[]{:S(2)}) collective-permute-start(bf16[64,512]{1,0:T(8,128)(2,1)S(1)} %weights.2.refs_0_), channel_id=1, source_target_pairs={{0,3},{1,2},{2,1},{3,0},{4,7},{5,6},{6,5},{7,4},{8,11},{9,10},{10,... | collective-permute-start | bytes 196616 | tf_op jit(solution)/shard_map/ppermute | solution.py:193
  41.9 2.1 %collective-permute-start.19 = (bf16[64,512]{1,0:T(8,128)(2,1)S(1)}, bf16[64,512]{1,0:T(8,128)(2,1)S(1)}, u32[]{:S(2)}, u32[]{:S(2)}) collective-permute-start(bf16[64,512]{1,0:T(8,128)(2,1)S(1)} %weights.2.refs_0_), channel_id=1, source_target_pairs={{0,2},{1,3},{2,0},{3,1},{4,6},{5,7},{6,4},{7,5},{8,10},{9,11},{10,... | collective-permute-start | bytes 196616 | tf_op jit(solution)/shard_map/ppermute | solution.py:193
  44.0 0.8 %collective-permute-start.24 = (bf16[64,512]{1,0:T(8,128)(2,1)S(1)}, bf16[64,512]{1,0:T(8,128)(2,1)S(1)}, u32[]{:S(2)}, u32[]{:S(2)}) collective-permute-start(bf16[64,512]{1,0:T(8,128)(2,1)S(1)} %collective-permute-done.22.refs_5_), channel_id=1, source_target_pairs={{0,1},{1,0},{2,3},{3,2},{4,5},{5,4},{6,7},{7,6},{8,9},{9,8},{10,11... | collective-permute-start | bytes 196616 | tf_op jit(solution)/shard_map/ppermute | solution.py:193
  44.7 1.0 %finish.1 = (f32[64,1024]{1,0:T(8,128)}, f32[64,1024]{1,0:T(8,128)}, f32[64,1024]{1,0:T(8,128)}) custom-call(f32[64,512]{1,0:T(8,128)S(1)} %get-tuple-element.17.refs_5_.refs_0_, bf16[64,512]{1,0:T(8,128)(2,1)S(1)} %collective-permute-done.13.refs_1_, f32[64,256]{1,0:T(8,128)S(1)} %get-tuple-element.16.refs_9_.refs_2_.refs_0_, ...), custom_call_target="tpu_custom_call" | custom-call | flops 2359296 | bytes 2359296 | tf_op jit(solution)/shard_map/finish/pallas_call | solution.py:36
  46.4 0.7 %collective-permute-done.19.refs_1_ = bf16[64,512]{1,0:T(8,128)(2,1)S(1)} collective-permute-done((bf16[64,512]{1,0:T(8,128)(2,1)S(1)}, bf16[64,512]{1,0:T(8,128)(2,1)S(1)}, u32[]{:S(2)}, u32[]{:S(2)}) %collective-permute-start.19) | collective-permute-done | bytes 65568 | tf_op jit(solution)/shard_map/ppermute | solution.py:193
  47.1 1.2 %collective-permute-done.24.refs_7_ = bf16[64,512]{1,0:T(8,128)(2,1)S(1)} collective-permute-done((bf16[64,512]{1,0:T(8,128)(2,1)S(1)}, bf16[64,512]{1,0:T(8,128)(2,1)S(1)}, u32[]{:S(2)}, u32[]{:S(2)}) %collective-permute-start.24) | collective-permute-done | bytes 65568 | tf_op jit(solution)/shard_map/ppermute | solution.py:193
  48.3 0.8 %assemble.1 = bf16[4,64,1024]{2,1,0:T(8,128)(2,1)} custom-call(bf16[64,512]{1,0:T(8,128)(2,1)S(1)} %weights.2.refs_0_, bf16[64,512]{1,0:T(8,128)(2,1)S(1)} %collective-permute-done.19.refs_1_, bf16[64,512]{1,0:T(8,128)(2,1)S(1)} %collective-permute-done.20.refs_2_, bf16[64,512]{1,0:T(8,128)(2,1)S(1)} %collective-permute-done.21.refs_3_, ...), custom_call_target="tpu_custom_call" | custom-call | flops 1572864 | bytes 1572864 | tf_op jit(solution)/shard_map/assemble/pallas_call | solution.py:36
  (59 shorter events, 7.6 us)
Async XLA Ops:
  3.2 4.4 %collective-permute-start.2 = (bf16[4,4,64,256]{3,2,1,0:T(8,128)(2,1)S(1)}, bf16[4,4,64,256]{3,2,1,0:T(8,128)(2,1)S(1)}, u32[]{:S(2)}, u32[]{:S(2)}) collective-permute-start(bf16[4,4,64,256]{3,2,1,0:T(8,128)(2,1)S(1)} %load_theirs.5.refs_1_), channel_id=1, source_target_pairs={{0,4},{4,0},{8,12},{12,8},{16,20},{20,16},{24,28},{28,24},{1,5},{5... | collective-permute-start | bytes 1572872 | tf_op jit(solution)/shard_map/ppermute | solution.py:183
  3.8 5.6 %collective-permute-start.3 = (bf16[4,4,64,256]{3,2,1,0:T(8,128)(2,1)S(1)}, bf16[4,4,64,256]{3,2,1,0:T(8,128)(2,1)S(1)}, u32[]{:S(2)}, u32[]{:S(2)}) collective-permute-start(bf16[4,4,64,256]{3,2,1,0:T(8,128)(2,1)S(1)} %load_theirs.6.refs_1_), channel_id=1, source_target_pairs={{0,4},{4,0},{8,12},{12,8},{16,20},{20,16},{24,28},{28,24},{1,5},{5... | collective-permute-start | bytes 1572872 | tf_op jit(solution)/shard_map/ppermute | solution.py:183
  4.1 6.1 %collective-permute-start.4 = (bf16[4,4,64,256]{3,2,1,0:T(8,128)(2,1)S(1)}, bf16[4,4,64,256]{3,2,1,0:T(8,128)(2,1)S(1)}, u32[]{:S(2)}, u32[]{:S(2)}) collective-permute-start(bf16[4,4,64,256]{3,2,1,0:T(8,128)(2,1)S(1)} %load_theirs.7.refs_1_), channel_id=1, source_target_pairs={{0,4},{4,0},{8,12},{12,8},{16,20},{20,16},{24,28},{28,24},{1,5},{5... | collective-permute-start | bytes 1572872 | tf_op jit(solution)/shard_map/ppermute | solution.py:183
  4.8 7.1 %collective-permute-start.1 = (bf16[2,4,64,256]{3,2,1,0:T(8,128)(2,1)S(1)}, bf16[2,4,64,256]{3,2,1,0:T(8,128)(2,1)S(1)}, u32[]{:S(2)}, u32[]{:S(2)}) collective-permute-start(bf16[2,4,64,256]{3,2,1,0:T(8,128)(2,1)S(1)} %first_sum.3.refs_1_), channel_id=1, source_target_pairs={{0,8},{4,20},{8,0},{12,28},{16,24},{20,4},{24,16},{28,12},{1,9},{5... | collective-permute-start | bytes 786440 | tf_op jit(solution)/shard_map/ppermute | solution.py:188
  7.6 8.5 %collective-permute-start.7 = (bf16[2,4,64,256]{3,2,1,0:T(8,128)(2,1)S(1)}, bf16[2,4,64,256]{3,2,1,0:T(8,128)(2,1)S(1)}, u32[]{:S(2)}, u32[]{:S(2)}) collective-permute-start(bf16[2,4,64,256]{3,2,1,0:T(8,128)(2,1)S(1)} %early_first.1.refs_1_), channel_id=1, source_target_pairs={{0,1},{1,0},{2,3},{3,2},{4,5},{5,4},{6,7},{7,6},{8,9},{9,8},{10,11... | collective-permute-start | bytes 786440 | tf_op jit(solution)/shard_map/ppermute | solution.py:193
  9.5 6.7 %collective-permute-start.6 = (bf16[2,4,64,256]{3,2,1,0:T(8,128)(2,1)S(1)}, bf16[2,4,64,256]{3,2,1,0:T(8,128)(2,1)S(1)}, u32[]{:S(2)}, u32[]{:S(2)}) collective-permute-start(bf16[2,4,64,256]{3,2,1,0:T(8,128)(2,1)S(1)} %first_sum.4.refs_1_), channel_id=1, source_target_pairs={{0,8},{4,20},{8,0},{12,28},{16,24},{20,4},{24,16},{28,12},{1,9},{5... | collective-permute-start | bytes 786440 | tf_op jit(solution)/shard_map/ppermute | solution.py:188
  10.3 11.6 %collective-permute-start.9 = (bf16[2,4,64,256]{3,2,1,0:T(8,128)(2,1)S(1)}, bf16[2,4,64,256]{3,2,1,0:T(8,128)(2,1)S(1)}, u32[]{:S(2)}, u32[]{:S(2)}) collective-permute-start(bf16[2,4,64,256]{3,2,1,0:T(8,128)(2,1)S(1)} %first_sum.5.refs_3_), channel_id=1, source_target_pairs={{0,8},{4,20},{8,0},{12,28},{16,24},{20,4},{24,16},{28,12},{1,9},{5... | collective-permute-start | bytes 786440 | tf_op jit(solution)/shard_map/ppermute | solution.py:188
  16.3 6.3 %collective-permute-start.8 = (bf16[4,64,256]{2,1,0:T(8,128)(2,1)S(1)}, bf16[4,64,256]{2,1,0:T(8,128)(2,1)S(1)}, u32[]{:S(2)}, u32[]{:S(2)}) collective-permute-start(bf16[4,64,256]{2,1,0:T(8,128)(2,1)S(1)} %second_sum.4.refs_3_), channel_id=1, source_target_pairs={{0,16},{4,12},{8,24},{12,4},{16,0},{20,28},{24,8},{28,20},{1,17},{... | collective-permute-start | bytes 393224 | tf_op jit(solution)/shard_map/ppermute | solution.py:188
  17.6 5.1 %collective-permute-start.5 = (bf16[4,64,256]{2,1,0:T(8,128)(2,1)S(1)}, bf16[4,64,256]{2,1,0:T(8,128)(2,1)S(1)}, u32[]{:S(2)}, u32[]{:S(2)}) collective-permute-start(bf16[4,64,256]{2,1,0:T(8,128)(2,1)S(1)} %second_sum.3.refs_3_), channel_id=1, source_target_pairs={{0,16},{4,12},{8,24},{12,4},{16,0},{20,28},{24,8},{28,20},{1,17},{... | collective-permute-start | bytes 393224 | tf_op jit(solution)/shard_map/ppermute | solution.py:188
  18.4 7.2 %collective-permute-start.12 = (bf16[4,64,256]{2,1,0:T(8,128)(2,1)S(1)}, bf16[4,64,256]{2,1,0:T(8,128)(2,1)S(1)}, u32[]{:S(2)}, u32[]{:S(2)}) collective-permute-start(bf16[4,64,256]{2,1,0:T(8,128)(2,1)S(1)} %early_second.1.refs_3_), channel_id=1, source_target_pairs={{0,3},{1,2},{2,1},{3,0},{4,7},{5,6},{6,5},{7,4},{8,11},{9,10},{10,... | collective-permute-start | bytes 393224 | tf_op jit(solution)/shard_map/ppermute | solution.py:193
  22.0 5.7 %collective-permute-start.11 = (bf16[4,64,256]{2,1,0:T(8,128)(2,1)S(1)}, bf16[4,64,256]{2,1,0:T(8,128)(2,1)S(1)}, u32[]{:S(2)}, u32[]{:S(2)}) collective-permute-start(bf16[4,64,256]{2,1,0:T(8,128)(2,1)S(1)} %second_sum.5.refs_8_), channel_id=1, source_target_pairs={{0,16},{4,12},{8,24},{12,4},{16,0},{20,28},{24,8},{28,20},{1,17},{... | collective-permute-start | bytes 393224 | tf_op jit(solution)/shard_map/ppermute | solution.py:188
  22.8 8.8 %collective-permute-start.10 = (bf16[2,64,512]{2,1,0:T(8,128)(2,1)S(1)}, bf16[2,64,512]{2,1,0:T(8,128)(2,1)S(1)}, u32[]{:S(2)}, u32[]{:S(2)}) collective-permute-start(bf16[2,64,512]{2,1,0:T(8,128)(2,1)S(1)} %halve.1.refs_4_), channel_id=1, source_target_pairs={{0,1},{1,0},{2,3},{3,2},{4,5},{5,4},{6,7},{7,6},{8,9},{9,8},{10,11... | collective-permute-start | bytes 393224 | tf_op jit(solution)/shard_map/ppermute | solution.py:193
  25.6 6.1 %collective-permute-start.17 = (bf16[2,64,256]{2,1,0:T(8,128)(2,1)S(1)}, bf16[2,64,256]{2,1,0:T(8,128)(2,1)S(1)}, u32[]{:S(2)}, u32[]{:S(2)}) collective-permute-start(bf16[2,64,256]{2,1,0:T(8,128)(2,1)S(1)} %get-tuple-element.22), channel_id=1, source_target_pairs={{0,8},{4,20},{8,0},{12,28},{16,24},{20,4},{24,16},{28,12},{1,9},{5... | collective-permute-start | bytes 196616 | tf_op jit(solution)/shard_map/ppermute | solution.py:188
  27.9 7.7 %collective-permute-start.14 = (bf16[64,256]{1,0:T(8,128)(2,1)S(1)}, bf16[64,256]{1,0:T(8,128)(2,1)S(1)}, u32[]{:S(2)}, u32[]{:S(2)}) collective-permute-start(bf16[64,256]{1,0:T(8,128)(2,1)S(1)} %get-tuple-element.19), channel_id=1, source_target_pairs={{0,2},{1,3},{2,0},{3,1},{4,6},{5,7},{6,4},{7,5},{8,10},{9,11},{10,... | collective-permute-start | bytes 98312 | tf_op jit(solution)/shard_map/ppermute | solution.py:193
  30.3 5.8 %collective-permute-start.15 = (bf16[64,256]{1,0:T(8,128)(2,1)S(1)}, bf16[64,256]{1,0:T(8,128)(2,1)S(1)}, u32[]{:S(2)}, u32[]{:S(2)}) collective-permute-start(bf16[64,256]{1,0:T(8,128)(2,1)S(1)} %get-tuple-element.20), channel_id=1, source_target_pairs={{0,3},{1,2},{2,1},{3,0},{4,7},{5,6},{6,5},{7,4},{8,11},{9,10},{10,... | collective-permute-start | bytes 98312 | tf_op jit(solution)/shard_map/ppermute | solution.py:193
  31.6 4.9 %collective-permute-start.16 = (bf16[64,256]{1,0:T(8,128)(2,1)S(1)}, bf16[64,256]{1,0:T(8,128)(2,1)S(1)}, u32[]{:S(2)}, u32[]{:S(2)}) collective-permute-start(bf16[64,256]{1,0:T(8,128)(2,1)S(1)} %get-tuple-element.21), channel_id=1, source_target_pairs={{0,1},{1,0},{2,3},{3,2},{4,5},{5,4},{6,7},{7,6},{8,9},{9,8},{10,11... | collective-permute-start | bytes 98312 | tf_op jit(solution)/shard_map/ppermute | solution.py:193
  31.8 4.7 %collective-permute-start.18 = (bf16[64,256]{1,0:T(8,128)(2,1)S(1)}, bf16[64,256]{1,0:T(8,128)(2,1)S(1)}, u32[]{:S(2)}, u32[]{:S(2)}) collective-permute-start(bf16[64,256]{1,0:T(8,128)(2,1)S(1)} %early_fourth.1), channel_id=1, source_target_pairs={{0,16},{4,12},{8,24},{12,4},{16,0},{20,28},{24,8},{28,20},{1,17},{... | collective-permute-start | bytes 98312 | tf_op jit(solution)/shard_map/ppermute | solution.py:188
  32.6 6.8 %collective-permute-start.13 = (bf16[64,512]{1,0:T(8,128)(2,1)S(1)}, bf16[64,512]{1,0:T(8,128)(2,1)S(1)}, u32[]{:S(2)}, u32[]{:S(2)}) collective-permute-start(bf16[64,512]{1,0:T(8,128)(2,1)S(1)} %get-tuple-element.18), channel_id=1, source_target_pairs={{0,3},{1,2},{2,1},{3,0},{4,7},{5,6},{6,5},{7,4},{8,11},{9,10},{10,... | collective-permute-start | bytes 196616 | tf_op jit(solution)/shard_map/ppermute | solution.py:193
  36.7 7.3 %collective-permute-start.22 = (bf16[64,512]{1,0:T(8,128)(2,1)S(1)}, bf16[64,512]{1,0:T(8,128)(2,1)S(1)}, u32[]{:S(2)}, u32[]{:S(2)}) collective-permute-start(bf16[64,512]{1,0:T(8,128)(2,1)S(1)} %weights.3.refs_4_), channel_id=1, source_target_pairs={{0,2},{1,3},{2,0},{3,1},{4,6},{5,7},{6,4},{7,5},{8,10},{9,11},{10,... | collective-permute-start | bytes 196616 | tf_op jit(solution)/shard_map/ppermute | solution.py:193
  39.0 6.7 %collective-permute-start.23 = (bf16[64,512]{1,0:T(8,128)(2,1)S(1)}, bf16[64,512]{1,0:T(8,128)(2,1)S(1)}, u32[]{:S(2)}, u32[]{:S(2)}) collective-permute-start(bf16[64,512]{1,0:T(8,128)(2,1)S(1)} %weights.3.refs_4_), channel_id=1, source_target_pairs={{0,1},{1,0},{2,3},{3,2},{4,5},{5,4},{6,7},{7,6},{8,9},{9,8},{10,11... | collective-permute-start | bytes 196616 | tf_op jit(solution)/shard_map/ppermute | solution.py:193
  39.5 6.2 %collective-permute-start.21 = (bf16[64,512]{1,0:T(8,128)(2,1)S(1)}, bf16[64,512]{1,0:T(8,128)(2,1)S(1)}, u32[]{:S(2)}, u32[]{:S(2)}) collective-permute-start(bf16[64,512]{1,0:T(8,128)(2,1)S(1)} %weights.2.refs_0_), channel_id=1, source_target_pairs={{0,3},{1,2},{2,1},{3,0},{4,7},{5,6},{6,5},{7,4},{8,11},{9,10},{10,... | collective-permute-start | bytes 196616 | tf_op jit(solution)/shard_map/ppermute | solution.py:193
  41.9 4.5 %collective-permute-start.20 = (bf16[64,512]{1,0:T(8,128)(2,1)S(1)}, bf16[64,512]{1,0:T(8,128)(2,1)S(1)}, u32[]{:S(2)}, u32[]{:S(2)}) collective-permute-start(bf16[64,512]{1,0:T(8,128)(2,1)S(1)} %weights.2.refs_0_), channel_id=1, source_target_pairs={{0,1},{1,0},{2,3},{3,2},{4,5},{5,4},{6,7},{7,6},{8,9},{9,8},{10,11... | collective-permute-start | bytes 196616 | tf_op jit(solution)/shard_map/ppermute | solution.py:193
  41.9 5.2 %collective-permute-start.19 = (bf16[64,512]{1,0:T(8,128)(2,1)S(1)}, bf16[64,512]{1,0:T(8,128)(2,1)S(1)}, u32[]{:S(2)}, u32[]{:S(2)}) collective-permute-start(bf16[64,512]{1,0:T(8,128)(2,1)S(1)} %weights.2.refs_0_), channel_id=1, source_target_pairs={{0,2},{1,3},{2,0},{3,1},{4,6},{5,7},{6,4},{7,5},{8,10},{9,11},{10,... | collective-permute-start | bytes 196616 | tf_op jit(solution)/shard_map/ppermute | solution.py:193
  44.0 4.3 %collective-permute-start.24 = (bf16[64,512]{1,0:T(8,128)(2,1)S(1)}, bf16[64,512]{1,0:T(8,128)(2,1)S(1)}, u32[]{:S(2)}, u32[]{:S(2)}) collective-permute-start(bf16[64,512]{1,0:T(8,128)(2,1)S(1)} %collective-permute-done.22.refs_5_), channel_id=1, source_target_pairs={{0,1},{1,0},{2,3},{3,2},{4,5},{5,4},{6,7},{7,6},{8,9},{9,8},{10,11... | collective-permute-start | bytes 196616 | tf_op jit(solution)/shard_map/ppermute | solution.py:193
  (5 other events, 46.4 us)

commit v5 on v4

--- a/solution.py
+++ b/solution.py
@@ -221,7 +221,7 @@
 
 
 CHIP_STEPS = [lambda chip, core: chip ^ (1 + core), lambda chip, core: chip ^ (2 - core)]
-OUTER_STEPS = [lambda z, core: z ^ 1, lambda z, core: z ^ 3]
+SPAN_STEPS, EARLY_STEPS = [[lambda z, core: z ^ 1, lambda z, core, far=far: z ^ far] for far in (2, 3)]
 PARTNERS = [2, 3, 1]
 
 
@@ -252,8 +252,8 @@
     def chip_targets(chip, core):
         return list(enumerate([CHIP_STEPS[0](chip, core), chip ^ 3]))
 
-    def outer_targets(here, core):
-        return list(enumerate([OUTER_STEPS[0](here, core), here ^ 2]))
+    def outer_targets(steps, here, core):
+        return list(enumerate([steps[0](here, core), steps[1](steps[0](here, core), core)]))
 
     def over_chips(k):
         def plan(refs, chip, core, here):
@@ -272,14 +272,14 @@
 
     def halve():
         def plan(refs, chip, core, here):
-            return [[p for i, to in outer_targets(here, core) for p in group_pieces(parts[:2], refs, chip, to, (i,))]]
+            return [[p for i, to in outer_targets(SPAN_STEPS, here, core) for p in group_pieces(parts[:2], refs, chip, to, (i,))]]
 
         [made] = run([*parts[0], *parts[1]], [bf16(2, depth, wide)], plan, "halve")
-        last["halve"] = to_group(made, OUTER_STEPS[0], inner, outer)
+        last["halve"] = to_group(made, SPAN_STEPS[0], inner, outer)
 
     def halve_again():
         def plan(refs, chip, core, here):
-            to = OUTER_STEPS[1](here, core)
+            to = SPAN_STEPS[1](here, core)
             return [
                 group_pieces(parts[:2], refs, chip, here, (), [(refs[-1], (0,))]),
                 group_pieces(parts[:2], refs, chip, to, (), [(refs[-1], (1,))]),
@@ -287,7 +287,7 @@
 
         shapes = [f32(depth, wide), bf16(depth, wide)]
         kept, made = run([*parts[0], *parts[1], last["halve"]], shapes, plan, "halve_again")
-        last["first"] = [(kept, ()), (to_group(made, OUTER_STEPS[1], inner, outer), ())]
+        last["first"] = [(kept, ()), (to_group(made, SPAN_STEPS[1], inner, outer), ())]
 
     def group():
         def plan(refs, chip, core, here):
@@ -302,19 +302,19 @@
     def early():
         def plan(refs, chip, core, here):
             return [
-                [((i, c), EVERY, local(*refs, c, to)) for i, to in outer_targets(here, core) for c in range(chips)]
+                [((i, c), EVERY, local(*refs, c, to)) for i, to in outer_targets(EARLY_STEPS, here, core) for c in range(chips)]
             ]
 
         [made] = run(parts[3], [bf16(2, chips, depth, widths[3])], plan, "early_first")
-        parts[3].append(to_group(made, OUTER_STEPS[0], inner, outer))
+        parts[3].append(to_group(made, EARLY_STEPS[0], inner, outer))
 
     def early_again():
         def plan(refs, chip, core, here):
-            to = OUTER_STEPS[1](here, core)
+            to = EARLY_STEPS[1](here, core)
             return [[((c,), EVERY, local(*refs[:2], c, to) + [(refs[2], (1, c))]) for c in range(chips)]]
 
         [made] = run(parts[3], [bf16(chips, depth, widths[3])], plan, "early_second")
-        parts[3].append(to_group(made, OUTER_STEPS[1], inner, outer))
+        parts[3].append(to_group(made, EARLY_STEPS[1], inner, outer))
 
     def line(refs, c, here):
         return local(*refs[:2], c, here) + [(refs[2], (0, c)), (refs[3], (c,))]
@@ -358,8 +358,8 @@
     ours(2)
     over_chips(2)
     over_chips_again(0)
+    over_chips_again(1)
     early_again()
-    over_chips_again(1)
     over_chips_again(2)
     halve()
     early_chips()

time: 49.3 us -> 49 us (level)
  waiting for transfers between devices: 9.96 us -> 7.51 us
  starting transfers between devices: 32.5 us -> 34.7 us
    ppermute x13, waiting for transfers between devices: 8.81 us -> 3.94 us  [to_group(): return lax.ppermute(x, ('inner', 'outer'), pairs)]
    ppermute x8, waiting for transfers between devices: 1.14 us -> 3.56 us  [to_chip(): return lax.ppermute(x, 'inner', pairs)]
    ppermute x8, starting transfers between devices: 9.33 us -> 11.7 us  [to_chip(): return lax.ppermute(x, 'inner', pairs)]
  transfers between devices with their start and end apart: 25 -> 25, of which waited for: 9 -> 7; matrix products, arithmetic and copies ran while one was open for 0% -> 0% of each run, Pallas kernels for 6% -> 6%
where the time goes in v5:
time: 49 us; the launch traced here: 48.9 us
  starting transfers between devices  34.7 us (71%)
  waiting for transfers between devices  7.51 us (15%)
  Pallas kernels  5.12 us (10%)
  between operations  0.9 us (2%)
  local copies, waits for them, and re-layouts  0.63 us (1%)
    ppermute x13, starting transfers between devices, to_group(): return lax.ppermute(x, ('inner', 'outer'), pairs)  21.3 us
    ppermute x8, starting transfers between devices, to_chip(): return lax.ppermute(x, 'inner', pairs)  11.7 us
    pallas_call x25, Pallas kernels, local_kernel(): pl.pallas_call(ordered, out_shape=out_shape, in_specs=in_specs + [ANY] *...  5.12 us
    ppermute x13, waiting for transfers between devices, to_group(): return lax.ppermute(x, ('inner', 'outer'), pairs)  3.94 us
    ppermute x8, waiting for transfers between devices, to_chip(): return lax.ppermute(x, 'inner', pairs)  3.56 us
    ppermute x4, starting transfers between devices, to_core(): return lax.ppermute(x, 'inner', [(i, i ^ 1) for i in range(inner)])  1.67 us
  transfers between devices with their start and end apart: 25, of which 7 were waited for; matrix products, arithmetic and copies ran while one was open for 0% of the time, Pallas kernels for 6%

profile of v5, /device:TPU:0, one launch (start us, length us, event | category | flops | bytes accessed | tf_op | source)
XLA Modules:
  0.0 48.9 jit_solution(14140459355720862757)
XLA Ops:
  0.6 1.3 %load_theirs.4.refs_1_ = bf16[4,4,64,256]{3,2,1,0:T(8,128)(2,1)S(1)} custom-call(bf16[4,64,8192]{2,1,0:T(8,128)(2,1)} %bitcast.2), custom_call_target="tpu_custom_call" | custom-call | flops 1572864 | bytes 1572864 | tf_op jit(solution)/shard_map/load_theirs/pallas_call | solution.py:36
  4.8 2.6 %collective-permute-start.1 = (bf16[2,4,64,256]{3,2,1,0:T(8,128)(2,1)S(1)}, bf16[2,4,64,256]{3,2,1,0:T(8,128)(2,1)S(1)}, u32[]{:S(2)}, u32[]{:S(2)}) collective-permute-start(bf16[2,4,64,256]{3,2,1,0:T(8,128)(2,1)S(1)} %first_sum.3.refs_1_), channel_id=1, source_target_pairs={{0,8},{4,20},{8,0},{12,28},{16,24},{20,4},{24,16},{28,12},{1,9},{5... | collective-permute-start | bytes 786440 | tf_op jit(solution)/shard_map/ppermute | solution.py:188
  7.9 1.1 %collective-permute-start.6 = (bf16[2,4,64,256]{3,2,1,0:T(8,128)(2,1)S(1)}, bf16[2,4,64,256]{3,2,1,0:T(8,128)(2,1)S(1)}, u32[]{:S(2)}, u32[]{:S(2)}) collective-permute-start(bf16[2,4,64,256]{3,2,1,0:T(8,128)(2,1)S(1)} %first_sum.4.refs_1_), channel_id=1, source_target_pairs={{0,8},{4,20},{8,0},{12,28},{16,24},{20,4},{24,16},{28,12},{1,9},{5... | collective-permute-start | bytes 786440 | tf_op jit(solution)/shard_map/ppermute | solution.py:188
  9.0 1.6 %collective-permute-start.9 = (bf16[2,4,64,256]{3,2,1,0:T(8,128)(2,1)S(1)}, bf16[2,4,64,256]{3,2,1,0:T(8,128)(2,1)S(1)}, u32[]{:S(2)}, u32[]{:S(2)}) collective-permute-start(bf16[2,4,64,256]{3,2,1,0:T(8,128)(2,1)S(1)} %early_first.1.refs_1_), channel_id=1, source_target_pairs={{0,1},{1,0},{2,3},{3,2},{4,5},{5,4},{6,7},{7,6},{8,9},{9,8},{10,11... | collective-permute-start | bytes 786440 | tf_op jit(solution)/shard_map/ppermute | solution.py:193
  10.8 1.0 %collective-permute-start.8 = (bf16[2,4,64,256]{3,2,1,0:T(8,128)(2,1)S(1)}, bf16[2,4,64,256]{3,2,1,0:T(8,128)(2,1)S(1)}, u32[]{:S(2)}, u32[]{:S(2)}) collective-permute-start(bf16[2,4,64,256]{3,2,1,0:T(8,128)(2,1)S(1)} %first_sum.5.refs_3_), channel_id=1, source_target_pairs={{0,8},{4,20},{8,0},{12,28},{16,24},{20,4},{24,16},{28,12},{1,9},{5... | collective-permute-start | bytes 786440 | tf_op jit(solution)/shard_map/ppermute | solution.py:188
  11.9 2.7 %collective-permute-done.6.refs_2_.refs_6_ = bf16[2,4,64,256]{3,2,1,0:T(8,128)(2,1)S(1)} collective-permute-done((bf16[2,4,64,256]{3,2,1,0:T(8,128)(2,1)S(1)}, bf16[2,4,64,256]{3,2,1,0:T(8,128)(2,1)S(1)}, u32[]{:S(2)}, u32[]{:S(2)}) %collective-permute-start.6) | collective-permute-done | bytes 262176 | tf_op jit(solution)/shard_map/ppermute | solution.py:188
  14.6 2.1 %collective-permute-start.7 = (bf16[4,64,256]{2,1,0:T(8,128)(2,1)S(1)}, bf16[4,64,256]{2,1,0:T(8,128)(2,1)S(1)}, u32[]{:S(2)}, u32[]{:S(2)}) collective-permute-start(bf16[4,64,256]{2,1,0:T(8,128)(2,1)S(1)} %second_sum.4.refs_3_), channel_id=1, source_target_pairs={{0,16},{4,12},{8,24},{12,4},{16,0},{20,28},{24,8},{28,20},{1,17},{... | collective-permute-start | bytes 393224 | tf_op jit(solution)/shard_map/ppermute | solution.py:188
  17.2 3.8 %collective-permute-start.12 = (bf16[4,64,256]{2,1,0:T(8,128)(2,1)S(1)}, bf16[4,64,256]{2,1,0:T(8,128)(2,1)S(1)}, u32[]{:S(2)}, u32[]{:S(2)}) collective-permute-start(bf16[4,64,256]{2,1,0:T(8,128)(2,1)S(1)} %early_second.1.refs_3_), channel_id=1, source_target_pairs={{0,3},{1,2},{2,1},{3,0},{4,7},{5,6},{6,5},{7,4},{8,11},{9,10},{10,... | collective-permute-start | bytes 393224 | tf_op jit(solution)/shard_map/ppermute | solution.py:193
  21.1 1.6 %collective-permute-start.11 = (bf16[4,64,256]{2,1,0:T(8,128)(2,1)S(1)}, bf16[4,64,256]{2,1,0:T(8,128)(2,1)S(1)}, u32[]{:S(2)}, u32[]{:S(2)}) collective-permute-start(bf16[4,64,256]{2,1,0:T(8,128)(2,1)S(1)} %second_sum.5.refs_8_), channel_id=1, source_target_pairs={{0,16},{4,12},{8,24},{12,4},{16,0},{20,28},{24,8},{28,20},{1,17},{... | collective-permute-start | bytes 393224 | tf_op jit(solution)/shard_map/ppermute | solution.py:188
  23.5 0.8 %collective-permute-done.12.refs_3_ = bf16[4,64,256]{2,1,0:T(8,128)(2,1)S(1)} collective-permute-done((bf16[4,64,256]{2,1,0:T(8,128)(2,1)S(1)}, bf16[4,64,256]{2,1,0:T(8,128)(2,1)S(1)}, u32[]{:S(2)}, u32[]{:S(2)}) %collective-permute-start.12) | collective-permute-done | bytes 131104 | tf_op jit(solution)/shard_map/ppermute | solution.py:193
  24.4 1.6 %collective-permute-start.17 = (bf16[2,64,256]{2,1,0:T(8,128)(2,1)S(1)}, bf16[2,64,256]{2,1,0:T(8,128)(2,1)S(1)}, u32[]{:S(2)}, u32[]{:S(2)}) collective-permute-start(bf16[2,64,256]{2,1,0:T(8,128)(2,1)S(1)} %get-tuple-element.22), channel_id=1, source_target_pairs={{0,8},{4,20},{8,0},{12,28},{16,24},{20,4},{24,16},{28,12},{1,9},{5... | collective-permute-start | bytes 196616 | tf_op jit(solution)/shard_map/ppermute | solution.py:188
  25.9 0.9 %collective-permute-done.11.refs_3_ = bf16[4,64,256]{2,1,0:T(8,128)(2,1)S(1)} collective-permute-done((bf16[4,64,256]{2,1,0:T(8,128)(2,1)S(1)}, bf16[4,64,256]{2,1,0:T(8,128)(2,1)S(1)}, u32[]{:S(2)}, u32[]{:S(2)}) %collective-permute-start.11) | collective-permute-done | bytes 131104 | tf_op jit(solution)/shard_map/ppermute | solution.py:188
  26.9 2.6 %collective-permute-start.14 = (bf16[64,256]{1,0:T(8,128)(2,1)S(1)}, bf16[64,256]{1,0:T(8,128)(2,1)S(1)}, u32[]{:S(2)}, u32[]{:S(2)}) collective-permute-start(bf16[64,256]{1,0:T(8,128)(2,1)S(1)} %get-tuple-element.19), channel_id=1, source_target_pairs={{0,2},{1,3},{2,0},{3,1},{4,6},{5,7},{6,4},{7,5},{8,10},{9,11},{10,... | collective-permute-start | bytes 98312 | tf_op jit(solution)/shard_map/ppermute | solution.py:193
  29.5 1.3 %collective-permute-start.15 = (bf16[64,256]{1,0:T(8,128)(2,1)S(1)}, bf16[64,256]{1,0:T(8,128)(2,1)S(1)}, u32[]{:S(2)}, u32[]{:S(2)}) collective-permute-start(bf16[64,256]{1,0:T(8,128)(2,1)S(1)} %get-tuple-element.20), channel_id=1, source_target_pairs={{0,3},{1,2},{2,1},{3,0},{4,7},{5,6},{6,5},{7,4},{8,11},{9,10},{10,... | collective-permute-start | bytes 98312 | tf_op jit(solution)/shard_map/ppermute | solution.py:193
  31.1 1.6 %collective-permute-start.18 = (bf16[64,256]{1,0:T(8,128)(2,1)S(1)}, bf16[64,256]{1,0:T(8,128)(2,1)S(1)}, u32[]{:S(2)}, u32[]{:S(2)}) collective-permute-start(bf16[64,256]{1,0:T(8,128)(2,1)S(1)} %early_fourth.1), channel_id=1, source_target_pairs={{0,16},{4,12},{8,24},{12,4},{16,0},{20,28},{24,8},{28,20},{1,17},{... | collective-permute-start | bytes 98312 | tf_op jit(solution)/shard_map/ppermute | solution.py:188
  32.7 3.0 %collective-permute-start.13 = (bf16[64,512]{1,0:T(8,128)(2,1)S(1)}, bf16[64,512]{1,0:T(8,128)(2,1)S(1)}, u32[]{:S(2)}, u32[]{:S(2)}) collective-permute-start(bf16[64,512]{1,0:T(8,128)(2,1)S(1)} %get-tuple-element.18), channel_id=1, source_target_pairs={{0,2},{1,3},{2,0},{3,1},{4,6},{5,7},{6,4},{7,5},{8,10},{9,11},{10,... | collective-permute-start | bytes 196616 | tf_op jit(solution)/shard_map/ppermute | solution.py:193
  35.8 2.4 %collective-permute-start.22 = (bf16[64,512]{1,0:T(8,128)(2,1)S(1)}, bf16[64,512]{1,0:T(8,128)(2,1)S(1)}, u32[]{:S(2)}, u32[]{:S(2)}) collective-permute-start(bf16[64,512]{1,0:T(8,128)(2,1)S(1)} %weights.3.refs_4_), channel_id=1, source_target_pairs={{0,2},{1,3},{2,0},{3,1},{4,6},{5,7},{6,4},{7,5},{8,10},{9,11},{10,... | collective-permute-start | bytes 196616 | tf_op jit(solution)/shard_map/ppermute | solution.py:193
  38.9 3.3 %collective-permute-start.21 = (bf16[64,512]{1,0:T(8,128)(2,1)S(1)}, bf16[64,512]{1,0:T(8,128)(2,1)S(1)}, u32[]{:S(2)}, u32[]{:S(2)}) collective-permute-start(bf16[64,512]{1,0:T(8,128)(2,1)S(1)} %weights.2.refs_0_), channel_id=1, source_target_pairs={{0,3},{1,2},{2,1},{3,0},{4,7},{5,6},{6,5},{7,4},{8,11},{9,10},{10,... | collective-permute-start | bytes 196616 | tf_op jit(solution)/shard_map/ppermute | solution.py:193
  42.1 1.2 %collective-permute-start.19 = (bf16[64,512]{1,0:T(8,128)(2,1)S(1)}, bf16[64,512]{1,0:T(8,128)(2,1)S(1)}, u32[]{:S(2)}, u32[]{:S(2)}) collective-permute-start(bf16[64,512]{1,0:T(8,128)(2,1)S(1)} %weights.2.refs_0_), channel_id=1, source_target_pairs={{0,2},{1,3},{2,0},{3,1},{4,6},{5,7},{6,4},{7,5},{8,10},{9,11},{10,... | collective-permute-start | bytes 196616 | tf_op jit(solution)/shard_map/ppermute | solution.py:193
  43.3 0.8 %collective-permute-start.24 = (bf16[64,512]{1,0:T(8,128)(2,1)S(1)}, bf16[64,512]{1,0:T(8,128)(2,1)S(1)}, u32[]{:S(2)}, u32[]{:S(2)}) collective-permute-start(bf16[64,512]{1,0:T(8,128)(2,1)S(1)} %collective-permute-done.22.refs_5_), channel_id=1, source_target_pairs={{0,1},{1,0},{2,3},{3,2},{4,5},{5,4},{6,7},{7,6},{8,9},{9,8},{10,11... | collective-permute-start | bytes 196616 | tf_op jit(solution)/shard_map/ppermute | solution.py:193
  44.2 1.0 %finish.1 = (f32[64,1024]{1,0:T(8,128)}, f32[64,1024]{1,0:T(8,128)}, f32[64,1024]{1,0:T(8,128)}) custom-call(f32[64,512]{1,0:T(8,128)S(1)} %get-tuple-element.17.refs_5_.refs_0_, bf16[64,512]{1,0:T(8,128)(2,1)S(1)} %collective-permute-done.13.refs_1_, f32[64,256]{1,0:T(8,128)S(1)} %get-tuple-element.16.refs_9_.refs_2_.refs_0_, ...), custom_call_target="tpu_custom_call" | custom-call | flops 2359296 | bytes 2359296 | tf_op jit(solution)/shard_map/finish/pallas_call | solution.py:36
  45.2 1.2 %collective-permute-done.20.refs_2_ = bf16[64,512]{1,0:T(8,128)(2,1)S(1)} collective-permute-done((bf16[64,512]{1,0:T(8,128)(2,1)S(1)}, bf16[64,512]{1,0:T(8,128)(2,1)S(1)}, u32[]{:S(2)}, u32[]{:S(2)}) %collective-permute-start.20) | collective-permute-done | bytes 65568 | tf_op jit(solution)/shard_map/ppermute | solution.py:193
  46.4 0.9 %collective-permute-done.19.refs_1_ = bf16[64,512]{1,0:T(8,128)(2,1)S(1)} collective-permute-done((bf16[64,512]{1,0:T(8,128)(2,1)S(1)}, bf16[64,512]{1,0:T(8,128)(2,1)S(1)}, u32[]{:S(2)}, u32[]{:S(2)}) %collective-permute-start.19) | collective-permute-done | bytes 65568 | tf_op jit(solution)/shard_map/ppermute | solution.py:193
  48.0 0.8 %assemble.1 = bf16[4,64,1024]{2,1,0:T(8,128)(2,1)} custom-call(bf16[64,512]{1,0:T(8,128)(2,1)S(1)} %weights.2.refs_0_, bf16[64,512]{1,0:T(8,128)(2,1)S(1)} %collective-permute-done.19.refs_1_, bf16[64,512]{1,0:T(8,128)(2,1)S(1)} %collective-permute-done.20.refs_2_, bf16[64,512]{1,0:T(8,128)(2,1)S(1)} %collective-permute-done.21.refs_3_, ...), custom_call_target="tpu_custom_call" | custom-call | flops 1572864 | bytes 1572864 | tf_op jit(solution)/shard_map/assemble/pallas_call | solution.py:36
  (59 shorter events, 6.7 us)
Async XLA Ops:
  3.2 4.4 %collective-permute-start.2 = (bf16[4,4,64,256]{3,2,1,0:T(8,128)(2,1)S(1)}, bf16[4,4,64,256]{3,2,1,0:T(8,128)(2,1)S(1)}, u32[]{:S(2)}, u32[]{:S(2)}) collective-permute-start(bf16[4,4,64,256]{3,2,1,0:T(8,128)(2,1)S(1)} %load_theirs.5.refs_1_), channel_id=1, source_target_pairs={{0,4},{4,0},{8,12},{12,8},{16,20},{20,16},{24,28},{28,24},{1,5},{5... | collective-permute-start | bytes 1572872 | tf_op jit(solution)/shard_map/ppermute | solution.py:183
  3.8 3.9 %collective-permute-start.3 = (bf16[4,4,64,256]{3,2,1,0:T(8,128)(2,1)S(1)}, bf16[4,4,64,256]{3,2,1,0:T(8,128)(2,1)S(1)}, u32[]{:S(2)}, u32[]{:S(2)}) collective-permute-start(bf16[4,4,64,256]{3,2,1,0:T(8,128)(2,1)S(1)} %load_theirs.6.refs_1_), channel_id=1, source_target_pairs={{0,4},{4,0},{8,12},{12,8},{16,20},{20,16},{24,28},{28,24},{1,5},{5... | collective-permute-start | bytes 1572872 | tf_op jit(solution)/shard_map/ppermute | solution.py:183
  4.1 6.6 %collective-permute-start.4 = (bf16[4,4,64,256]{3,2,1,0:T(8,128)(2,1)S(1)}, bf16[4,4,64,256]{3,2,1,0:T(8,128)(2,1)S(1)}, u32[]{:S(2)}, u32[]{:S(2)}) collective-permute-start(bf16[4,4,64,256]{3,2,1,0:T(8,128)(2,1)S(1)} %load_theirs.7.refs_1_), channel_id=1, source_target_pairs={{0,4},{4,0},{8,12},{12,8},{16,20},{20,16},{24,28},{28,24},{1,5},{5... | collective-permute-start | bytes 1572872 | tf_op jit(solution)/shard_map/ppermute | solution.py:183
  4.8 7.0 %collective-permute-start.1 = (bf16[2,4,64,256]{3,2,1,0:T(8,128)(2,1)S(1)}, bf16[2,4,64,256]{3,2,1,0:T(8,128)(2,1)S(1)}, u32[]{:S(2)}, u32[]{:S(2)}) collective-permute-start(bf16[2,4,64,256]{3,2,1,0:T(8,128)(2,1)S(1)} %first_sum.3.refs_1_), channel_id=1, source_target_pairs={{0,8},{4,20},{8,0},{12,28},{16,24},{20,4},{24,16},{28,12},{1,9},{5... | collective-permute-start | bytes 786440 | tf_op jit(solution)/shard_map/ppermute | solution.py:188
  7.9 6.7 %collective-permute-start.6 = (bf16[2,4,64,256]{3,2,1,0:T(8,128)(2,1)S(1)}, bf16[2,4,64,256]{3,2,1,0:T(8,128)(2,1)S(1)}, u32[]{:S(2)}, u32[]{:S(2)}) collective-permute-start(bf16[2,4,64,256]{3,2,1,0:T(8,128)(2,1)S(1)} %first_sum.4.refs_1_), channel_id=1, source_target_pairs={{0,8},{4,20},{8,0},{12,28},{16,24},{20,4},{24,16},{28,12},{1,9},{5... | collective-permute-start | bytes 786440 | tf_op jit(solution)/shard_map/ppermute | solution.py:188
  9.0 8.1 %collective-permute-start.9 = (bf16[2,4,64,256]{3,2,1,0:T(8,128)(2,1)S(1)}, bf16[2,4,64,256]{3,2,1,0:T(8,128)(2,1)S(1)}, u32[]{:S(2)}, u32[]{:S(2)}) collective-permute-start(bf16[2,4,64,256]{3,2,1,0:T(8,128)(2,1)S(1)} %early_first.1.refs_1_), channel_id=1, source_target_pairs={{0,1},{1,0},{2,3},{3,2},{4,5},{5,4},{6,7},{7,6},{8,9},{9,8},{10,11... | collective-permute-start | bytes 786440 | tf_op jit(solution)/shard_map/ppermute | solution.py:193
  10.8 10.2 %collective-permute-start.8 = (bf16[2,4,64,256]{3,2,1,0:T(8,128)(2,1)S(1)}, bf16[2,4,64,256]{3,2,1,0:T(8,128)(2,1)S(1)}, u32[]{:S(2)}, u32[]{:S(2)}) collective-permute-start(bf16[2,4,64,256]{3,2,1,0:T(8,128)(2,1)S(1)} %first_sum.5.refs_3_), channel_id=1, source_target_pairs={{0,8},{4,20},{8,0},{12,28},{16,24},{20,4},{24,16},{28,12},{1,9},{5... | collective-permute-start | bytes 786440 | tf_op jit(solution)/shard_map/ppermute | solution.py:188
  14.6 8.0 %collective-permute-start.7 = (bf16[4,64,256]{2,1,0:T(8,128)(2,1)S(1)}, bf16[4,64,256]{2,1,0:T(8,128)(2,1)S(1)}, u32[]{:S(2)}, u32[]{:S(2)}) collective-permute-start(bf16[4,64,256]{2,1,0:T(8,128)(2,1)S(1)} %second_sum.4.refs_3_), channel_id=1, source_target_pairs={{0,16},{4,12},{8,24},{12,4},{16,0},{20,28},{24,8},{28,20},{1,17},{... | collective-permute-start | bytes 393224 | tf_op jit(solution)/shard_map/ppermute | solution.py:188
  16.8 5.9 %collective-permute-start.5 = (bf16[4,64,256]{2,1,0:T(8,128)(2,1)S(1)}, bf16[4,64,256]{2,1,0:T(8,128)(2,1)S(1)}, u32[]{:S(2)}, u32[]{:S(2)}) collective-permute-start(bf16[4,64,256]{2,1,0:T(8,128)(2,1)S(1)} %second_sum.3.refs_3_), channel_id=1, source_target_pairs={{0,16},{4,12},{8,24},{12,4},{16,0},{20,28},{24,8},{28,20},{1,17},{... | collective-permute-start | bytes 393224 | tf_op jit(solution)/shard_map/ppermute | solution.py:188
  17.2 7.1 %collective-permute-start.12 = (bf16[4,64,256]{2,1,0:T(8,128)(2,1)S(1)}, bf16[4,64,256]{2,1,0:T(8,128)(2,1)S(1)}, u32[]{:S(2)}, u32[]{:S(2)}) collective-permute-start(bf16[4,64,256]{2,1,0:T(8,128)(2,1)S(1)} %early_second.1.refs_3_), channel_id=1, source_target_pairs={{0,3},{1,2},{2,1},{3,0},{4,7},{5,6},{6,5},{7,4},{8,11},{9,10},{10,... | collective-permute-start | bytes 393224 | tf_op jit(solution)/shard_map/ppermute | solution.py:193
  21.1 5.7 %collective-permute-start.11 = (bf16[4,64,256]{2,1,0:T(8,128)(2,1)S(1)}, bf16[4,64,256]{2,1,0:T(8,128)(2,1)S(1)}, u32[]{:S(2)}, u32[]{:S(2)}) collective-permute-start(bf16[4,64,256]{2,1,0:T(8,128)(2,1)S(1)} %second_sum.5.refs_8_), channel_id=1, source_target_pairs={{0,16},{4,12},{8,24},{12,4},{16,0},{20,28},{24,8},{28,20},{1,17},{... | collective-permute-start | bytes 393224 | tf_op jit(solution)/shard_map/ppermute | solution.py:188
  22.8 8.1 %collective-permute-start.10 = (bf16[2,64,512]{2,1,0:T(8,128)(2,1)S(1)}, bf16[2,64,512]{2,1,0:T(8,128)(2,1)S(1)}, u32[]{:S(2)}, u32[]{:S(2)}) collective-permute-start(bf16[2,64,512]{2,1,0:T(8,128)(2,1)S(1)} %halve.1.refs_4_), channel_id=1, source_target_pairs={{0,1},{1,0},{2,3},{3,2},{4,5},{5,4},{6,7},{7,6},{8,9},{9,8},{10,11... | collective-permute-start | bytes 393224 | tf_op jit(solution)/shard_map/ppermute | solution.py:193
  24.4 6.7 %collective-permute-start.17 = (bf16[2,64,256]{2,1,0:T(8,128)(2,1)S(1)}, bf16[2,64,256]{2,1,0:T(8,128)(2,1)S(1)}, u32[]{:S(2)}, u32[]{:S(2)}) collective-permute-start(bf16[2,64,256]{2,1,0:T(8,128)(2,1)S(1)} %get-tuple-element.22), channel_id=1, source_target_pairs={{0,8},{4,20},{8,0},{12,28},{16,24},{20,4},{24,16},{28,12},{1,9},{5... | collective-permute-start | bytes 196616 | tf_op jit(solution)/shard_map/ppermute | solution.py:188
  26.9 8.8 %collective-permute-start.14 = (bf16[64,256]{1,0:T(8,128)(2,1)S(1)}, bf16[64,256]{1,0:T(8,128)(2,1)S(1)}, u32[]{:S(2)}, u32[]{:S(2)}) collective-permute-start(bf16[64,256]{1,0:T(8,128)(2,1)S(1)} %get-tuple-element.19), channel_id=1, source_target_pairs={{0,2},{1,3},{2,0},{3,1},{4,6},{5,7},{6,4},{7,5},{8,10},{9,11},{10,... | collective-permute-start | bytes 98312 | tf_op jit(solution)/shard_map/ppermute | solution.py:193
  29.5 6.1 %collective-permute-start.15 = (bf16[64,256]{1,0:T(8,128)(2,1)S(1)}, bf16[64,256]{1,0:T(8,128)(2,1)S(1)}, u32[]{:S(2)}, u32[]{:S(2)}) collective-permute-start(bf16[64,256]{1,0:T(8,128)(2,1)S(1)} %get-tuple-element.20), channel_id=1, source_target_pairs={{0,3},{1,2},{2,1},{3,0},{4,7},{5,6},{6,5},{7,4},{8,11},{9,10},{10,... | collective-permute-start | bytes 98312 | tf_op jit(solution)/shard_map/ppermute | solution.py:193
  30.8 4.9 %collective-permute-start.16 = (bf16[64,256]{1,0:T(8,128)(2,1)S(1)}, bf16[64,256]{1,0:T(8,128)(2,1)S(1)}, u32[]{:S(2)}, u32[]{:S(2)}) collective-permute-start(bf16[64,256]{1,0:T(8,128)(2,1)S(1)} %get-tuple-element.21), channel_id=1, source_target_pairs={{0,1},{1,0},{2,3},{3,2},{4,5},{5,4},{6,7},{7,6},{8,9},{9,8},{10,11... | collective-permute-start | bytes 98312 | tf_op jit(solution)/shard_map/ppermute | solution.py:193
  31.1 4.6 %collective-permute-start.18 = (bf16[64,256]{1,0:T(8,128)(2,1)S(1)}, bf16[64,256]{1,0:T(8,128)(2,1)S(1)}, u32[]{:S(2)}, u32[]{:S(2)}) collective-permute-start(bf16[64,256]{1,0:T(8,128)(2,1)S(1)} %early_fourth.1), channel_id=1, source_target_pairs={{0,16},{4,12},{8,24},{12,4},{16,0},{20,28},{24,8},{28,20},{1,17},{... | collective-permute-start | bytes 98312 | tf_op jit(solution)/shard_map/ppermute | solution.py:188
  32.7 6.1 %collective-permute-start.13 = (bf16[64,512]{1,0:T(8,128)(2,1)S(1)}, bf16[64,512]{1,0:T(8,128)(2,1)S(1)}, u32[]{:S(2)}, u32[]{:S(2)}) collective-permute-start(bf16[64,512]{1,0:T(8,128)(2,1)S(1)} %get-tuple-element.18), channel_id=1, source_target_pairs={{0,2},{1,3},{2,0},{3,1},{4,6},{5,7},{6,4},{7,5},{8,10},{9,11},{10,... | collective-permute-start | bytes 196616 | tf_op jit(solution)/shard_map/ppermute | solution.py:193
  35.8 7.5 %collective-permute-start.22 = (bf16[64,512]{1,0:T(8,128)(2,1)S(1)}, bf16[64,512]{1,0:T(8,128)(2,1)S(1)}, u32[]{:S(2)}, u32[]{:S(2)}) collective-permute-start(bf16[64,512]{1,0:T(8,128)(2,1)S(1)} %weights.3.refs_4_), channel_id=1, source_target_pairs={{0,2},{1,3},{2,0},{3,1},{4,6},{5,7},{6,4},{7,5},{8,10},{9,11},{10,... | collective-permute-start | bytes 196616 | tf_op jit(solution)/shard_map/ppermute | solution.py:193
  38.3 6.9 %collective-permute-start.23 = (bf16[64,512]{1,0:T(8,128)(2,1)S(1)}, bf16[64,512]{1,0:T(8,128)(2,1)S(1)}, u32[]{:S(2)}, u32[]{:S(2)}) collective-permute-start(bf16[64,512]{1,0:T(8,128)(2,1)S(1)} %weights.3.refs_4_), channel_id=1, source_target_pairs={{0,1},{1,0},{2,3},{3,2},{4,5},{5,4},{6,7},{7,6},{8,9},{9,8},{10,11... | collective-permute-start | bytes 196616 | tf_op jit(solution)/shard_map/ppermute | solution.py:193
  38.9 6.3 %collective-permute-start.21 = (bf16[64,512]{1,0:T(8,128)(2,1)S(1)}, bf16[64,512]{1,0:T(8,128)(2,1)S(1)}, u32[]{:S(2)}, u32[]{:S(2)}) collective-permute-start(bf16[64,512]{1,0:T(8,128)(2,1)S(1)} %weights.2.refs_0_), channel_id=1, source_target_pairs={{0,3},{1,2},{2,1},{3,0},{4,7},{5,6},{6,5},{7,4},{8,11},{9,10},{10,... | collective-permute-start | bytes 196616 | tf_op jit(solution)/shard_map/ppermute | solution.py:193
  42.1 4.3 %collective-permute-start.20 = (bf16[64,512]{1,0:T(8,128)(2,1)S(1)}, bf16[64,512]{1,0:T(8,128)(2,1)S(1)}, u32[]{:S(2)}, u32[]{:S(2)}) collective-permute-start(bf16[64,512]{1,0:T(8,128)(2,1)S(1)} %weights.2.refs_0_), channel_id=1, source_target_pairs={{0,1},{1,0},{2,3},{3,2},{4,5},{5,4},{6,7},{7,6},{8,9},{9,8},{10,11... | collective-permute-start | bytes 196616 | tf_op jit(solution)/shard_map/ppermute | solution.py:193
  42.1 5.2 %collective-permute-start.19 = (bf16[64,512]{1,0:T(8,128)(2,1)S(1)}, bf16[64,512]{1,0:T(8,128)(2,1)S(1)}, u32[]{:S(2)}, u32[]{:S(2)}) collective-permute-start(bf16[64,512]{1,0:T(8,128)(2,1)S(1)} %weights.2.refs_0_), channel_id=1, source_target_pairs={{0,2},{1,3},{2,0},{3,1},{4,6},{5,7},{6,4},{7,5},{8,10},{9,11},{10,... | collective-permute-start | bytes 196616 | tf_op jit(solution)/shard_map/ppermute | solution.py:193
  43.3 4.7 %collective-permute-start.24 = (bf16[64,512]{1,0:T(8,128)(2,1)S(1)}, bf16[64,512]{1,0:T(8,128)(2,1)S(1)}, u32[]{:S(2)}, u32[]{:S(2)}) collective-permute-start(bf16[64,512]{1,0:T(8,128)(2,1)S(1)} %collective-permute-done.22.refs_5_), channel_id=1, source_target_pairs={{0,1},{1,0},{2,3},{3,2},{4,5},{5,4},{6,7},{7,6},{8,9},{9,8},{10,11... | collective-permute-start | bytes 196616 | tf_op jit(solution)/shard_map/ppermute | solution.py:193
  (5 other events, 44.1 us)

commit v6 on v5

--- a/solution.py
+++ b/solution.py
@@ -99,9 +99,12 @@
 
 
 def sums(operands, shapes, plan, name, after=()):
+    arrays = [x.grads if isinstance(x, Own) else x for x in operands]
+
     def kernel(*refs):
         outs = refs[len(operands) :]
-        for out, pieces in zip(outs, plan(refs[: len(operands)], *place())):
+        given = [x.with_ref(ref) if isinstance(x, Own) else ref for x, ref in zip(operands, refs)]
+        for out, pieces in zip(outs, plan(given, *place())):
             for index, columns, terms in pieces:
 
                 def do(rows, out=out, index=index, columns=columns, terms=terms):
@@ -109,7 +112,7 @@
 
                 each_step(out.shape[-2], do)
 
-    return local_kernel(kernel, shapes, operands, name, after=after)
+    return local_kernel(kernel, shapes, arrays, name, after=after)
 
 
 def adam(total, master, first, second):
@@ -193,8 +196,21 @@
     return lax.ppermute(x, ("inner", "outer"), pairs)
 
 
+class Own:
+    def __init__(self, grads, base, size, width):
+        self.grads, self.base, self.size, self.width = grads, base, size, width
+
+    def with_ref(self, ref):
+        return Own(ref, self.base, self.size, self.width)
+
+    def term(self, chip, block):
+        start = (CORES * chip + place()[1]) * self.width + self.base
+        return self.grads.at[:, :, pl.ds(pl.multiple_of(start, LANES), self.size)], (block,)
+
+
 def local(mine, core_in, chip, block):
-    return [(mine, (chip, block)), (core_in, (chip, block))]
+    own = mine.term(chip, block) if isinstance(mine, Own) else (mine, (chip, block))
+    return [own, (core_in, (chip, block))]
 
 
 EVERY = slice(None)
@@ -227,10 +243,10 @@
 
 def group_pieces(parts, refs, chip, z, index, more=()):
     out, at = [], 0
-    for k, (mine, *_) in enumerate(parts):
+    for k, (_, core_in, *_) in enumerate(parts):
         mine_ref, core_ref, got, last = refs[4 * k : 4 * k + 4]
-        columns = pl.ds(at, mine.shape[-1])
-        at += mine.shape[-1]
+        columns = pl.ds(at, core_in.shape[-1])
+        at += core_in.shape[-1]
         terms = local(mine_ref, core_ref, chip, z) + [(got, (0, z)), (last, (z,))]
         out.append((index, columns, terms + [(ref.at[..., columns], lead) for ref, lead in more]))
     return out
@@ -242,7 +258,7 @@
     widths = [width // 4] * 4
     wide = widths[0] + widths[1]
     order, last = [], {}
-    parts = [[None, None] for _ in widths]
+    parts = [[Own(grads, sum(widths[:k]), size, width), None] for k, size in enumerate(widths)]
 
     def run(arrays, shapes, plan, name):
         made = sums(arrays, shapes, plan, name, order[-1:])
@@ -342,22 +358,15 @@
         order.append(load(grads, place, 1, width, chips, "load_theirs", order[-1:], grant))
         parts[k][1] = to_core(order[-1], inner)
 
-    def ours(k):
-        place = sum(widths[:k]), widths[k]
-        order.append(load(grads, place, 0, width, chips, "load_mine", order[-1:]))
-        parts[k][0] = order[-1]
-
-    for k in (0, 3, 1, 2):
-        theirs(k)
-    ours(0)
+    theirs(0)
+    theirs(1)
+    theirs(3)
+    theirs(2)
     over_chips(0)
-    ours(3)
     early()
-    ours(1)
     over_chips(1)
-    ours(2)
+    over_chips_again(0)
     over_chips(2)
-    over_chips_again(0)
     over_chips_again(1)
     early_again()
     over_chips_again(2)

time: 49 us -> 49 us (level)
  starting transfers between devices: 34.7 us -> 37.9 us
  waiting for transfers between devices: 7.51 us -> 4.83 us
    ppermute x8, waiting for transfers between devices: 3.56 us -> 1.14 us  [to_chip(): return lax.ppermute(x, 'inner', pairs)]
    ppermute x8, starting transfers between devices: 11.7 us -> 13.7 us  [to_chip(): return lax.ppermute(x, 'inner', pairs)]
    ppermute x13, starting transfers between devices: 21.3 us -> 22.6 us  [to_group(): return lax.ppermute(x, ('inner', 'outer'), pairs)]
    pallas_call x25 -> x21, Pallas kernels: 5.12 us -> 4.66 us  [local_kernel(): pl.pallas_call(ordered, out_shape=out_shape, in_specs=in_specs + [ANY] *...]
  transfers between devices with their start and end apart: 25 -> 25, of which waited for: 7 -> 8; matrix products, arithmetic and copies ran while one was open for 0% -> 0% of each run, Pallas kernels for 6% -> 5%
where the time goes in v6:
time: 49 us; the launch traced here: 48.9 us
  starting transfers between devices  37.9 us (77%)
  waiting for transfers between devices  4.83 us (10%)
  Pallas kernels  4.66 us (10%)
  between operations  0.83 us (2%)
  local copies, waits for them, and re-layouts  0.63 us (1%)
    ppermute x13, starting transfers between devices, to_group(): return lax.ppermute(x, ('inner', 'outer'), pairs)  22.6 us
    ppermute x8, starting transfers between devices, to_chip(): return lax.ppermute(x, 'inner', pairs)  13.7 us
    pallas_call x21, Pallas kernels, local_kernel(): pl.pallas_call(ordered, out_shape=out_shape, in_specs=in_specs + [ANY] *...  4.66 us
    ppermute x13, waiting for transfers between devices, to_group(): return lax.ppermute(x, ('inner', 'outer'), pairs)  3.69 us
    ppermute x4, starting transfers between devices, to_core(): return lax.ppermute(x, 'inner', [(i, i ^ 1) for i in range(inner)])  1.61 us
    ppermute x8, waiting for transfers between devices, to_chip(): return lax.ppermute(x, 'inner', pairs)  1.14 us
  transfers between devices with their start and end apart: 25, of which 8 were waited for; matrix products, arithmetic and copies ran while one was open for 0% of the time, Pallas kernels for 5%

profile of v6, /device:TPU:0, one launch (start us, length us, event | category | flops | bytes accessed | tf_op | source)
XLA Modules:
  0.0 48.9 jit_solution(4976371941674029943)
XLA Ops:
  0.6 1.3 %load_theirs.4.refs_1_ = bf16[4,4,64,256]{3,2,1,0:T(8,128)(2,1)S(1)} custom-call(bf16[4,64,8192]{2,1,0:T(8,128)(2,1)} %bitcast.2), custom_call_target="tpu_custom_call" | custom-call | flops 1572864 | bytes 1572864 | tf_op jit(solution)/shard_map/load_theirs/pallas_call | solution.py:36
  4.6 2.6 %collective-permute-start.1 = (bf16[2,4,64,256]{3,2,1,0:T(8,128)(2,1)S(1)}, bf16[2,4,64,256]{3,2,1,0:T(8,128)(2,1)S(1)}, u32[]{:S(2)}, u32[]{:S(2)}) collective-permute-start(bf16[2,4,64,256]{3,2,1,0:T(8,128)(2,1)S(1)} %first_sum.3.refs_2_), channel_id=1, source_target_pairs={{0,8},{4,20},{8,0},{12,28},{16,24},{20,4},{24,16},{28,12},{1,9},{5... | collective-permute-start | bytes 786440 | tf_op jit(solution)/shard_map/ppermute | solution.py:191
  7.4 1.7 %collective-permute-start.5 = (bf16[2,4,64,256]{3,2,1,0:T(8,128)(2,1)S(1)}, bf16[2,4,64,256]{3,2,1,0:T(8,128)(2,1)S(1)}, u32[]{:S(2)}, u32[]{:S(2)}) collective-permute-start(bf16[2,4,64,256]{3,2,1,0:T(8,128)(2,1)S(1)} %first_sum.4.refs_3_), channel_id=1, source_target_pairs={{0,8},{4,20},{8,0},{12,28},{16,24},{20,4},{24,16},{28,12},{1,9},{5... | collective-permute-start | bytes 786440 | tf_op jit(solution)/shard_map/ppermute | solution.py:191
  9.2 1.6 %collective-permute-start.9 = (bf16[2,4,64,256]{3,2,1,0:T(8,128)(2,1)S(1)}, bf16[2,4,64,256]{3,2,1,0:T(8,128)(2,1)S(1)}, u32[]{:S(2)}, u32[]{:S(2)}) collective-permute-start(bf16[2,4,64,256]{3,2,1,0:T(8,128)(2,1)S(1)} %early_first.1.refs_2_), channel_id=1, source_target_pairs={{0,1},{1,0},{2,3},{3,2},{4,5},{5,4},{6,7},{7,6},{8,9},{9,8},{10,11... | collective-permute-start | bytes 786440 | tf_op jit(solution)/shard_map/ppermute | solution.py:196
  10.7 0.9 %collective-permute-done.1.refs_2_ = bf16[2,4,64,256]{3,2,1,0:T(8,128)(2,1)S(1)} collective-permute-done((bf16[2,4,64,256]{3,2,1,0:T(8,128)(2,1)S(1)}, bf16[2,4,64,256]{3,2,1,0:T(8,128)(2,1)S(1)}, u32[]{:S(2)}, u32[]{:S(2)}) %collective-permute-start.1) | collective-permute-done | bytes 262176 | tf_op jit(solution)/shard_map/ppermute | solution.py:191
  11.8 2.1 %collective-permute-start.8 = (bf16[2,4,64,256]{3,2,1,0:T(8,128)(2,1)S(1)}, bf16[2,4,64,256]{3,2,1,0:T(8,128)(2,1)S(1)}, u32[]{:S(2)}, u32[]{:S(2)}) collective-permute-start(bf16[2,4,64,256]{3,2,1,0:T(8,128)(2,1)S(1)} %first_sum.5.refs_3_), channel_id=1, source_target_pairs={{0,8},{4,20},{8,0},{12,28},{16,24},{20,4},{24,16},{28,12},{1,9},{5... | collective-permute-start | bytes 786440 | tf_op jit(solution)/shard_map/ppermute | solution.py:191
  13.9 1.5 %collective-permute-start.4 = (bf16[4,64,256]{2,1,0:T(8,128)(2,1)S(1)}, bf16[4,64,256]{2,1,0:T(8,128)(2,1)S(1)}, u32[]{:S(2)}, u32[]{:S(2)}) collective-permute-start(bf16[4,64,256]{2,1,0:T(8,128)(2,1)S(1)} %second_sum.3.refs_2_), channel_id=1, source_target_pairs={{0,16},{4,12},{8,24},{12,4},{16,0},{20,28},{24,8},{28,20},{1,17},{... | collective-permute-start | bytes 393224 | tf_op jit(solution)/shard_map/ppermute | solution.py:191
  15.5 1.4 %collective-permute-start.7 = (bf16[4,64,256]{2,1,0:T(8,128)(2,1)S(1)}, bf16[4,64,256]{2,1,0:T(8,128)(2,1)S(1)}, u32[]{:S(2)}, u32[]{:S(2)}) collective-permute-start(bf16[4,64,256]{2,1,0:T(8,128)(2,1)S(1)} %second_sum.4.refs_3_), channel_id=1, source_target_pairs={{0,16},{4,12},{8,24},{12,4},{16,0},{20,28},{24,8},{28,20},{1,17},{... | collective-permute-start | bytes 393224 | tf_op jit(solution)/shard_map/ppermute | solution.py:191
  17.3 3.7 %collective-permute-start.12 = (bf16[4,64,256]{2,1,0:T(8,128)(2,1)S(1)}, bf16[4,64,256]{2,1,0:T(8,128)(2,1)S(1)}, u32[]{:S(2)}, u32[]{:S(2)}) collective-permute-start(bf16[4,64,256]{2,1,0:T(8,128)(2,1)S(1)} %early_second.1.refs_3_), channel_id=1, source_target_pairs={{0,3},{1,2},{2,1},{3,0},{4,7},{5,6},{6,5},{7,4},{8,11},{9,10},{10,... | collective-permute-start | bytes 393224 | tf_op jit(solution)/shard_map/ppermute | solution.py:196
  21.1 1.2 %collective-permute-start.11 = (bf16[4,64,256]{2,1,0:T(8,128)(2,1)S(1)}, bf16[4,64,256]{2,1,0:T(8,128)(2,1)S(1)}, u32[]{:S(2)}, u32[]{:S(2)}) collective-permute-start(bf16[4,64,256]{2,1,0:T(8,128)(2,1)S(1)} %second_sum.5.refs_8_), channel_id=1, source_target_pairs={{0,16},{4,12},{8,24},{12,4},{16,0},{20,28},{24,8},{28,20},{1,17},{... | collective-permute-start | bytes 393224 | tf_op jit(solution)/shard_map/ppermute | solution.py:191
  22.3 1.6 %collective-permute-start.10 = (bf16[2,64,512]{2,1,0:T(8,128)(2,1)S(1)}, bf16[2,64,512]{2,1,0:T(8,128)(2,1)S(1)}, u32[]{:S(2)}, u32[]{:S(2)}) collective-permute-start(bf16[2,64,512]{2,1,0:T(8,128)(2,1)S(1)} %halve.1.refs_4_), channel_id=1, source_target_pairs={{0,1},{1,0},{2,3},{3,2},{4,5},{5,4},{6,7},{7,6},{8,9},{9,8},{10,11... | collective-permute-start | bytes 393224 | tf_op jit(solution)/shard_map/ppermute | solution.py:196
  24.3 2.2 %collective-permute-start.17 = (bf16[2,64,256]{2,1,0:T(8,128)(2,1)S(1)}, bf16[2,64,256]{2,1,0:T(8,128)(2,1)S(1)}, u32[]{:S(2)}, u32[]{:S(2)}) collective-permute-start(bf16[2,64,256]{2,1,0:T(8,128)(2,1)S(1)} %get-tuple-element.22), channel_id=1, source_target_pairs={{0,8},{4,20},{8,0},{12,28},{16,24},{20,4},{24,16},{28,12},{1,9},{5... | collective-permute-start | bytes 196616 | tf_op jit(solution)/shard_map/ppermute | solution.py:191
  26.8 3.3 %collective-permute-start.14 = (bf16[64,256]{1,0:T(8,128)(2,1)S(1)}, bf16[64,256]{1,0:T(8,128)(2,1)S(1)}, u32[]{:S(2)}, u32[]{:S(2)}) collective-permute-start(bf16[64,256]{1,0:T(8,128)(2,1)S(1)} %get-tuple-element.19), channel_id=1, source_target_pairs={{0,2},{1,3},{2,0},{3,1},{4,6},{5,7},{6,4},{7,5},{8,10},{9,11},{10,... | collective-permute-start | bytes 98312 | tf_op jit(solution)/shard_map/ppermute | solution.py:196
  30.1 1.2 %collective-permute-start.15 = (bf16[64,256]{1,0:T(8,128)(2,1)S(1)}, bf16[64,256]{1,0:T(8,128)(2,1)S(1)}, u32[]{:S(2)}, u32[]{:S(2)}) collective-permute-start(bf16[64,256]{1,0:T(8,128)(2,1)S(1)} %get-tuple-element.20), channel_id=1, source_target_pairs={{0,3},{1,2},{2,1},{3,0},{4,7},{5,6},{6,5},{7,4},{8,11},{9,10},{10,... | collective-permute-start | bytes 98312 | tf_op jit(solution)/shard_map/ppermute | solution.py:196
  31.5 1.0 %collective-permute-start.18 = (bf16[64,256]{1,0:T(8,128)(2,1)S(1)}, bf16[64,256]{1,0:T(8,128)(2,1)S(1)}, u32[]{:S(2)}, u32[]{:S(2)}) collective-permute-start(bf16[64,256]{1,0:T(8,128)(2,1)S(1)} %early_fourth.1), channel_id=1, source_target_pairs={{0,16},{4,12},{8,24},{12,4},{16,0},{20,28},{24,8},{28,20},{1,17},{... | collective-permute-start | bytes 98312 | tf_op jit(solution)/shard_map/ppermute | solution.py:191
  32.5 2.8 %collective-permute-start.13 = (bf16[64,512]{1,0:T(8,128)(2,1)S(1)}, bf16[64,512]{1,0:T(8,128)(2,1)S(1)}, u32[]{:S(2)}, u32[]{:S(2)}) collective-permute-start(bf16[64,512]{1,0:T(8,128)(2,1)S(1)} %get-tuple-element.18), channel_id=1, source_target_pairs={{0,2},{1,3},{2,0},{3,1},{4,6},{5,7},{6,4},{7,5},{8,10},{9,11},{10,... | collective-permute-start | bytes 196616 | tf_op jit(solution)/shard_map/ppermute | solution.py:196
  36.1 2.8 %collective-permute-start.22 = (bf16[64,512]{1,0:T(8,128)(2,1)S(1)}, bf16[64,512]{1,0:T(8,128)(2,1)S(1)}, u32[]{:S(2)}, u32[]{:S(2)}) collective-permute-start(bf16[64,512]{1,0:T(8,128)(2,1)S(1)} %weights.3.refs_4_), channel_id=1, source_target_pairs={{0,2},{1,3},{2,0},{3,1},{4,6},{5,7},{6,4},{7,5},{8,10},{9,11},{10,... | collective-permute-start | bytes 196616 | tf_op jit(solution)/shard_map/ppermute | solution.py:196
  39.3 2.4 %collective-permute-start.21 = (bf16[64,512]{1,0:T(8,128)(2,1)S(1)}, bf16[64,512]{1,0:T(8,128)(2,1)S(1)}, u32[]{:S(2)}, u32[]{:S(2)}) collective-permute-start(bf16[64,512]{1,0:T(8,128)(2,1)S(1)} %weights.2.refs_0_), channel_id=1, source_target_pairs={{0,3},{1,2},{2,1},{3,0},{4,7},{5,6},{6,5},{7,4},{8,11},{9,10},{10,... | collective-permute-start | bytes 196616 | tf_op jit(solution)/shard_map/ppermute | solution.py:196
  41.7 2.1 %collective-permute-start.19 = (bf16[64,512]{1,0:T(8,128)(2,1)S(1)}, bf16[64,512]{1,0:T(8,128)(2,1)S(1)}, u32[]{:S(2)}, u32[]{:S(2)}) collective-permute-start(bf16[64,512]{1,0:T(8,128)(2,1)S(1)} %weights.2.refs_0_), channel_id=1, source_target_pairs={{0,2},{1,3},{2,0},{3,1},{4,6},{5,7},{6,4},{7,5},{8,10},{9,11},{10,... | collective-permute-start | bytes 196616 | tf_op jit(solution)/shard_map/ppermute | solution.py:196
  43.7 0.8 %collective-permute-start.24 = (bf16[64,512]{1,0:T(8,128)(2,1)S(1)}, bf16[64,512]{1,0:T(8,128)(2,1)S(1)}, u32[]{:S(2)}, u32[]{:S(2)}) collective-permute-start(bf16[64,512]{1,0:T(8,128)(2,1)S(1)} %collective-permute-done.22.refs_5_), channel_id=1, source_target_pairs={{0,1},{1,0},{2,3},{3,2},{4,5},{5,4},{6,7},{7,6},{8,9},{9,8},{10,11... | collective-permute-start | bytes 196616 | tf_op jit(solution)/shard_map/ppermute | solution.py:196
  44.6 1.0 %finish.1 = (f32[64,1024]{1,0:T(8,128)}, f32[64,1024]{1,0:T(8,128)}, f32[64,1024]{1,0:T(8,128)}) custom-call(f32[64,512]{1,0:T(8,128)S(1)} %get-tuple-element.17.refs_5_.refs_0_, bf16[64,512]{1,0:T(8,128)(2,1)S(1)} %collective-permute-done.13.refs_1_, f32[64,256]{1,0:T(8,128)S(1)} %get-tuple-element.16.refs_9_.refs_2_.refs_0_, ...), custom_call_target="tpu_custom_call" | custom-call | flops 2359296 | bytes 2359296 | tf_op jit(solution)/shard_map/finish/pallas_call | solution.py:36
  46.2 0.7 %collective-permute-done.19.refs_1_ = bf16[64,512]{1,0:T(8,128)(2,1)S(1)} collective-permute-done((bf16[64,512]{1,0:T(8,128)(2,1)S(1)}, bf16[64,512]{1,0:T(8,128)(2,1)S(1)}, u32[]{:S(2)}, u32[]{:S(2)}) %collective-permute-start.19) | collective-permute-done | bytes 65568 | tf_op jit(solution)/shard_map/ppermute | solution.py:196
  46.9 1.1 %collective-permute-done.24.refs_7_ = bf16[64,512]{1,0:T(8,128)(2,1)S(1)} collective-permute-done((bf16[64,512]{1,0:T(8,128)(2,1)S(1)}, bf16[64,512]{1,0:T(8,128)(2,1)S(1)}, u32[]{:S(2)}, u32[]{:S(2)}) %collective-permute-start.24) | collective-permute-done | bytes 65568 | tf_op jit(solution)/shard_map/ppermute | solution.py:196
  48.0 0.8 %assemble.1 = bf16[4,64,1024]{2,1,0:T(8,128)(2,1)} custom-call(bf16[64,512]{1,0:T(8,128)(2,1)S(1)} %weights.2.refs_0_, bf16[64,512]{1,0:T(8,128)(2,1)S(1)} %collective-permute-done.19.refs_1_, bf16[64,512]{1,0:T(8,128)(2,1)S(1)} %collective-permute-done.20.refs_2_, bf16[64,512]{1,0:T(8,128)(2,1)S(1)} %collective-permute-done.21.refs_3_, ...), custom_call_target="tpu_custom_call" | custom-call | flops 1572864 | bytes 1572864 | tf_op jit(solution)/shard_map/assemble/pallas_call | solution.py:36
  (55 shorter events, 6.2 us)
Async XLA Ops:
  3.4 3.9 %collective-permute-start.3 = (bf16[4,4,64,256]{3,2,1,0:T(8,128)(2,1)S(1)}, bf16[4,4,64,256]{3,2,1,0:T(8,128)(2,1)S(1)}, u32[]{:S(2)}, u32[]{:S(2)}) collective-permute-start(bf16[4,4,64,256]{3,2,1,0:T(8,128)(2,1)S(1)} %load_theirs.6.refs_1_), channel_id=1, source_target_pairs={{0,4},{4,0},{8,12},{12,8},{16,20},{20,16},{24,28},{28,24},{1,5},{5... | collective-permute-start | bytes 1572872 | tf_op jit(solution)/shard_map/ppermute | solution.py:186
  3.9 3.5 %collective-permute-start.2 = (bf16[4,4,64,256]{3,2,1,0:T(8,128)(2,1)S(1)}, bf16[4,4,64,256]{3,2,1,0:T(8,128)(2,1)S(1)}, u32[]{:S(2)}, u32[]{:S(2)}) collective-permute-start(bf16[4,4,64,256]{3,2,1,0:T(8,128)(2,1)S(1)} %load_theirs.5.refs_1_), channel_id=1, source_target_pairs={{0,4},{4,0},{8,12},{12,8},{16,20},{20,16},{24,28},{28,24},{1,5},{5... | collective-permute-start | bytes 1572872 | tf_op jit(solution)/shard_map/ppermute | solution.py:186
  4.1 7.6 %collective-permute-start.6 = (bf16[4,4,64,256]{3,2,1,0:T(8,128)(2,1)S(1)}, bf16[4,4,64,256]{3,2,1,0:T(8,128)(2,1)S(1)}, u32[]{:S(2)}, u32[]{:S(2)}) collective-permute-start(bf16[4,4,64,256]{3,2,1,0:T(8,128)(2,1)S(1)} %load_theirs.7.refs_2_), channel_id=1, source_target_pairs={{0,4},{4,0},{8,12},{12,8},{16,20},{20,16},{24,28},{28,24},{1,5},{5... | collective-permute-start | bytes 1572872 | tf_op jit(solution)/shard_map/ppermute | solution.py:186
  4.6 7.0 %collective-permute-start.1 = (bf16[2,4,64,256]{3,2,1,0:T(8,128)(2,1)S(1)}, bf16[2,4,64,256]{3,2,1,0:T(8,128)(2,1)S(1)}, u32[]{:S(2)}, u32[]{:S(2)}) collective-permute-start(bf16[2,4,64,256]{3,2,1,0:T(8,128)(2,1)S(1)} %first_sum.3.refs_2_), channel_id=1, source_target_pairs={{0,8},{4,20},{8,0},{12,28},{16,24},{20,4},{24,16},{28,12},{1,9},{5... | collective-permute-start | bytes 786440 | tf_op jit(solution)/shard_map/ppermute | solution.py:191
  7.4 7.9 %collective-permute-start.5 = (bf16[2,4,64,256]{3,2,1,0:T(8,128)(2,1)S(1)}, bf16[2,4,64,256]{3,2,1,0:T(8,128)(2,1)S(1)}, u32[]{:S(2)}, u32[]{:S(2)}) collective-permute-start(bf16[2,4,64,256]{3,2,1,0:T(8,128)(2,1)S(1)} %first_sum.4.refs_3_), channel_id=1, source_target_pairs={{0,8},{4,20},{8,0},{12,28},{16,24},{20,4},{24,16},{28,12},{1,9},{5... | collective-permute-start | bytes 786440 | tf_op jit(solution)/shard_map/ppermute | solution.py:191
  9.2 8.1 %collective-permute-start.9 = (bf16[2,4,64,256]{3,2,1,0:T(8,128)(2,1)S(1)}, bf16[2,4,64,256]{3,2,1,0:T(8,128)(2,1)S(1)}, u32[]{:S(2)}, u32[]{:S(2)}) collective-permute-start(bf16[2,4,64,256]{3,2,1,0:T(8,128)(2,1)S(1)} %early_first.1.refs_2_), channel_id=1, source_target_pairs={{0,1},{1,0},{2,3},{3,2},{4,5},{5,4},{6,7},{7,6},{8,9},{9,8},{10,11... | collective-permute-start | bytes 786440 | tf_op jit(solution)/shard_map/ppermute | solution.py:196
  11.8 9.2 %collective-permute-start.8 = (bf16[2,4,64,256]{3,2,1,0:T(8,128)(2,1)S(1)}, bf16[2,4,64,256]{3,2,1,0:T(8,128)(2,1)S(1)}, u32[]{:S(2)}, u32[]{:S(2)}) collective-permute-start(bf16[2,4,64,256]{3,2,1,0:T(8,128)(2,1)S(1)} %first_sum.5.refs_3_), channel_id=1, source_target_pairs={{0,8},{4,20},{8,0},{12,28},{16,24},{20,4},{24,16},{28,12},{1,9},{5... | collective-permute-start | bytes 786440 | tf_op jit(solution)/shard_map/ppermute | solution.py:191
  13.9 8.4 %collective-permute-start.4 = (bf16[4,64,256]{2,1,0:T(8,128)(2,1)S(1)}, bf16[4,64,256]{2,1,0:T(8,128)(2,1)S(1)}, u32[]{:S(2)}, u32[]{:S(2)}) collective-permute-start(bf16[4,64,256]{2,1,0:T(8,128)(2,1)S(1)} %second_sum.3.refs_2_), channel_id=1, source_target_pairs={{0,16},{4,12},{8,24},{12,4},{16,0},{20,28},{24,8},{28,20},{1,17},{... | collective-permute-start | bytes 393224 | tf_op jit(solution)/shard_map/ppermute | solution.py:191
  15.5 6.8 %collective-permute-start.7 = (bf16[4,64,256]{2,1,0:T(8,128)(2,1)S(1)}, bf16[4,64,256]{2,1,0:T(8,128)(2,1)S(1)}, u32[]{:S(2)}, u32[]{:S(2)}) collective-permute-start(bf16[4,64,256]{2,1,0:T(8,128)(2,1)S(1)} %second_sum.4.refs_3_), channel_id=1, source_target_pairs={{0,16},{4,12},{8,24},{12,4},{16,0},{20,28},{24,8},{28,20},{1,17},{... | collective-permute-start | bytes 393224 | tf_op jit(solution)/shard_map/ppermute | solution.py:191
  17.3 6.9 %collective-permute-start.12 = (bf16[4,64,256]{2,1,0:T(8,128)(2,1)S(1)}, bf16[4,64,256]{2,1,0:T(8,128)(2,1)S(1)}, u32[]{:S(2)}, u32[]{:S(2)}) collective-permute-start(bf16[4,64,256]{2,1,0:T(8,128)(2,1)S(1)} %early_second.1.refs_3_), channel_id=1, source_target_pairs={{0,3},{1,2},{2,1},{3,0},{4,7},{5,6},{6,5},{7,4},{8,11},{9,10},{10,... | collective-permute-start | bytes 393224 | tf_op jit(solution)/shard_map/ppermute | solution.py:196
  21.1 5.6 %collective-permute-start.11 = (bf16[4,64,256]{2,1,0:T(8,128)(2,1)S(1)}, bf16[4,64,256]{2,1,0:T(8,128)(2,1)S(1)}, u32[]{:S(2)}, u32[]{:S(2)}) collective-permute-start(bf16[4,64,256]{2,1,0:T(8,128)(2,1)S(1)} %second_sum.5.refs_8_), channel_id=1, source_target_pairs={{0,16},{4,12},{8,24},{12,4},{16,0},{20,28},{24,8},{28,20},{1,17},{... | collective-permute-start | bytes 393224 | tf_op jit(solution)/shard_map/ppermute | solution.py:191
  22.3 9.0 %collective-permute-start.10 = (bf16[2,64,512]{2,1,0:T(8,128)(2,1)S(1)}, bf16[2,64,512]{2,1,0:T(8,128)(2,1)S(1)}, u32[]{:S(2)}, u32[]{:S(2)}) collective-permute-start(bf16[2,64,512]{2,1,0:T(8,128)(2,1)S(1)} %halve.1.refs_4_), channel_id=1, source_target_pairs={{0,1},{1,0},{2,3},{3,2},{4,5},{5,4},{6,7},{7,6},{8,9},{9,8},{10,11... | collective-permute-start | bytes 393224 | tf_op jit(solution)/shard_map/ppermute | solution.py:196
  24.3 7.2 %collective-permute-start.17 = (bf16[2,64,256]{2,1,0:T(8,128)(2,1)S(1)}, bf16[2,64,256]{2,1,0:T(8,128)(2,1)S(1)}, u32[]{:S(2)}, u32[]{:S(2)}) collective-permute-start(bf16[2,64,256]{2,1,0:T(8,128)(2,1)S(1)} %get-tuple-element.22), channel_id=1, source_target_pairs={{0,8},{4,20},{8,0},{12,28},{16,24},{20,4},{24,16},{28,12},{1,9},{5... | collective-permute-start | bytes 196616 | tf_op jit(solution)/shard_map/ppermute | solution.py:191
  26.8 8.5 %collective-permute-start.14 = (bf16[64,256]{1,0:T(8,128)(2,1)S(1)}, bf16[64,256]{1,0:T(8,128)(2,1)S(1)}, u32[]{:S(2)}, u32[]{:S(2)}) collective-permute-start(bf16[64,256]{1,0:T(8,128)(2,1)S(1)} %get-tuple-element.19), channel_id=1, source_target_pairs={{0,2},{1,3},{2,0},{3,1},{4,6},{5,7},{6,4},{7,5},{8,10},{9,11},{10,... | collective-permute-start | bytes 98312 | tf_op jit(solution)/shard_map/ppermute | solution.py:196
  30.1 5.8 %collective-permute-start.15 = (bf16[64,256]{1,0:T(8,128)(2,1)S(1)}, bf16[64,256]{1,0:T(8,128)(2,1)S(1)}, u32[]{:S(2)}, u32[]{:S(2)}) collective-permute-start(bf16[64,256]{1,0:T(8,128)(2,1)S(1)} %get-tuple-element.20), channel_id=1, source_target_pairs={{0,3},{1,2},{2,1},{3,0},{4,7},{5,6},{6,5},{7,4},{8,11},{9,10},{10,... | collective-permute-start | bytes 98312 | tf_op jit(solution)/shard_map/ppermute | solution.py:196
  31.3 4.6 %collective-permute-start.16 = (bf16[64,256]{1,0:T(8,128)(2,1)S(1)}, bf16[64,256]{1,0:T(8,128)(2,1)S(1)}, u32[]{:S(2)}, u32[]{:S(2)}) collective-permute-start(bf16[64,256]{1,0:T(8,128)(2,1)S(1)} %get-tuple-element.21), channel_id=1, source_target_pairs={{0,1},{1,0},{2,3},{3,2},{4,5},{5,4},{6,7},{7,6},{8,9},{9,8},{10,11... | collective-permute-start | bytes 98312 | tf_op jit(solution)/shard_map/ppermute | solution.py:196
  31.5 4.4 %collective-permute-start.18 = (bf16[64,256]{1,0:T(8,128)(2,1)S(1)}, bf16[64,256]{1,0:T(8,128)(2,1)S(1)}, u32[]{:S(2)}, u32[]{:S(2)}) collective-permute-start(bf16[64,256]{1,0:T(8,128)(2,1)S(1)} %early_fourth.1), channel_id=1, source_target_pairs={{0,16},{4,12},{8,24},{12,4},{16,0},{20,28},{24,8},{28,20},{1,17},{... | collective-permute-start | bytes 98312 | tf_op jit(solution)/shard_map/ppermute | solution.py:191
  32.5 6.7 %collective-permute-start.13 = (bf16[64,512]{1,0:T(8,128)(2,1)S(1)}, bf16[64,512]{1,0:T(8,128)(2,1)S(1)}, u32[]{:S(2)}, u32[]{:S(2)}) collective-permute-start(bf16[64,512]{1,0:T(8,128)(2,1)S(1)} %get-tuple-element.18), channel_id=1, source_target_pairs={{0,2},{1,3},{2,0},{3,1},{4,6},{5,7},{6,4},{7,5},{8,10},{9,11},{10,... | collective-permute-start | bytes 196616 | tf_op jit(solution)/shard_map/ppermute | solution.py:196
  36.1 7.7 %collective-permute-start.22 = (bf16[64,512]{1,0:T(8,128)(2,1)S(1)}, bf16[64,512]{1,0:T(8,128)(2,1)S(1)}, u32[]{:S(2)}, u32[]{:S(2)}) collective-permute-start(bf16[64,512]{1,0:T(8,128)(2,1)S(1)} %weights.3.refs_4_), channel_id=1, source_target_pairs={{0,2},{1,3},{2,0},{3,1},{4,6},{5,7},{6,4},{7,5},{8,10},{9,11},{10,... | collective-permute-start | bytes 196616 | tf_op jit(solution)/shard_map/ppermute | solution.py:196
  38.9 6.7 %collective-permute-start.23 = (bf16[64,512]{1,0:T(8,128)(2,1)S(1)}, bf16[64,512]{1,0:T(8,128)(2,1)S(1)}, u32[]{:S(2)}, u32[]{:S(2)}) collective-permute-start(bf16[64,512]{1,0:T(8,128)(2,1)S(1)} %weights.3.refs_4_), channel_id=1, source_target_pairs={{0,1},{1,0},{2,3},{3,2},{4,5},{5,4},{6,7},{7,6},{8,9},{9,8},{10,11... | collective-permute-start | bytes 196616 | tf_op jit(solution)/shard_map/ppermute | solution.py:196
  39.3 6.3 %collective-permute-start.21 = (bf16[64,512]{1,0:T(8,128)(2,1)S(1)}, bf16[64,512]{1,0:T(8,128)(2,1)S(1)}, u32[]{:S(2)}, u32[]{:S(2)}) collective-permute-start(bf16[64,512]{1,0:T(8,128)(2,1)S(1)} %weights.2.refs_0_), channel_id=1, source_target_pairs={{0,3},{1,2},{2,1},{3,0},{4,7},{5,6},{6,5},{7,4},{8,11},{9,10},{10,... | collective-permute-start | bytes 196616 | tf_op jit(solution)/shard_map/ppermute | solution.py:196
  41.7 4.5 %collective-permute-start.20 = (bf16[64,512]{1,0:T(8,128)(2,1)S(1)}, bf16[64,512]{1,0:T(8,128)(2,1)S(1)}, u32[]{:S(2)}, u32[]{:S(2)}) collective-permute-start(bf16[64,512]{1,0:T(8,128)(2,1)S(1)} %weights.2.refs_0_), channel_id=1, source_target_pairs={{0,1},{1,0},{2,3},{3,2},{4,5},{5,4},{6,7},{7,6},{8,9},{9,8},{10,11... | collective-permute-start | bytes 196616 | tf_op jit(solution)/shard_map/ppermute | solution.py:196
  41.7 5.2 %collective-permute-start.19 = (bf16[64,512]{1,0:T(8,128)(2,1)S(1)}, bf16[64,512]{1,0:T(8,128)(2,1)S(1)}, u32[]{:S(2)}, u32[]{:S(2)}) collective-permute-start(bf16[64,512]{1,0:T(8,128)(2,1)S(1)} %weights.2.refs_0_), channel_id=1, source_target_pairs={{0,2},{1,3},{2,0},{3,1},{4,6},{5,7},{6,4},{7,5},{8,10},{9,11},{10,... | collective-permute-start | bytes 196616 | tf_op jit(solution)/shard_map/ppermute | solution.py:196
  43.7 4.3 %collective-permute-start.24 = (bf16[64,512]{1,0:T(8,128)(2,1)S(1)}, bf16[64,512]{1,0:T(8,128)(2,1)S(1)}, u32[]{:S(2)}, u32[]{:S(2)}) collective-permute-start(bf16[64,512]{1,0:T(8,128)(2,1)S(1)} %collective-permute-done.22.refs_5_), channel_id=1, source_target_pairs={{0,1},{1,0},{2,3},{3,2},{4,5},{5,4},{6,7},{7,6},{8,9},{9,8},{10,11... | collective-permute-start | bytes 196616 | tf_op jit(solution)/shard_map/ppermute | solution.py:196
  (5 other events, 18.6 us)

commit v7 on v6

--- a/solution.py
+++ b/solution.py
@@ -405,7 +405,9 @@
 
     sizes = [sum(size for size, _ in total) for total in totals]
     spans = [(sum(sizes[:k]), size) for k, size in enumerate(sizes)]
-    made = [weights(total, span, state, "weights") for total, span in zip(totals, spans)]
+    made = []
+    for total, span in list(zip(totals, spans))[::-1]:
+        made.insert(0, weights(total, span, state, "weights", made[:1]))
     copy = assemble([gather(new, inner, outer, k == 0) for k, new in enumerate(made)], sources, spans, outer, width)
     return (*finish(totals, state), copy.reshape(depth, width))
 

time: 49 us -> 49 us (level)
  no operation moved by 1% of the time
where the time goes in v7:
time: 49 us; the launch traced here: 48.9 us
  starting transfers between devices  37.9 us (77%)
  waiting for transfers between devices  4.83 us (10%)
  Pallas kernels  4.66 us (10%)
  between operations  0.83 us (2%)
  local copies, waits for them, and re-layouts  0.63 us (1%)
    ppermute x13, starting transfers between devices, to_group(): return lax.ppermute(x, ('inner', 'outer'), pairs)  22.6 us
    ppermute x8, starting transfers between devices, to_chip(): return lax.ppermute(x, 'inner', pairs)  13.7 us
    pallas_call x21, Pallas kernels, local_kernel(): pl.pallas_call(ordered, out_shape=out_shape, in_specs=in_specs + [ANY] *...  4.66 us
    ppermute x13, waiting for transfers between devices, to_group(): return lax.ppermute(x, ('inner', 'outer'), pairs)  3.69 us
    ppermute x4, starting transfers between devices, to_core(): return lax.ppermute(x, 'inner', [(i, i ^ 1) for i in range(inner)])  1.61 us
    ppermute x8, waiting for transfers between devices, to_chip(): return lax.ppermute(x, 'inner', pairs)  1.14 us
  transfers between devices with their start and end apart: 25, of which 8 were waited for; matrix products, arithmetic and copies ran while one was open for 0% of the time, Pallas kernels for 5%

profile of v7, /device:TPU:0, one launch (start us, length us, event | category | flops | bytes accessed | tf_op | source)
XLA Modules:
  0.0 48.9 jit_solution(5642466957779664331)
XLA Ops:
  0.6 1.3 %load_theirs.4.refs_1_ = bf16[4,4,64,256]{3,2,1,0:T(8,128)(2,1)S(1)} custom-call(bf16[4,64,8192]{2,1,0:T(8,128)(2,1)} %bitcast.2), custom_call_target="tpu_custom_call" | custom-call | flops 1572864 | bytes 1572864 | tf_op jit(solution)/shard_map/load_theirs/pallas_call | solution.py:36
  4.6 2.6 %collective-permute-start.1 = (bf16[2,4,64,256]{3,2,1,0:T(8,128)(2,1)S(1)}, bf16[2,4,64,256]{3,2,1,0:T(8,128)(2,1)S(1)}, u32[]{:S(2)}, u32[]{:S(2)}) collective-permute-start(bf16[2,4,64,256]{3,2,1,0:T(8,128)(2,1)S(1)} %first_sum.3.refs_2_), channel_id=1, source_target_pairs={{0,8},{4,20},{8,0},{12,28},{16,24},{20,4},{24,16},{28,12},{1,9},{5... | collective-permute-start | bytes 786440 | tf_op jit(solution)/shard_map/ppermute | solution.py:191
  7.4 1.7 %collective-permute-start.5 = (bf16[2,4,64,256]{3,2,1,0:T(8,128)(2,1)S(1)}, bf16[2,4,64,256]{3,2,1,0:T(8,128)(2,1)S(1)}, u32[]{:S(2)}, u32[]{:S(2)}) collective-permute-start(bf16[2,4,64,256]{3,2,1,0:T(8,128)(2,1)S(1)} %first_sum.4.refs_3_), channel_id=1, source_target_pairs={{0,8},{4,20},{8,0},{12,28},{16,24},{20,4},{24,16},{28,12},{1,9},{5... | collective-permute-start | bytes 786440 | tf_op jit(solution)/shard_map/ppermute | solution.py:191
  9.2 1.6 %collective-permute-start.9 = (bf16[2,4,64,256]{3,2,1,0:T(8,128)(2,1)S(1)}, bf16[2,4,64,256]{3,2,1,0:T(8,128)(2,1)S(1)}, u32[]{:S(2)}, u32[]{:S(2)}) collective-permute-start(bf16[2,4,64,256]{3,2,1,0:T(8,128)(2,1)S(1)} %early_first.1.refs_2_), channel_id=1, source_target_pairs={{0,1},{1,0},{2,3},{3,2},{4,5},{5,4},{6,7},{7,6},{8,9},{9,8},{10,11... | collective-permute-start | bytes 786440 | tf_op jit(solution)/shard_map/ppermute | solution.py:196
  10.7 0.9 %collective-permute-done.1.refs_2_ = bf16[2,4,64,256]{3,2,1,0:T(8,128)(2,1)S(1)} collective-permute-done((bf16[2,4,64,256]{3,2,1,0:T(8,128)(2,1)S(1)}, bf16[2,4,64,256]{3,2,1,0:T(8,128)(2,1)S(1)}, u32[]{:S(2)}, u32[]{:S(2)}) %collective-permute-start.1) | collective-permute-done | bytes 262176 | tf_op jit(solution)/shard_map/ppermute | solution.py:191
  11.8 2.1 %collective-permute-start.8 = (bf16[2,4,64,256]{3,2,1,0:T(8,128)(2,1)S(1)}, bf16[2,4,64,256]{3,2,1,0:T(8,128)(2,1)S(1)}, u32[]{:S(2)}, u32[]{:S(2)}) collective-permute-start(bf16[2,4,64,256]{3,2,1,0:T(8,128)(2,1)S(1)} %first_sum.5.refs_3_), channel_id=1, source_target_pairs={{0,8},{4,20},{8,0},{12,28},{16,24},{20,4},{24,16},{28,12},{1,9},{5... | collective-permute-start | bytes 786440 | tf_op jit(solution)/shard_map/ppermute | solution.py:191
  13.9 1.5 %collective-permute-start.4 = (bf16[4,64,256]{2,1,0:T(8,128)(2,1)S(1)}, bf16[4,64,256]{2,1,0:T(8,128)(2,1)S(1)}, u32[]{:S(2)}, u32[]{:S(2)}) collective-permute-start(bf16[4,64,256]{2,1,0:T(8,128)(2,1)S(1)} %second_sum.3.refs_2_), channel_id=1, source_target_pairs={{0,16},{4,12},{8,24},{12,4},{16,0},{20,28},{24,8},{28,20},{1,17},{... | collective-permute-start | bytes 393224 | tf_op jit(solution)/shard_map/ppermute | solution.py:191
  15.5 1.4 %collective-permute-start.7 = (bf16[4,64,256]{2,1,0:T(8,128)(2,1)S(1)}, bf16[4,64,256]{2,1,0:T(8,128)(2,1)S(1)}, u32[]{:S(2)}, u32[]{:S(2)}) collective-permute-start(bf16[4,64,256]{2,1,0:T(8,128)(2,1)S(1)} %second_sum.4.refs_3_), channel_id=1, source_target_pairs={{0,16},{4,12},{8,24},{12,4},{16,0},{20,28},{24,8},{28,20},{1,17},{... | collective-permute-start | bytes 393224 | tf_op jit(solution)/shard_map/ppermute | solution.py:191
  17.3 3.7 %collective-permute-start.12 = (bf16[4,64,256]{2,1,0:T(8,128)(2,1)S(1)}, bf16[4,64,256]{2,1,0:T(8,128)(2,1)S(1)}, u32[]{:S(2)}, u32[]{:S(2)}) collective-permute-start(bf16[4,64,256]{2,1,0:T(8,128)(2,1)S(1)} %early_second.1.refs_3_), channel_id=1, source_target_pairs={{0,3},{1,2},{2,1},{3,0},{4,7},{5,6},{6,5},{7,4},{8,11},{9,10},{10,... | collective-permute-start | bytes 393224 | tf_op jit(solution)/shard_map/ppermute | solution.py:196
  21.1 1.2 %collective-permute-start.11 = (bf16[4,64,256]{2,1,0:T(8,128)(2,1)S(1)}, bf16[4,64,256]{2,1,0:T(8,128)(2,1)S(1)}, u32[]{:S(2)}, u32[]{:S(2)}) collective-permute-start(bf16[4,64,256]{2,1,0:T(8,128)(2,1)S(1)} %second_sum.5.refs_8_), channel_id=1, source_target_pairs={{0,16},{4,12},{8,24},{12,4},{16,0},{20,28},{24,8},{28,20},{1,17},{... | collective-permute-start | bytes 393224 | tf_op jit(solution)/shard_map/ppermute | solution.py:191
  22.3 1.6 %collective-permute-start.10 = (bf16[2,64,512]{2,1,0:T(8,128)(2,1)S(1)}, bf16[2,64,512]{2,1,0:T(8,128)(2,1)S(1)}, u32[]{:S(2)}, u32[]{:S(2)}) collective-permute-start(bf16[2,64,512]{2,1,0:T(8,128)(2,1)S(1)} %halve.1.refs_4_), channel_id=1, source_target_pairs={{0,1},{1,0},{2,3},{3,2},{4,5},{5,4},{6,7},{7,6},{8,9},{9,8},{10,11... | collective-permute-start | bytes 393224 | tf_op jit(solution)/shard_map/ppermute | solution.py:196
  24.3 2.2 %collective-permute-start.17 = (bf16[2,64,256]{2,1,0:T(8,128)(2,1)S(1)}, bf16[2,64,256]{2,1,0:T(8,128)(2,1)S(1)}, u32[]{:S(2)}, u32[]{:S(2)}) collective-permute-start(bf16[2,64,256]{2,1,0:T(8,128)(2,1)S(1)} %get-tuple-element.22), channel_id=1, source_target_pairs={{0,8},{4,20},{8,0},{12,28},{16,24},{20,4},{24,16},{28,12},{1,9},{5... | collective-permute-start | bytes 196616 | tf_op jit(solution)/shard_map/ppermute | solution.py:191
  26.8 3.3 %collective-permute-start.14 = (bf16[64,256]{1,0:T(8,128)(2,1)S(1)}, bf16[64,256]{1,0:T(8,128)(2,1)S(1)}, u32[]{:S(2)}, u32[]{:S(2)}) collective-permute-start(bf16[64,256]{1,0:T(8,128)(2,1)S(1)} %get-tuple-element.19), channel_id=1, source_target_pairs={{0,2},{1,3},{2,0},{3,1},{4,6},{5,7},{6,4},{7,5},{8,10},{9,11},{10,... | collective-permute-start | bytes 98312 | tf_op jit(solution)/shard_map/ppermute | solution.py:196
  30.1 1.2 %collective-permute-start.15 = (bf16[64,256]{1,0:T(8,128)(2,1)S(1)}, bf16[64,256]{1,0:T(8,128)(2,1)S(1)}, u32[]{:S(2)}, u32[]{:S(2)}) collective-permute-start(bf16[64,256]{1,0:T(8,128)(2,1)S(1)} %get-tuple-element.20), channel_id=1, source_target_pairs={{0,3},{1,2},{2,1},{3,0},{4,7},{5,6},{6,5},{7,4},{8,11},{9,10},{10,... | collective-permute-start | bytes 98312 | tf_op jit(solution)/shard_map/ppermute | solution.py:196
  31.5 1.0 %collective-permute-start.18 = (bf16[64,256]{1,0:T(8,128)(2,1)S(1)}, bf16[64,256]{1,0:T(8,128)(2,1)S(1)}, u32[]{:S(2)}, u32[]{:S(2)}) collective-permute-start(bf16[64,256]{1,0:T(8,128)(2,1)S(1)} %early_fourth.1), channel_id=1, source_target_pairs={{0,16},{4,12},{8,24},{12,4},{16,0},{20,28},{24,8},{28,20},{1,17},{... | collective-permute-start | bytes 98312 | tf_op jit(solution)/shard_map/ppermute | solution.py:191
  32.5 2.8 %collective-permute-start.13 = (bf16[64,512]{1,0:T(8,128)(2,1)S(1)}, bf16[64,512]{1,0:T(8,128)(2,1)S(1)}, u32[]{:S(2)}, u32[]{:S(2)}) collective-permute-start(bf16[64,512]{1,0:T(8,128)(2,1)S(1)} %get-tuple-element.18), channel_id=1, source_target_pairs={{0,2},{1,3},{2,0},{3,1},{4,6},{5,7},{6,4},{7,5},{8,10},{9,11},{10,... | collective-permute-start | bytes 196616 | tf_op jit(solution)/shard_map/ppermute | solution.py:196
  36.1 2.8 %collective-permute-start.22 = (bf16[64,512]{1,0:T(8,128)(2,1)S(1)}, bf16[64,512]{1,0:T(8,128)(2,1)S(1)}, u32[]{:S(2)}, u32[]{:S(2)}) collective-permute-start(bf16[64,512]{1,0:T(8,128)(2,1)S(1)} %weights.2.refs_5_.refs_4_), channel_id=1, source_target_pairs={{0,2},{1,3},{2,0},{3,1},{4,6},{5,7},{6,4},{7,5},{8,10},{9,11},{10,... | collective-permute-start | bytes 196616 | tf_op jit(solution)/shard_map/ppermute | solution.py:196
  39.3 2.4 %collective-permute-start.21 = (bf16[64,512]{1,0:T(8,128)(2,1)S(1)}, bf16[64,512]{1,0:T(8,128)(2,1)S(1)}, u32[]{:S(2)}, u32[]{:S(2)}) collective-permute-start(bf16[64,512]{1,0:T(8,128)(2,1)S(1)} %weights.3.refs_0_), channel_id=1, source_target_pairs={{0,3},{1,2},{2,1},{3,0},{4,7},{5,6},{6,5},{7,4},{8,11},{9,10},{10,... | collective-permute-start | bytes 196616 | tf_op jit(solution)/shard_map/ppermute | solution.py:196
  41.7 2.1 %collective-permute-start.19 = (bf16[64,512]{1,0:T(8,128)(2,1)S(1)}, bf16[64,512]{1,0:T(8,128)(2,1)S(1)}, u32[]{:S(2)}, u32[]{:S(2)}) collective-permute-start(bf16[64,512]{1,0:T(8,128)(2,1)S(1)} %weights.3.refs_0_), channel_id=1, source_target_pairs={{0,2},{1,3},{2,0},{3,1},{4,6},{5,7},{6,4},{7,5},{8,10},{9,11},{10,... | collective-permute-start | bytes 196616 | tf_op jit(solution)/shard_map/ppermute | solution.py:196
  43.7 0.8 %collective-permute-start.24 = (bf16[64,512]{1,0:T(8,128)(2,1)S(1)}, bf16[64,512]{1,0:T(8,128)(2,1)S(1)}, u32[]{:S(2)}, u32[]{:S(2)}) collective-permute-start(bf16[64,512]{1,0:T(8,128)(2,1)S(1)} %collective-permute-done.22.refs_5_), channel_id=1, source_target_pairs={{0,1},{1,0},{2,3},{3,2},{4,5},{5,4},{6,7},{7,6},{8,9},{9,8},{10,11... | collective-permute-start | bytes 196616 | tf_op jit(solution)/shard_map/ppermute | solution.py:196
  44.6 1.0 %finish.1 = (f32[64,1024]{1,0:T(8,128)}, f32[64,1024]{1,0:T(8,128)}, f32[64,1024]{1,0:T(8,128)}) custom-call(f32[64,512]{1,0:T(8,128)S(1)} %get-tuple-element.17.refs_5_.refs_0_, bf16[64,512]{1,0:T(8,128)(2,1)S(1)} %collective-permute-done.13.refs_1_, f32[64,256]{1,0:T(8,128)S(1)} %get-tuple-element.16.refs_9_.refs_2_.refs_0_, ...), custom_call_target="tpu_custom_call" | custom-call | flops 2359296 | bytes 2359296 | tf_op jit(solution)/shard_map/finish/pallas_call | solution.py:36
  46.2 0.7 %collective-permute-done.19.refs_1_ = bf16[64,512]{1,0:T(8,128)(2,1)S(1)} collective-permute-done((bf16[64,512]{1,0:T(8,128)(2,1)S(1)}, bf16[64,512]{1,0:T(8,128)(2,1)S(1)}, u32[]{:S(2)}, u32[]{:S(2)}) %collective-permute-start.19) | collective-permute-done | bytes 65568 | tf_op jit(solution)/shard_map/ppermute | solution.py:196
  46.9 1.1 %collective-permute-done.24.refs_7_ = bf16[64,512]{1,0:T(8,128)(2,1)S(1)} collective-permute-done((bf16[64,512]{1,0:T(8,128)(2,1)S(1)}, bf16[64,512]{1,0:T(8,128)(2,1)S(1)}, u32[]{:S(2)}, u32[]{:S(2)}) %collective-permute-start.24) | collective-permute-done | bytes 65568 | tf_op jit(solution)/shard_map/ppermute | solution.py:196
  48.0 0.8 %assemble.1 = bf16[4,64,1024]{2,1,0:T(8,128)(2,1)} custom-call(bf16[64,512]{1,0:T(8,128)(2,1)S(1)} %weights.3.refs_0_, bf16[64,512]{1,0:T(8,128)(2,1)S(1)} %collective-permute-done.19.refs_1_, bf16[64,512]{1,0:T(8,128)(2,1)S(1)} %collective-permute-done.20.refs_2_, bf16[64,512]{1,0:T(8,128)(2,1)S(1)} %collective-permute-done.21.refs_3_, ...), custom_call_target="tpu_custom_call" | custom-call | flops 1572864 | bytes 1572864 | tf_op jit(solution)/shard_map/assemble/pallas_call | solution.py:36
  (55 shorter events, 6.2 us)
Async XLA Ops:
  3.4 3.9 %collective-permute-start.3 = (bf16[4,4,64,256]{3,2,1,0:T(8,128)(2,1)S(1)}, bf16[4,4,64,256]{3,2,1,0:T(8,128)(2,1)S(1)}, u32[]{:S(2)}, u32[]{:S(2)}) collective-permute-start(bf16[4,4,64,256]{3,2,1,0:T(8,128)(2,1)S(1)} %load_theirs.6.refs_1_), channel_id=1, source_target_pairs={{0,4},{4,0},{8,12},{12,8},{16,20},{20,16},{24,28},{28,24},{1,5},{5... | collective-permute-start | bytes 1572872 | tf_op jit(solution)/shard_map/ppermute | solution.py:186
  3.9 3.5 %collective-permute-start.2 = (bf16[4,4,64,256]{3,2,1,0:T(8,128)(2,1)S(1)}, bf16[4,4,64,256]{3,2,1,0:T(8,128)(2,1)S(1)}, u32[]{:S(2)}, u32[]{:S(2)}) collective-permute-start(bf16[4,4,64,256]{3,2,1,0:T(8,128)(2,1)S(1)} %load_theirs.5.refs_1_), channel_id=1, source_target_pairs={{0,4},{4,0},{8,12},{12,8},{16,20},{20,16},{24,28},{28,24},{1,5},{5... | collective-permute-start | bytes 1572872 | tf_op jit(solution)/shard_map/ppermute | solution.py:186
  4.1 7.6 %collective-permute-start.6 = (bf16[4,4,64,256]{3,2,1,0:T(8,128)(2,1)S(1)}, bf16[4,4,64,256]{3,2,1,0:T(8,128)(2,1)S(1)}, u32[]{:S(2)}, u32[]{:S(2)}) collective-permute-start(bf16[4,4,64,256]{3,2,1,0:T(8,128)(2,1)S(1)} %load_theirs.7.refs_2_), channel_id=1, source_target_pairs={{0,4},{4,0},{8,12},{12,8},{16,20},{20,16},{24,28},{28,24},{1,5},{5... | collective-permute-start | bytes 1572872 | tf_op jit(solution)/shard_map/ppermute | solution.py:186
  4.6 7.0 %collective-permute-start.1 = (bf16[2,4,64,256]{3,2,1,0:T(8,128)(2,1)S(1)}, bf16[2,4,64,256]{3,2,1,0:T(8,128)(2,1)S(1)}, u32[]{:S(2)}, u32[]{:S(2)}) collective-permute-start(bf16[2,4,64,256]{3,2,1,0:T(8,128)(2,1)S(1)} %first_sum.3.refs_2_), channel_id=1, source_target_pairs={{0,8},{4,20},{8,0},{12,28},{16,24},{20,4},{24,16},{28,12},{1,9},{5... | collective-permute-start | bytes 786440 | tf_op jit(solution)/shard_map/ppermute | solution.py:191
  7.4 7.9 %collective-permute-start.5 = (bf16[2,4,64,256]{3,2,1,0:T(8,128)(2,1)S(1)}, bf16[2,4,64,256]{3,2,1,0:T(8,128)(2,1)S(1)}, u32[]{:S(2)}, u32[]{:S(2)}) collective-permute-start(bf16[2,4,64,256]{3,2,1,0:T(8,128)(2,1)S(1)} %first_sum.4.refs_3_), channel_id=1, source_target_pairs={{0,8},{4,20},{8,0},{12,28},{16,24},{20,4},{24,16},{28,12},{1,9},{5... | collective-permute-start | bytes 786440 | tf_op jit(solution)/shard_map/ppermute | solution.py:191
  9.2 8.1 %collective-permute-start.9 = (bf16[2,4,64,256]{3,2,1,0:T(8,128)(2,1)S(1)}, bf16[2,4,64,256]{3,2,1,0:T(8,128)(2,1)S(1)}, u32[]{:S(2)}, u32[]{:S(2)}) collective-permute-start(bf16[2,4,64,256]{3,2,1,0:T(8,128)(2,1)S(1)} %early_first.1.refs_2_), channel_id=1, source_target_pairs={{0,1},{1,0},{2,3},{3,2},{4,5},{5,4},{6,7},{7,6},{8,9},{9,8},{10,11... | collective-permute-start | bytes 786440 | tf_op jit(solution)/shard_map/ppermute | solution.py:196
  11.8 9.2 %collective-permute-start.8 = (bf16[2,4,64,256]{3,2,1,0:T(8,128)(2,1)S(1)}, bf16[2,4,64,256]{3,2,1,0:T(8,128)(2,1)S(1)}, u32[]{:S(2)}, u32[]{:S(2)}) collective-permute-start(bf16[2,4,64,256]{3,2,1,0:T(8,128)(2,1)S(1)} %first_sum.5.refs_3_), channel_id=1, source_target_pairs={{0,8},{4,20},{8,0},{12,28},{16,24},{20,4},{24,16},{28,12},{1,9},{5... | collective-permute-start | bytes 786440 | tf_op jit(solution)/shard_map/ppermute | solution.py:191
  13.9 8.4 %collective-permute-start.4 = (bf16[4,64,256]{2,1,0:T(8,128)(2,1)S(1)}, bf16[4,64,256]{2,1,0:T(8,128)(2,1)S(1)}, u32[]{:S(2)}, u32[]{:S(2)}) collective-permute-start(bf16[4,64,256]{2,1,0:T(8,128)(2,1)S(1)} %second_sum.3.refs_2_), channel_id=1, source_target_pairs={{0,16},{4,12},{8,24},{12,4},{16,0},{20,28},{24,8},{28,20},{1,17},{... | collective-permute-start | bytes 393224 | tf_op jit(solution)/shard_map/ppermute | solution.py:191
  15.5 6.8 %collective-permute-start.7 = (bf16[4,64,256]{2,1,0:T(8,128)(2,1)S(1)}, bf16[4,64,256]{2,1,0:T(8,128)(2,1)S(1)}, u32[]{:S(2)}, u32[]{:S(2)}) collective-permute-start(bf16[4,64,256]{2,1,0:T(8,128)(2,1)S(1)} %second_sum.4.refs_3_), channel_id=1, source_target_pairs={{0,16},{4,12},{8,24},{12,4},{16,0},{20,28},{24,8},{28,20},{1,17},{... | collective-permute-start | bytes 393224 | tf_op jit(solution)/shard_map/ppermute | solution.py:191
  17.3 6.9 %collective-permute-start.12 = (bf16[4,64,256]{2,1,0:T(8,128)(2,1)S(1)}, bf16[4,64,256]{2,1,0:T(8,128)(2,1)S(1)}, u32[]{:S(2)}, u32[]{:S(2)}) collective-permute-start(bf16[4,64,256]{2,1,0:T(8,128)(2,1)S(1)} %early_second.1.refs_3_), channel_id=1, source_target_pairs={{0,3},{1,2},{2,1},{3,0},{4,7},{5,6},{6,5},{7,4},{8,11},{9,10},{10,... | collective-permute-start | bytes 393224 | tf_op jit(solution)/shard_map/ppermute | solution.py:196
  21.1 5.6 %collective-permute-start.11 = (bf16[4,64,256]{2,1,0:T(8,128)(2,1)S(1)}, bf16[4,64,256]{2,1,0:T(8,128)(2,1)S(1)}, u32[]{:S(2)}, u32[]{:S(2)}) collective-permute-start(bf16[4,64,256]{2,1,0:T(8,128)(2,1)S(1)} %second_sum.5.refs_8_), channel_id=1, source_target_pairs={{0,16},{4,12},{8,24},{12,4},{16,0},{20,28},{24,8},{28,20},{1,17},{... | collective-permute-start | bytes 393224 | tf_op jit(solution)/shard_map/ppermute | solution.py:191
  22.3 9.0 %collective-permute-start.10 = (bf16[2,64,512]{2,1,0:T(8,128)(2,1)S(1)}, bf16[2,64,512]{2,1,0:T(8,128)(2,1)S(1)}, u32[]{:S(2)}, u32[]{:S(2)}) collective-permute-start(bf16[2,64,512]{2,1,0:T(8,128)(2,1)S(1)} %halve.1.refs_4_), channel_id=1, source_target_pairs={{0,1},{1,0},{2,3},{3,2},{4,5},{5,4},{6,7},{7,6},{8,9},{9,8},{10,11... | collective-permute-start | bytes 393224 | tf_op jit(solution)/shard_map/ppermute | solution.py:196
  24.3 7.2 %collective-permute-start.17 = (bf16[2,64,256]{2,1,0:T(8,128)(2,1)S(1)}, bf16[2,64,256]{2,1,0:T(8,128)(2,1)S(1)}, u32[]{:S(2)}, u32[]{:S(2)}) collective-permute-start(bf16[2,64,256]{2,1,0:T(8,128)(2,1)S(1)} %get-tuple-element.22), channel_id=1, source_target_pairs={{0,8},{4,20},{8,0},{12,28},{16,24},{20,4},{24,16},{28,12},{1,9},{5... | collective-permute-start | bytes 196616 | tf_op jit(solution)/shard_map/ppermute | solution.py:191
  26.8 8.5 %collective-permute-start.14 = (bf16[64,256]{1,0:T(8,128)(2,1)S(1)}, bf16[64,256]{1,0:T(8,128)(2,1)S(1)}, u32[]{:S(2)}, u32[]{:S(2)}) collective-permute-start(bf16[64,256]{1,0:T(8,128)(2,1)S(1)} %get-tuple-element.19), channel_id=1, source_target_pairs={{0,2},{1,3},{2,0},{3,1},{4,6},{5,7},{6,4},{7,5},{8,10},{9,11},{10,... | collective-permute-start | bytes 98312 | tf_op jit(solution)/shard_map/ppermute | solution.py:196
  30.1 5.8 %collective-permute-start.15 = (bf16[64,256]{1,0:T(8,128)(2,1)S(1)}, bf16[64,256]{1,0:T(8,128)(2,1)S(1)}, u32[]{:S(2)}, u32[]{:S(2)}) collective-permute-start(bf16[64,256]{1,0:T(8,128)(2,1)S(1)} %get-tuple-element.20), channel_id=1, source_target_pairs={{0,3},{1,2},{2,1},{3,0},{4,7},{5,6},{6,5},{7,4},{8,11},{9,10},{10,... | collective-permute-start | bytes 98312 | tf_op jit(solution)/shard_map/ppermute | solution.py:196
  31.3 4.6 %collective-permute-start.16 = (bf16[64,256]{1,0:T(8,128)(2,1)S(1)}, bf16[64,256]{1,0:T(8,128)(2,1)S(1)}, u32[]{:S(2)}, u32[]{:S(2)}) collective-permute-start(bf16[64,256]{1,0:T(8,128)(2,1)S(1)} %get-tuple-element.21), channel_id=1, source_target_pairs={{0,1},{1,0},{2,3},{3,2},{4,5},{5,4},{6,7},{7,6},{8,9},{9,8},{10,11... | collective-permute-start | bytes 98312 | tf_op jit(solution)/shard_map/ppermute | solution.py:196
  31.5 4.4 %collective-permute-start.18 = (bf16[64,256]{1,0:T(8,128)(2,1)S(1)}, bf16[64,256]{1,0:T(8,128)(2,1)S(1)}, u32[]{:S(2)}, u32[]{:S(2)}) collective-permute-start(bf16[64,256]{1,0:T(8,128)(2,1)S(1)} %early_fourth.1), channel_id=1, source_target_pairs={{0,16},{4,12},{8,24},{12,4},{16,0},{20,28},{24,8},{28,20},{1,17},{... | collective-permute-start | bytes 98312 | tf_op jit(solution)/shard_map/ppermute | solution.py:191
  32.5 6.7 %collective-permute-start.13 = (bf16[64,512]{1,0:T(8,128)(2,1)S(1)}, bf16[64,512]{1,0:T(8,128)(2,1)S(1)}, u32[]{:S(2)}, u32[]{:S(2)}) collective-permute-start(bf16[64,512]{1,0:T(8,128)(2,1)S(1)} %get-tuple-element.18), channel_id=1, source_target_pairs={{0,2},{1,3},{2,0},{3,1},{4,6},{5,7},{6,4},{7,5},{8,10},{9,11},{10,... | collective-permute-start | bytes 196616 | tf_op jit(solution)/shard_map/ppermute | solution.py:196
  36.1 7.7 %collective-permute-start.22 = (bf16[64,512]{1,0:T(8,128)(2,1)S(1)}, bf16[64,512]{1,0:T(8,128)(2,1)S(1)}, u32[]{:S(2)}, u32[]{:S(2)}) collective-permute-start(bf16[64,512]{1,0:T(8,128)(2,1)S(1)} %weights.2.refs_5_.refs_4_), channel_id=1, source_target_pairs={{0,2},{1,3},{2,0},{3,1},{4,6},{5,7},{6,4},{7,5},{8,10},{9,11},{10,... | collective-permute-start | bytes 196616 | tf_op jit(solution)/shard_map/ppermute | solution.py:196
  38.9 6.7 %collective-permute-start.23 = (bf16[64,512]{1,0:T(8,128)(2,1)S(1)}, bf16[64,512]{1,0:T(8,128)(2,1)S(1)}, u32[]{:S(2)}, u32[]{:S(2)}) collective-permute-start(bf16[64,512]{1,0:T(8,128)(2,1)S(1)} %weights.2.refs_5_.refs_4_), channel_id=1, source_target_pairs={{0,1},{1,0},{2,3},{3,2},{4,5},{5,4},{6,7},{7,6},{8,9},{9,8},{10,11... | collective-permute-start | bytes 196616 | tf_op jit(solution)/shard_map/ppermute | solution.py:196
  39.3 6.3 %collective-permute-start.21 = (bf16[64,512]{1,0:T(8,128)(2,1)S(1)}, bf16[64,512]{1,0:T(8,128)(2,1)S(1)}, u32[]{:S(2)}, u32[]{:S(2)}) collective-permute-start(bf16[64,512]{1,0:T(8,128)(2,1)S(1)} %weights.3.refs_0_), channel_id=1, source_target_pairs={{0,3},{1,2},{2,1},{3,0},{4,7},{5,6},{6,5},{7,4},{8,11},{9,10},{10,... | collective-permute-start | bytes 196616 | tf_op jit(solution)/shard_map/ppermute | solution.py:196
  41.7 4.5 %collective-permute-start.20 = (bf16[64,512]{1,0:T(8,128)(2,1)S(1)}, bf16[64,512]{1,0:T(8,128)(2,1)S(1)}, u32[]{:S(2)}, u32[]{:S(2)}) collective-permute-start(bf16[64,512]{1,0:T(8,128)(2,1)S(1)} %weights.3.refs_0_), channel_id=1, source_target_pairs={{0,1},{1,0},{2,3},{3,2},{4,5},{5,4},{6,7},{7,6},{8,9},{9,8},{10,11... | collective-permute-start | bytes 196616 | tf_op jit(solution)/shard_map/ppermute | solution.py:196
  41.7 5.2 %collective-permute-start.19 = (bf16[64,512]{1,0:T(8,128)(2,1)S(1)}, bf16[64,512]{1,0:T(8,128)(2,1)S(1)}, u32[]{:S(2)}, u32[]{:S(2)}) collective-permute-start(bf16[64,512]{1,0:T(8,128)(2,1)S(1)} %weights.3.refs_0_), channel_id=1, source_target_pairs={{0,2},{1,3},{2,0},{3,1},{4,6},{5,7},{6,4},{7,5},{8,10},{9,11},{10,... | collective-permute-start | bytes 196616 | tf_op jit(solution)/shard_map/ppermute | solution.py:196
  43.7 4.3 %collective-permute-start.24 = (bf16[64,512]{1,0:T(8,128)(2,1)S(1)}, bf16[64,512]{1,0:T(8,128)(2,1)S(1)}, u32[]{:S(2)}, u32[]{:S(2)}) collective-permute-start(bf16[64,512]{1,0:T(8,128)(2,1)S(1)} %collective-permute-done.22.refs_5_), channel_id=1, source_target_pairs={{0,1},{1,0},{2,3},{3,2},{4,5},{5,4},{6,7},{7,6},{8,9},{9,8},{10,11... | collective-permute-start | bytes 196616 | tf_op jit(solution)/shard_map/ppermute | solution.py:196
  (5 other events, 18.6 us)
